TPU v7x, 32 devices: a whole 2x2x4 slice. The times are simulated.
32 devices in a mesh: dp: 4 (over y, x), fsdp: 8 (over z, core).
Axes of the slice: x: 2, y: 2, z: 4, core: 2. Of those that a mesh axis runs over, the one named last changes fastest.
Arguments:
- tokens: bfloat16 [256, 104, 768], P(('dp', 'fsdp')), may hold values from -6 to 6
- captions: int32 [256], P(('dp', 'fsdp')), may hold values from 5 to 60, as said below
- cotangent: bfloat16 [256, 104, 768], P(('dp', 'fsdp')), may hold values from -6 to 6
- project_weight: bfloat16 [768, 2304], P('fsdp'), may hold values from -0.21875 to 0.21875
- project_bias: bfloat16 [1536], P('fsdp'), may hold values from -3 to 3
- output_weight: bfloat16 [768, 768], P('fsdp'), may hold values from -1.75 to 1.75
- output_bias: bfloat16 [768], P('fsdp'), may hold values from -3 to 3
- first_gain: bfloat16 [768], P('fsdp'), may hold values from 0.25 to 1.75
- first_shift: bfloat16 [768], P('fsdp'), may hold values from -2 to 2
- expand_weight: bfloat16 [768, 3072], P('fsdp'), may hold values from -0.21875 to 0.21875
- expand_bias: bfloat16 [3072], P('fsdp'), may hold values from -3 to 3
- shrink_weight: bfloat16 [3072, 768], P('fsdp'), may hold values from -0.15625 to 0.15625
- shrink_bias: bfloat16 [768], P('fsdp'), may hold values from -3 to 3
- second_gain: bfloat16 [768], P('fsdp'), may hold values from 0.25 to 1.75
- second_shift: bfloat16 [768], P('fsdp'), may hold values from -2 to 2
Outputs:
- layer_out: bfloat16 [256, 104, 768], P(('dp', 'fsdp'))
- token_grad: float32 [256, 104, 768], P(('dp', 'fsdp'))
- grad_project_weight: float32 [768, 2304], P('fsdp')
- grad_project_bias: float32 [1536], P('fsdp')
- grad_output_weight: float32 [768, 768], P('fsdp')
- grad_output_bias: float32 [768], P('fsdp')
- grad_first_gain: float32 [768], P('fsdp')
- grad_first_shift: float32 [768], P('fsdp')
- grad_expand_weight: float32 [768, 3072], P('fsdp')
- grad_expand_bias: float32 [3072], P('fsdp')
- grad_shrink_weight: float32 [3072, 768], P('fsdp')
- grad_shrink_bias: float32 [768], P('fsdp')
- grad_second_gain: float32 [768], P('fsdp')
- grad_second_shift: float32 [768], P('fsdp')
Inputs may be any that keep to these rules, and one draw needn't show every extreme that they name: In every draw some pair's caption has exactly 5 words and some pair's exactly 60; most captions are short (lengths are heavy-tailed toward 5).
All inputs are finite; a program needn't handle non-finite values.
Results may differ from a plain program's by a relative error of at most 0.017.
Values may be sent and summed in bfloat16 or wider, within the bound.
No kernel may reach another device: no remote copies, remote signals or barrier semaphores. Data moves between devices by JAX's collectives and lax.ppermute only.
A program may use at most 128 MiB of HBM per device.

v0:
```python
import jax
import jax.numpy as jnp
from jax import lax
from jax.sharding import PartitionSpec as P

HEADS = 12
HEAD_DIM = 64
REGIONS = 36


def layer_norm(inputs, scale_row, shift_row):
    row_mean = jnp.mean(inputs, axis=-1, keepdims=True)
    centred = inputs - row_mean
    spread = jnp.mean(centred * centred, axis=-1, keepdims=True)
    return centred * lax.rsqrt(spread + 1e-05) * scale_row + shift_row


def gelu_exact(inputs):
    return 0.5 * inputs * (1.0 + jax.scipy.special.erf(inputs * 0.7071067811865476))


def inner_rows(left, right):
    return lax.dot_general(
        left, right, (((0,), (0,)), ((), ())), preferred_element_type=jnp.float32
    )


def against(left, right):
    return lax.dot_general(
        left, right, (((1,), (1,)), ((), ())), preferred_element_type=jnp.float32
    )


def forward(tokens, key_valid, attention, feedforward):
    project_weight, project_bias, output_weight, output_bias, first_gain, first_shift = attention
    expand_weight, expand_bias, shrink_weight, shrink_bias, second_gain, second_shift = feedforward
    pair_count, seq_len, model_width = tokens.shape
    token_rows = tokens.reshape(pair_count * seq_len, model_width)
    bias_row = project_bias.astype(jnp.float32)
    bias_full = jnp.concatenate(
        [bias_row[:model_width], jnp.zeros((model_width,), jnp.float32), bias_row[model_width:]]
    )
    joined = jnp.dot(token_rows, project_weight, preferred_element_type=jnp.float32) + bias_full
    joined_low = joined.astype(jnp.bfloat16).reshape(pair_count, seq_len, 3, HEADS, HEAD_DIM)
    query_heads = joined_low[:, :, 0]
    key_heads = joined_low[:, :, 1]
    value_heads = joined_low[:, :, 2]
    mask_bias = jnp.where(key_valid, 0.0, -1000000000.0).astype(jnp.float32)
    scores = jnp.einsum(
        "pqhd,pkhd->phqk", query_heads, key_heads, preferred_element_type=jnp.float32
    )
    scores = scores * HEAD_DIM ** (-0.5) + mask_bias[:, None, None, :]
    prob_full = jax.nn.softmax(scores, axis=-1)
    prob_low = prob_full.astype(jnp.bfloat16)
    context = jnp.einsum(
        "phqk,pkhd->pqhd", prob_low, value_heads, preferred_element_type=jnp.float32
    )
    context_low = context.astype(jnp.bfloat16).reshape(pair_count * seq_len, model_width)
    branch = jnp.dot(
        context_low, output_weight, preferred_element_type=jnp.float32
    ) + output_bias.astype(jnp.float32)
    first_sum = token_rows.astype(jnp.float32) + branch
    normed = layer_norm(first_sum, first_gain.astype(jnp.float32), first_shift.astype(jnp.float32))
    normed_low = normed.astype(jnp.bfloat16)
    expand = jnp.dot(
        normed_low, expand_weight, preferred_element_type=jnp.float32
    ) + expand_bias.astype(jnp.float32)
    active_low = gelu_exact(expand).astype(jnp.bfloat16)
    shrink = jnp.dot(
        active_low, shrink_weight, preferred_element_type=jnp.float32
    ) + shrink_bias.astype(jnp.float32)
    second_sum = normed + shrink
    result = layer_norm(
        second_sum, second_gain.astype(jnp.float32), second_shift.astype(jnp.float32)
    )
    kept_values = (
        token_rows,
        query_heads,
        key_heads,
        value_heads,
        prob_full,
        prob_low,
        context_low,
        first_sum,
        normed_low,
        expand,
        active_low,
        second_sum,
    )
    return (result.reshape(pair_count, seq_len, model_width), kept_values)


def backward(upstream, kept_values, attention, feedforward):
    project_weight, project_bias, output_weight, output_bias, first_gain, first_shift = attention
    expand_weight, expand_bias, shrink_weight, shrink_bias, second_gain, second_shift = feedforward
    (
        token_rows,
        query_heads,
        key_heads,
        value_heads,
        prob_full,
        prob_low,
        context_low,
        first_sum,
        normed_low,
        expand,
        active_low,
        second_sum,
    ) = kept_values
    row_count, model_width = token_rows.shape
    pair_count, seq_len = (query_heads.shape[0], query_heads.shape[1])
    unused_norm, second_pull = jax.vjp(
        layer_norm, second_sum, second_gain.astype(jnp.float32), second_shift.astype(jnp.float32)
    )
    second_grad, grad_second_gain, grad_second_shift = second_pull(upstream)
    grad_shrink_bias = jnp.sum(second_grad, axis=0)
    shrink_low = second_grad.astype(jnp.bfloat16)
    grad_shrink_weight = inner_rows(active_low, shrink_low)
    active_grad = against(shrink_low, shrink_weight)
    unused_gelu, gelu_pull = jax.vjp(gelu_exact, expand)
    expand_grad = gelu_pull(active_grad)[0]
    grad_expand_bias = jnp.sum(expand_grad, axis=0)
    expand_low = expand_grad.astype(jnp.bfloat16)
    grad_expand_weight = inner_rows(normed_low, expand_low)
    normed_grad = against(expand_low, expand_weight) + second_grad
    unused_first, first_pull = jax.vjp(
        layer_norm, first_sum, first_gain.astype(jnp.float32), first_shift.astype(jnp.float32)
    )
    first_grad, grad_first_gain, grad_first_shift = first_pull(normed_grad)
    grad_output_bias = jnp.sum(first_grad, axis=0)
    branch_low = first_grad.astype(jnp.bfloat16)
    grad_output_weight = inner_rows(context_low, branch_low)
    context_grad = (
        against(branch_low, output_weight)
        .astype(jnp.bfloat16)
        .reshape(pair_count, seq_len, HEADS, HEAD_DIM)
    )
    values_grad = jnp.einsum(
        "phqk,pqhd->pkhd", prob_low, context_grad, preferred_element_type=jnp.float32
    )
    probs_grad = jnp.einsum(
        "pqhd,pkhd->phqk", context_grad, value_heads, preferred_element_type=jnp.float32
    )
    row_dot = jnp.sum(prob_full * probs_grad, axis=-1, keepdims=True)
    scores_grad = (prob_full * (probs_grad - row_dot) * HEAD_DIM ** (-0.5)).astype(jnp.bfloat16)
    query_grad = jnp.einsum(
        "phqk,pkhd->pqhd", scores_grad, key_heads, preferred_element_type=jnp.float32
    )
    keys_grad = jnp.einsum(
        "phqk,pqhd->pkhd", scores_grad, query_heads, preferred_element_type=jnp.float32
    )
    joined_grad = jnp.stack([query_grad, keys_grad, values_grad], axis=2).reshape(
        row_count, 3 * model_width
    )
    grad_project_bias = jnp.concatenate(
        [
            jnp.sum(joined_grad[:, :model_width], axis=0),
            jnp.sum(joined_grad[:, 2 * model_width :], axis=0),
        ]
    )
    joined_grad_low = joined_grad.astype(jnp.bfloat16)
    grad_project_weight = inner_rows(token_rows, joined_grad_low)
    token_grad = against(joined_grad_low, project_weight) + first_grad
    attention_grads = (
        grad_project_weight,
        grad_project_bias,
        grad_output_weight,
        grad_output_bias,
        grad_first_gain,
        grad_first_shift,
    )
    feedforward_grads = (
        grad_expand_weight,
        grad_expand_bias,
        grad_shrink_weight,
        grad_shrink_bias,
        grad_second_gain,
        grad_second_shift,
    )
    return (token_grad, attention_grads, feedforward_grads)


def local(
    tokens,
    captions,
    cotangent,
    project_weight,
    project_bias,
    output_weight,
    output_bias,
    first_gain,
    first_shift,
    expand_weight,
    expand_bias,
    shrink_weight,
    shrink_bias,
    second_gain,
    second_shift,
):
    pair_count, seq_len, model_width = tokens.shape
    row_count = pair_count * seq_len
    attention = (
        lax.all_gather(project_weight, "fsdp", axis=0, tiled=True),
        lax.all_gather(project_bias, "fsdp", axis=0, tiled=True),
        lax.all_gather(output_weight, "fsdp", axis=0, tiled=True),
        lax.all_gather(output_bias, "fsdp", axis=0, tiled=True),
        lax.all_gather(first_gain, "fsdp", axis=0, tiled=True),
        lax.all_gather(first_shift, "fsdp", axis=0, tiled=True),
    )
    feedforward = (
        lax.all_gather(expand_weight, "fsdp", axis=0, tiled=True),
        lax.all_gather(expand_bias, "fsdp", axis=0, tiled=True),
        lax.all_gather(shrink_weight, "fsdp", axis=0, tiled=True),
        lax.all_gather(shrink_bias, "fsdp", axis=0, tiled=True),
        lax.all_gather(second_gain, "fsdp", axis=0, tiled=True),
        lax.all_gather(second_shift, "fsdp", axis=0, tiled=True),
    )
    positions = jnp.arange(seq_len, dtype=jnp.int32)
    key_valid = positions[None, :] < captions[:, None] + 2 + REGIONS
    result, unused_kept = forward(tokens, key_valid, attention, feedforward)
    feedforward_back = (
        lax.all_gather(expand_weight, "fsdp", axis=0, tiled=True),
        lax.all_gather(expand_bias, "fsdp", axis=0, tiled=True),
        lax.all_gather(shrink_weight, "fsdp", axis=0, tiled=True),
        lax.all_gather(shrink_bias, "fsdp", axis=0, tiled=True),
        lax.all_gather(second_gain, "fsdp", axis=0, tiled=True),
        lax.all_gather(second_shift, "fsdp", axis=0, tiled=True),
    )
    attention_back = (
        lax.all_gather(project_weight, "fsdp", axis=0, tiled=True),
        lax.all_gather(project_bias, "fsdp", axis=0, tiled=True),
        lax.all_gather(output_weight, "fsdp", axis=0, tiled=True),
        lax.all_gather(output_bias, "fsdp", axis=0, tiled=True),
        lax.all_gather(first_gain, "fsdp", axis=0, tiled=True),
        lax.all_gather(first_shift, "fsdp", axis=0, tiled=True),
    )
    unused_result, kept_values = forward(tokens, key_valid, attention_back, feedforward_back)
    row_mask = key_valid.reshape(row_count, 1).astype(jnp.float32)
    upstream = cotangent.reshape(row_count, model_width).astype(jnp.float32) * row_mask
    token_grad, attention_grads, feedforward_grads = backward(
        upstream, kept_values, attention_back, feedforward_back
    )
    ff_part = (
        lax.psum_scatter(feedforward_grads[0], "fsdp", scatter_dimension=0, tiled=True),
        lax.psum_scatter(feedforward_grads[1], "fsdp", scatter_dimension=0, tiled=True),
        lax.psum_scatter(feedforward_grads[2], "fsdp", scatter_dimension=0, tiled=True),
        lax.psum_scatter(feedforward_grads[3], "fsdp", scatter_dimension=0, tiled=True),
        lax.psum_scatter(feedforward_grads[4], "fsdp", scatter_dimension=0, tiled=True),
        lax.psum_scatter(feedforward_grads[5], "fsdp", scatter_dimension=0, tiled=True),
    )
    attn_part = (
        lax.psum_scatter(attention_grads[0], "fsdp", scatter_dimension=0, tiled=True),
        lax.psum_scatter(attention_grads[1], "fsdp", scatter_dimension=0, tiled=True),
        lax.psum_scatter(attention_grads[2], "fsdp", scatter_dimension=0, tiled=True),
        lax.psum_scatter(attention_grads[3], "fsdp", scatter_dimension=0, tiled=True),
        lax.psum_scatter(attention_grads[4], "fsdp", scatter_dimension=0, tiled=True),
        lax.psum_scatter(attention_grads[5], "fsdp", scatter_dimension=0, tiled=True),
    )
    summed = (
        lax.psum(attn_part[0].astype(jnp.bfloat16), "dp").astype(jnp.float32),
        lax.psum(attn_part[1].astype(jnp.bfloat16), "dp").astype(jnp.float32),
        lax.psum(attn_part[2].astype(jnp.bfloat16), "dp").astype(jnp.float32),
        lax.psum(attn_part[3].astype(jnp.bfloat16), "dp").astype(jnp.float32),
        lax.psum(attn_part[4].astype(jnp.bfloat16), "dp").astype(jnp.float32),
        lax.psum(attn_part[5].astype(jnp.bfloat16), "dp").astype(jnp.float32),
        lax.psum(ff_part[0].astype(jnp.bfloat16), "dp").astype(jnp.float32),
        lax.psum(ff_part[1].astype(jnp.bfloat16), "dp").astype(jnp.float32),
        lax.psum(ff_part[2].astype(jnp.bfloat16), "dp").astype(jnp.float32),
        lax.psum(ff_part[3].astype(jnp.bfloat16), "dp").astype(jnp.float32),
        lax.psum(ff_part[4].astype(jnp.bfloat16), "dp").astype(jnp.float32),
        lax.psum(ff_part[5].astype(jnp.bfloat16), "dp").astype(jnp.float32),
    )
    layer_out = result.astype(jnp.bfloat16)
    token_out = token_grad.reshape(pair_count, seq_len, model_width)
    return (
        layer_out,
        token_out,
        summed[0],
        summed[1],
        summed[2],
        summed[3],
        summed[4],
        summed[5],
        summed[6],
        summed[7],
        summed[8],
        summed[9],
        summed[10],
        summed[11],
    )


def solution(mesh):
    return jax.shard_map(
        local,
        mesh=mesh,
        in_specs=(
            P(("dp", "fsdp"), None, None),
            P(("dp", "fsdp")),
            P(("dp", "fsdp"), None, None),
            P("fsdp", None),
            P("fsdp"),
            P("fsdp", None),
            P("fsdp"),
            P("fsdp"),
            P("fsdp"),
            P("fsdp", None),
            P("fsdp"),
            P("fsdp", None),
            P("fsdp"),
            P("fsdp"),
            P("fsdp"),
        ),
        out_specs=(
            P(("dp", "fsdp"), None, None),
            P(("dp", "fsdp"), None, None),
            P("fsdp", None),
            P("fsdp"),
            P("fsdp", None),
            P("fsdp"),
            P("fsdp"),
            P("fsdp"),
            P("fsdp", None),
            P("fsdp"),
            P("fsdp", None),
            P("fsdp"),
            P("fsdp"),
            P("fsdp"),
        ),
        check_vma=False,
    )
```

profile of v0, /device:TPU:0, one launch (start us, length us, event | category | flops | bytes accessed | tf_op | source)
XLA Modules:
  0.0 672.3 jit_solution(9091270048184089727)
XLA Ops:
  20.0 31.5 %all-reduce.16 = (bf16[1536]{0:T(1024)(128)(2,1)S(1)}, bf16[768]{0:T(1024)(128)(2,1)S(1)}, bf16[768]{0:T(1024)(128)(2,1)S(1)}, bf16[768]{0:T(1024)(128)(2,1)S(1)...) all-reduce(bf16[1536]{0:T(1024)(128)(2,1)S(1)} %dynamic-update-slic, ...), channel_id=1, replica_groups=mesh['dp'=4,'fsdp'=8] {'fsdp'}, use_global_device_ids=true, to_apply=%add | all-reduce | flops 6144 | bytes 24576
  51.6 12.7 %all-gather = bf16[8,1,384]{2,1,0:T(2,128)(2,1)S(1)} all-gather(bf16[1,1,384]{2,1,0:T(2,128)(2,1)S(1)} %reshape.203), channel_id=1, replica_groups=mesh['dp'=4,'fsdp'=8] {'fsdp'}, dimensions={0}, use_global_device_ids=true | all-gather | bytes 6912 | tf_op jit(solution)/shard_map/all_gather | solution.py:212
  66.2 6.8 %add_convert_fusion = bf16[832,2304]{1,0:T(8,128)(2,1)} fusion(bf16[832,768]{1,0:T(8,128)(2,1)S(1)} %bitcast.83, bf16[768,2304]{1,0:T(8,128)(2,1)} %all-gather.6.cloned.1.call-done, f32[2304]{0:T(1024)S(1)} %pad_maximum_fusion.1), kind=kOutput, calls=%fused_computation.6 | convolution fusion | flops 2948235264 | bytes 8659968 | tf_op jit(solution)/shard_map/dot_general | solution.py:43
  73.0 12.4 %reshape.230 = bf16[8,104,3,12,64]{4,3,2,1,0:T(8,128)(2,1)} reshape(bf16[832,2304]{1,0:T(8,128)(2,1)} %add_convert_fusion) | data formatting | bytes 7667712 | tf_op jit(solution)/shard_map/reshape | solution.py:44
  85.4 7.3 %fusion.63 = (bf16[8,104,1,12,64]{4,3,2,1,0:T(8,128)(2,1)}, bf16[8,104,1,12,64]{4,3,2,1,0:T(8,128)(2,1)}, bf16[8,104,1,12,64]{4,3,2,1,0:T(8,128)(2,1)S(1)}) fusion(bf16[8,104,3,12,64]{4,3,2,1,0:T(8,128)(2,1)} %reshape.230), kind=kLoop, calls=%fused_computation.101 | loop fusion | bytes 7667712 | tf_op jit(solution)/shard_map/slice | solution.py:45
  121.2 9.7 %all-gather.10.cloned.1.call-done = bf16[768,3072]{1,0:T(8,128)(2,1)} async-done(((bf16[96,3072]{1,0:T(8,128)(2,1)}), bf16[768,3072]{1,0:T(8,128)(2,1)}) %all-gather.10.cloned.1.call-update) | async-done | bytes 4718608 | tf_op jit(solution)/shard_map/all_gather | solution.py:211
  130.9 11.3 %multiply_convert_fusion = (bf16[832,3072]{1,0:T(8,128)(2,1)}, f32[832,3072]{1,0:T(8,128)}) fusion(f32[3072]{0:T(1024)S(1)} %bitcast.79, bf16[768,3072]{1,0:T(8,128)(2,1)} %all-gather.10.cloned.1.call-done, f32[832,768]{1,0:T(8,128)S(1)} %get-tuple-element.104, f32[768]{0:T(1024)S(1)} %convert_element_type.197, f32[768]{0:T(1024)S(1)} %convert_element_type.196, ...), kind=kOutput, calls=%fused_computation.3 | convolution fusion | flops 3944398848 | bytes 22635008 | tf_op jit(solution)/shard_map/dot_general | solution.py:65
  142.2 40.8 %all-gather.12.cloned.1.call-done = bf16[3072,768]{1,0:T(8,128)(2,1)} async-done(((bf16[384,768]{1,0:T(8,128)(2,1)}), bf16[3072,768]{1,0:T(8,128)(2,1)}) %all-gather.12.cloned.1.call-update) | async-done | bytes 4718608 | tf_op jit(solution)/shard_map/all_gather | solution.py:213
  183.0 8.4 %fusion.68 = (f32[832]{0:T(1024)S(1)}, f32[832,768]{1,0:T(8,128)S(1)}) fusion(f32[768]{0:T(1024)S(1)} %convert_element_type.201, bf16[832,3072]{1,0:T(8,128)(2,1)} %get-tuple-element.105, bf16[3072,768]{1,0:T(8,128)(2,1)} %all-gather.12.cloned.1.call-done, f32[768]{0:T(1024)S(1)} %convert_element_type.197, f32[768]{0:T(1024)S(1)} %convert_element_type.196, ...), kind=kOutput, calls=%fused_computation.106 | convolution fusion | flops 3930340608 | bytes 14961408 | tf_op jit(solution)/shard_map/dot_general | solution.py:69
  198.2 12.1 %fusion.69 = (f32[3072]{0:T(1024)S(1)}, bf16[832,3072]{1,0:T(8,128)(2,1)S(1)}) fusion(bf16[3072,768]{1,0:T(8,128)(2,1)} %all-gather.12.cloned.1.call-done, f32[832,768]{1,0:T(8,128)} %get-tuple-element.95, f32[832]{0:T(1024)S(1)} %negate_multiply_fusion.1, f32[832,3072]{1,0:T(8,128)} %get-tuple-element.106, f32[3072]{0:T(1024)S(1)} %bitcast.80), kind=kOutput, calls=%fused_computation.107 | convolution fusion | flops 3965481984 | bytes 22637824 | tf_op jit(solution)/shard_map/dot_general | solution.py:29
  210.4 8.9 %multiply_reduce_fusion.3 = (f32[768]{0:T(1024)S(1)}, f32[832]{0:T(1024)S(1)}, f32[768]{0:T(1024)S(1)}, f32[832,768]{1,0:T(8,128)S(1)}) fusion(f32[832,768]{1,0:T(8,128)S(1)} %get-tuple-element.104, f32[832]{0:T(1024)S(1)} %fusion.48, f32[832]{0:T(1024)S(1)} %broadcast_multiply_fusion.1, f32[768]{0:T(1024)S(1)} %convert_element_type.196, ...), kind=kOutput, calls=%fused_computation.25 | convolution fusion | flops 3932256000 | bytes 17520640 | tf_op jit(solution)/shard_map/dot_general | solution.py:29
  229.0 5.5 reshape.231
  239.4 5.7 fusion.38
  245.1 10.8 %fusion.26 = f32[8,104,1,12,64]{1,4,3,0,2:T(8,128)} fusion(f32[8,12,104,104]{2,3,1,0:T(8,128)} %fusion.38, bf16[8,104,1,12,64]{1,4,3,0,2:T(8,128)(2,1)} %copy.80, f32[8,12,104,104]{2,3,1,0:T(8,128)} %copy-done.12, f32[8,12,104]{2,1,0:T(8,128)S(1)} %get-tuple-element.101), kind=kOutput, calls=%fused_computation.51 | convolution fusion | flops 140185440 | bytes 12180480 | tf_op jit(solution)/shard_map/phqk,pqhd->pkhd/dot_general | solution.py:149
  255.9 10.8 %fusion.23 = f32[8,104,1,12,64]{1,4,3,0,2:T(8,128)} fusion(f32[8,12,104,104]{2,3,1,0:T(8,128)} %fusion.38, bf16[8,104,1,12,64]{1,4,3,0,2:T(8,128)(2,1)} %copy.81, f32[8,12,104,104]{2,3,1,0:T(8,128)} %copy-done.12, f32[8,12,104]{2,1,0:T(8,128)S(1)} %get-tuple-element.101), kind=kOutput, calls=%fused_computation.50 | convolution fusion | flops 140185440 | bytes 12180480 | tf_op jit(solution)/shard_map/phqk,pkhd->pqhd/dot_general | solution.py:146
  266.8 4.9 convolution_bitcast_fusion.1
  273.4 11.4 %copy.67 = bf16[8,104,3,12,64]{1,0,4,3,2:T(8,128)(2,1)} copy(bf16[8,104,3,12,64]{1,4,3,0,2:T(8,128)(2,1)S(1)} %fusion.61) | data formatting | bytes 7667712 | tf_op jit(solution)/shard_map/convert_element_type | solution.py:161
  284.8 8.9 %convert_element_type.217 = bf16[832,2304]{0,1:T(8,128)(2,1)} reshape(bf16[8,104,3,12,64]{1,0,4,3,2:T(8,128)(2,1)} %copy.67) | data formatting | bytes 7667712 | tf_op jit(solution)/shard_map/convert_element_type | solution.py:161
  293.7 9.3 %convolution_bitcast_fusion = f32[768,2304]{0,1:T(8,128)} fusion(bf16[832,2304]{0,1:T(8,128)(2,1)} %convert_element_type.217, bf16[832,768]{1,0:T(8,128)(2,1)} %bitcast.82), kind=kOutput, calls=%fused_computation.7 | convolution fusion | flops 2944401408 | bytes 12189696 | tf_op jit(solution)/shard_map/dot_general | solution.py:23
  303.0 8.0 %copy.73 = f32[768,2304]{1,0:T(8,128)} copy(f32[768,2304]{0,1:T(8,128)} %convolution_bitcast_fusion) | data formatting | bytes 14155776
  311.1 10.3 %fusion.14 = f32[768,3072]{1,0:T(8,128)} fusion(bf16[832,3072]{1,0:T(8,128)(2,1)} %copy-done.10, f32[832,768]{1,0:T(8,128)S(1)} %get-tuple-element.104, f32[768]{0:T(1024)S(1)} %convert_element_type.197, f32[768]{0:T(1024)S(1)} %convert_element_type.196, f32[832]{0:T(1024)S(1)} %fusion.48, f32[832]{0:T(1024)S(1)} %broadcast_multiply_fusion.1), kind=kOutput, calls=%fused_computation.27 | convolution fusion | flops 3929063424 | bytes 17117696 | tf_op jit(solution)/shard_map/dot_general | solution.py:23
  323.1 10.3 %fusion.55 = f32[3072,768]{1,0:T(8,128)} fusion(bf16[832,3072]{1,0:T(8,128)(2,1)} %get-tuple-element.105, f32[832,768]{1,0:T(8,128)S(1)} %copy-done.1, f32[832]{0:T(1024)S(1)} %negate_multiply_fusion.1), kind=kOutput, calls=%fused_computation.95 | convolution fusion | flops 3927146496 | bytes 17108224 | tf_op jit(solution)/shard_map/dot_general | solution.py:23
  337.4 5.0 pad_maximum_fusion
  342.3 12.5 %copy.66 = f32[8,104,3,12,64]{1,0,4,3,2:T(8,128)} copy(f32[8,104,3,12,64]{1,4,3,0,2:T(8,128)S(1)} %pad_maximum_fusion) | data formatting | bytes 15335424 | tf_op jit(solution)/shard_map/stack | solution.py:152
  354.8 10.8 %reshape.178 = f32[832,2304]{0,1:T(8,128)} reshape(f32[8,104,3,12,64]{1,0,4,3,2:T(8,128)} %copy.66) | data formatting | bytes 15335424 | tf_op jit(solution)/shard_map/reshape | solution.py:152
  367.3 19.9 %reduce-scatter.13.cloned.1.call-done = f32[96,2304]{1,0:T(8,128)} async-done(((f32[768,2304]{1,0:T(8,128)}), f32[96,2304]{1,0:T(8,128)}) %reduce-scatter.13.cloned.1.call-update) | async-done | bytes 884752
  389.4 98.0 %reduce-scatter.9.cloned.1.call-done = f32[96,3072]{1,0:T(8,128)} async-done(((f32[768,3072]{1,0:T(8,128)}), f32[96,3072]{1,0:T(8,128)}) %reduce-scatter.9.cloned.1.call-update) | async-done | bytes 1179664 | tf_op jit(solution)/shard_map/reduce_scatter | solution.py:244
  489.5 98.0 %reduce-scatter.11.cloned.1.call-done = f32[384,768]{1,0:T(8,128)} async-done(((f32[3072,768]{1,0:T(8,128)}), f32[384,768]{1,0:T(8,128)}) %reduce-scatter.11.cloned.1.call-update) | async-done | bytes 1179664 | tf_op jit(solution)/shard_map/reduce_scatter | solution.py:246
  593.6 26.4 %all-reduce.15 = (bf16[1536]{0:T(1024)(128)(2,1)S(1)}, bf16[768]{0:T(1024)(128)(2,1)S(1)}, bf16[768]{0:T(1024)(128)(2,1)S(1)}, bf16[768]{0:T(1024)(128)(2,1)S(1)...) all-reduce(f32[1536]{0:T(1024)S(1)} %pad_maximum_fusion.2, ...), channel_id=3, replica_groups=mesh['dp'=4,'fsdp'=8] {'fsdp'}, use_global_device_ids=true, to_apply=%region_15.16.clone | all-reduce | flops 9216 | bytes 55296
  620.6 10.0 %all-reduce.17 = (bf16[192]{0:T(256)(128)(2,1)S(1)}, bf16[96]{0:T(256)(128)(2,1)S(1)}, bf16[96]{0:T(256)(128)(2,1)S(1)}, bf16[96]{0:T(256)(128)(2,1)S(1)}, bf16[...) all-reduce(bf16[192]{0:T(256)(128)(2,1)S(1)} %dynamic-slice.32, ...), channel_id=1, replica_groups=mesh['dp'=4,'fsdp'=8] {'dp'}, use_global_device_ids=true, to_apply=%region_16.17 | all-reduce | flops 1152 | bytes 4608 | tf_op jit(solution)/shard_map/psum | solution.py:261
  634.8 10.3 %add_add_fusion.4 = f32[832,768]{1,0:T(8,128)} fusion(f32[832,768]{1,0:T(8,128)} %copy-done.7, bf16[768,2304]{1,0:T(8,128)(2,1)} %all-gather.6.cloned.1.call-done, f32[832,2304]{0,1:T(8,128)} %reshape.178, f32[832]{0:T(1024)S(1)} %negate_multiply_fusion), kind=kOutput, calls=%fused_computation.44 | convolution fusion | flops 2947596288 | bytes 16321792 | tf_op jit(solution)/shard_map/dot_general | solution.py:29
  645.1 13.3 %all-reduce.21.cloned.1.call-done = (bf16[96,2304]{0,1:T(8,128)(2,1)}, bf16[96,768]{1,0:T(8,128)(2,1)}, bf16[96,3072]{1,0:T(8,128)(2,1)}, bf16[384,768]{1,0:T(8,128)(2,1)}) async-done(((bf16[96,2304]{0,1:T(8,128)(2,1)}, bf16[96,768]{1,0:T(8,128)(2,1)}, bf16[96,3072]{1,0:T(8,128)(2,1)}, bf16[384,768]{1,0:T(8,128)(2,1)}), (bf16[96,2304]{0,1:T(8,128)(2,1)}, bf16[96,768]{1,0:T(8,128)(2,1)}, ...) | async-done | bytes 1769488 | tf_op jit(solution)/shard_map/psum | solution.py:260
  (144 shorter events, 92.7 us)
Async XLA Ops:
  7.2 57.2 %copy-start.2 = (bf16[8,104,768]{2,1,0:T(8,128)(2,1)S(1)}, bf16[8,104,768]{2,1,0:T(8,128)(2,1)}, u32[]{:S(2)}) copy-start(bf16[8,104,768]{2,1,0:T(8,128)(2,1)} %param.17) | copy-start | bytes 3833860
  7.2 59.0 %all-gather.6.cloned.1.call-start = ((), (), s32[]{:S(2)}) async-start(), calls=%async_computation.4 | async-start | bytes 3981312 | tf_op jit(solution)/shard_map/all_gather | solution.py:203
  7.9 109.3 %all-gather.8.cloned.1.call-start = ((), (), s32[]{:S(2)}) async-start(), calls=%async_computation.5 | async-start | bytes 1327104 | tf_op jit(solution)/shard_map/all_gather | solution.py:205
  8.7 57.6 %copy-start.17 = (bf16[8,104,768]{2,1,0:T(8,128)(2,1)S(1)}, bf16[8,104,768]{2,1,0:T(8,128)(2,1)}, u32[]{:S(2)}) copy-start(bf16[8,104,768]{2,1,0:T(8,128)(2,1)} %param.15) | copy-start | bytes 3833860
  8.7 122.2 %all-gather.10.cloned.1.call-start = ((), (), s32[]{:S(2)}) async-start(), calls=%async_computation.6 | async-start | bytes 5308416 | tf_op jit(solution)/shard_map/all_gather | solution.py:211
  9.4 173.6 %all-gather.12.cloned.1.call-start = ((), (), s32[]{:S(2)}) async-start(), calls=%async_computation.7 | async-start | bytes 5308416 | tf_op jit(solution)/shard_map/all_gather | solution.py:213
  10.0 355.6 %reduce-scatter.7.cloned.1.call-start = ((), (), s32[]{:S(2)}) async-start(), calls=%async_computation.8 | async-start | bytes 2654208 | tf_op jit(solution)/shard_map/reduce_scatter | solution.py:254
  14.1 37.5 %copy-start.15 = (f32[8,104]{1,0:T(8,128)}, f32[8,104]{1,0:T(8,128)S(1)}, u32[]{:S(2)}) copy-start(f32[8,104]{1,0:T(8,128)S(1)} %fusion.46) | copy-start | bytes 9988
  109.1 2.4 copy-start.11
  111.5 2.3 copy-start.12
  183.0 8.9 %copy-start.9 = (f32[832,768]{1,0:T(8,128)S(1)}, f32[832,768]{1,0:T(8,128)}, u32[]{:S(2)}) copy-start(f32[832,768]{1,0:T(8,128)} %bitcast_multiply_fusion) | copy-start | bytes 7667716
  191.4 1.3 copy-start.3
  198.2 12.2 %copy-start = (f32[832,768]{1,0:T(8,128)S(1)}, f32[832,768]{1,0:T(8,128)}, u32[]{:S(2)}) copy-start(f32[832,768]{1,0:T(8,128)} %get-tuple-element.95) | copy-start | bytes 7667716
  210.4 9.0 %copy-start.10 = (bf16[832,3072]{1,0:T(8,128)(2,1)}, bf16[832,3072]{1,0:T(8,128)(2,1)S(1)}, u32[]{:S(2)}) copy-start(bf16[832,3072]{1,0:T(8,128)(2,1)S(1)} %get-tuple-element.111) | copy-start | bytes 15335428
  219.4 2.4 copy-start.13
  220.3 1.4 copy-start.7
  224.6 162.5 %reduce-scatter.13.cloned.1.call-start = ((), (), s32[]{:S(2)}) async-start(), calls=%async_computation.11 | async-start | bytes 7962624
  266.8 4.9 copy-start.4
  266.8 5.0 copy-start.5
  271.7 1.7 copy-start.6
  311.0 176.3 %reduce-scatter.9.cloned.1.call-start = ((), (), s32[]{:S(2)}) async-start(), calls=%async_computation.9 | async-start | bytes 10616832 | tf_op jit(solution)/shard_map/reduce_scatter | solution.py:244
  321.3 1.7 copy-start.1
  321.4 266.2 %reduce-scatter.11.cloned.1.call-start = ((), (), s32[]{:S(2)}) async-start(), calls=%async_computation.10 | async-start | bytes 10616832 | tf_op jit(solution)/shard_map/reduce_scatter | solution.py:246
  333.3 2.4 copy-start.16
  333.3 325.0 %all-reduce.21.cloned.1.call-start = ((), (), s32[]{:S(2)}) async-start(), calls=%async_computation.12 | async-start | bytes 3833856 | tf_op jit(solution)/shard_map/psum | solution.py:260
  589.7 3.4 copy-start.8
  658.4 6.1 copy-start.14
Sparse Core Ops, SparseCore 0:
  9.7 44.8 all-gather.5
  56.2 21.5 all-gather.7
  79.4 51.4 all-gather.9
  132.4 50.5 all-gather.11
  224.7 35.1 reduce-scatter.6
  311.1 75.9 reduce-scatter.12
  389.4 97.8 reduce-scatter.8
  489.6 97.8 reduce-scatter.10
  592.2 66.1 all-reduce.20
where the time goes:
time: 677 us; the launch traced here: 672 us
  waiting for transfers between devices  282 us (42%)
  matrix products  135 us (20%)
  local copies, waits for them, and re-layouts  117 us (17%)
  blocking collectives  80.6 us (12%)
  other arithmetic  38.6 us (6%)
  between operations  17.7 us (3%)
    reduce_scatter x1, waiting for transfers between devices, local(): lax.psum_scatter(feedforward_grads[2], 'fsdp', scatter_dimension=0, tiled...  98 us
    reduce_scatter x1, waiting for transfers between devices, local(): lax.psum_scatter(feedforward_grads[0], 'fsdp', scatter_dimension=0, tiled...  98 us
    unnamed x2, blocking collectives  57.9 us
    all_gather x1, waiting for transfers between devices, local(): lax.all_gather(shrink_weight, 'fsdp', axis=0, tiled=True)  40.8 us
    unnamed x66, local copies, waits for them, and re-layouts  40.2 us
    dot_general x4, matrix products, against(): lax.dot_general(left, right, (((1,), (1,)), ((), ())), preferred_element_...  35.6 us
    dot_general x4, matrix products, inner_rows(): lax.dot_general(left, right, (((0,), (0,)), ((), ())), preferred_element_...  32.7 us
    unnamed x10, waiting for transfers between devices  22.5 us
  transfers between devices with their start and end apart: 9, of which 6 were waited for; matrix products, arithmetic and copies ran while one was open for 35% of the time, Pallas kernels for 0%

commit v1 on v0

v1 whole, which is shorter than its diff:
```python
import functools

import jax
import jax.numpy as jnp
from jax import lax
from jax.experimental import pallas as pl
from jax.experimental.pallas import tpu as pltpu
from jax.sharding import PartitionSpec as P

HEADS = 12
HEAD_DIM = 64
REGIONS = 36
BF16 = jnp.bfloat16
F32 = jnp.float32
VMEM_LIMIT = 56 * 1024 * 1024

NN = (((1,), (0,)), ((), ()))
NT = (((1,), (1,)), ((), ()))
TN = (((0,), (0,)), ((), ()))


def dot(left, right, dims=NN):
    return lax.dot_general(left, right, dims, preferred_element_type=F32)


def params():
    return pltpu.CompilerParams(vmem_limit_bytes=VMEM_LIMIT)


def cost(flops, moved):
    return pl.CostEstimate(flops=flops, bytes_accessed=moved, transcendentals=0)


def whole(shape):
    return pl.BlockSpec(shape, lambda *at: (0,) * len(shape))


def tile_of(size, most):
    return max(t for t in range(128, most + 1, 128) if size % t == 0)


def rows_of(count, most):
    fits = [t for t in range(16, most + 1, 16) if count % t == 0]
    return max(fits) if fits else count


def join_kernel(tokens, weight, bias, out):
    out[...] = (dot(tokens[...], weight[...]) + bias[...]).astype(BF16)


def join(token_rows, weight, bias):
    rows, width = token_rows.shape
    columns = weight.shape[1]
    tile = tile_of(columns, 768)
    return pl.pallas_call(
        join_kernel,
        grid=(columns // tile,),
        in_specs=[
            whole((rows, width)),
            pl.BlockSpec((width, tile), lambda i: (0, i)),
            pl.BlockSpec((1, tile), lambda i: (0, i)),
        ],
        out_specs=pl.BlockSpec((rows, tile), lambda i: (0, i)),
        out_shape=jax.ShapeDtypeStruct((rows, columns), BF16),
        compiler_params=params(),
        cost_estimate=cost(2 * rows * width * columns, 2 * (width * columns + rows * columns)),
        name="join",
    )(token_rows, weight, bias)


def head_stack(block, low_half, padded):
    rows = block.shape[0]
    filler = jnp.zeros((padded - rows, block.shape[1]), F32)
    first = jnp.where(low_half, block, 0.0)
    second = jnp.where(low_half, 0.0, block)
    return jnp.concatenate([first, filler, second, filler], axis=0).astype(BF16)


def attend_kernel(captions, joined, context, probs):
    seq = joined.shape[1]
    width = context.shape[2]
    padded = probs.shape[3] // 2
    valid = captions[pl.program_id(0)] + 2 + REGIONS
    keep = lax.broadcasted_iota(jnp.int32, (seq, 2 * padded), 0) < valid
    low_half = lax.broadcasted_iota(jnp.int32, (1, 2 * HEAD_DIM), 1) < HEAD_DIM
    for pair in range(HEADS // 2):
        at = pair * 2 * HEAD_DIM
        query = joined[0, :, at : at + 2 * HEAD_DIM].astype(F32)
        keys = joined[0, :, width + at : width + at + 2 * HEAD_DIM]
        values = joined[0, :, 2 * width + at : 2 * width + at + 2 * HEAD_DIM]
        stacked = head_stack(query, low_half, padded)
        scores = dot(keys, stacked, NT) * HEAD_DIM ** (-0.5)
        scores = jnp.where(keep, scores, -1000000000.0)
        top = jnp.max(scores, axis=0, keepdims=True)
        grown = jnp.exp(scores - top)
        total = jnp.sum(grown, axis=0, keepdims=True)
        prob = (grown * (1.0 / total)).astype(BF16)
        probs[0, pair] = prob
        mixed = dot(prob, values, TN)
        context[0, :, at : at + 2 * HEAD_DIM] = jnp.where(
            low_half, mixed[:seq], mixed[padded : padded + seq]
        ).astype(BF16)


def attend(joined, captions):
    pairs, seq, columns = joined.shape
    width = columns // 3
    padded = (seq + 127) // 128 * 128
    return pl.pallas_call(
        attend_kernel,
        grid_spec=pltpu.PrefetchScalarGridSpec(
            num_scalar_prefetch=1,
            grid=(pairs,),
            in_specs=[pl.BlockSpec((1, seq, columns), lambda i, c: (i, 0, 0))],
            out_specs=[
                pl.BlockSpec((1, seq, width), lambda i, c: (i, 0, 0)),
                pl.BlockSpec((1, HEADS // 2, seq, 2 * padded), lambda i, c: (i, 0, 0, 0)),
            ],
        ),
        out_shape=[
            jax.ShapeDtypeStruct((pairs, seq, width), BF16),
            jax.ShapeDtypeStruct((pairs, HEADS // 2, seq, 2 * padded), BF16),
        ],
        compiler_params=params(),
        cost_estimate=cost(8 * pairs * seq * padded * width, 2 * joined.size),
        name="attend",
    )(captions, joined)


def attend_back_kernel(joined, probs, grads, out, sums):
    seq = joined.shape[1]
    width = grads.shape[2]
    padded = probs.shape[3] // 2
    low_half = lax.broadcasted_iota(jnp.int32, (1, 2 * HEAD_DIM), 1) < HEAD_DIM

    @pl.when(pl.program_id(0) == 0)
    def _():
        sums[...] = jnp.zeros_like(sums)

    for pair in range(HEADS // 2):
        at = pair * 2 * HEAD_DIM
        query = joined[0, :, at : at + 2 * HEAD_DIM].astype(F32)
        keys = joined[0, :, width + at : width + at + 2 * HEAD_DIM]
        values = joined[0, :, 2 * width + at : 2 * width + at + 2 * HEAD_DIM]
        grad = grads[0, :, at : at + 2 * HEAD_DIM].astype(F32)
        query_stack = head_stack(query, low_half, padded)
        grad_stack = head_stack(grad, low_half, padded)
        prob = probs[0, pair]
        prob_full = prob.astype(F32)
        prob_grad = dot(values, grad_stack, NT)
        row_dot = jnp.sum(prob_full * prob_grad, axis=0, keepdims=True)
        score_grad = (prob_full * (prob_grad - row_dot) * HEAD_DIM ** (-0.5)).astype(BF16)
        values_grad = dot(prob, grad_stack)
        keys_grad = dot(score_grad, query_stack)
        mixed = dot(score_grad, keys, TN)
        query_grad = jnp.where(low_half, mixed[:seq], mixed[padded : padded + seq])
        out[0, :, at : at + 2 * HEAD_DIM] = query_grad.astype(BF16)
        out[0, :, width + at : width + at + 2 * HEAD_DIM] = keys_grad.astype(BF16)
        out[0, :, 2 * width + at : 2 * width + at + 2 * HEAD_DIM] = values_grad.astype(BF16)
        sums[:, at : at + 2 * HEAD_DIM] += jnp.sum(query_grad, axis=0, keepdims=True)
        sums[:, width + at : width + at + 2 * HEAD_DIM] += jnp.sum(values_grad, axis=0, keepdims=True)


def attend_back(joined, probs, grads):
    pairs, seq, columns = joined.shape
    width = columns // 3
    padded = probs.shape[3] // 2
    return pl.pallas_call(
        attend_back_kernel,
        grid=(pairs,),
        in_specs=[
            pl.BlockSpec((1, seq, columns), lambda i: (i, 0, 0)),
            pl.BlockSpec((1, HEADS // 2, seq, 2 * padded), lambda i: (i, 0, 0, 0)),
            pl.BlockSpec((1, seq, width), lambda i: (i, 0, 0)),
        ],
        out_specs=[
            pl.BlockSpec((1, seq, columns), lambda i: (i, 0, 0)),
            pl.BlockSpec((1, 2 * width), lambda i: (0, 0)),
        ],
        out_shape=[
            jax.ShapeDtypeStruct((pairs, seq, columns), BF16),
            jax.ShapeDtypeStruct((1, 2 * width), F32),
        ],
        compiler_params=params(),
        cost_estimate=cost(20 * pairs * seq * padded * width, 5 * joined.size),
        name="attend_back",
    )(joined, probs, grads)


def norm_parts(values):
    centred = values - jnp.mean(values, axis=-1, keepdims=True)
    spread = jnp.mean(centred * centred, axis=-1, keepdims=True)
    scale = lax.rsqrt(spread + 1e-05)
    return centred * scale, scale


def norm_back(upstream, unit, scale, gain):
    scaled = upstream * gain
    return scale * (
        scaled
        - jnp.mean(scaled, axis=-1, keepdims=True)
        - unit * jnp.mean(scaled * unit, axis=-1, keepdims=True)
    )


def add_sums(sums, rows):
    @pl.when(pl.program_id(0) == 0)
    def _():
        sums[...] = jnp.zeros_like(sums)

    for at, values in enumerate(rows):
        sums[at : at + 1, :] += jnp.sum(values, axis=0, keepdims=True)


def first_kernel(context, weight, bias, tokens, gain, shift, unit, scale, normed_low):
    total = tokens[...].astype(F32) + (dot(context[...], weight[...]) + bias[...])
    unit_rows, scale_rows = norm_parts(total)
    unit[...] = unit_rows
    scale[...] = scale_rows
    normed_low[...] = (unit_rows * gain[...] + shift[...]).astype(BF16)


def first_norm(context, weight, bias, token_rows, gain, shift):
    rows, width = token_rows.shape
    tile = rows_of(rows, 416)
    block = pl.BlockSpec((tile, width), lambda i: (i, 0))
    return pl.pallas_call(
        first_kernel,
        grid=(rows // tile,),
        in_specs=[block, whole((width, width)), whole((1, width)), block, whole((1, width)), whole((1, width))],
        out_specs=[block, pl.BlockSpec((tile, 1), lambda i: (i, 0)), block],
        out_shape=[
            jax.ShapeDtypeStruct((rows, width), F32),
            jax.ShapeDtypeStruct((rows, 1), F32),
            jax.ShapeDtypeStruct((rows, width), BF16),
        ],
        compiler_params=params(),
        cost_estimate=cost(2 * rows * width * width, 10 * rows * width + 2 * width * width),
        name="first_norm",
    )(context, weight, bias, token_rows, gain, shift)


def expand_kernel(normed_low, weight, bias, active, slope):
    expand = dot(normed_low[...], weight[...]) + bias[...]
    half = 0.5 * (1.0 + lax.erf(expand * 0.7071067811865476))
    active[...] = (expand * half).astype(BF16)
    slope[...] = (half + expand * jnp.exp(-0.5 * expand * expand) * 0.3989422804014327).astype(BF16)


def expand_act(normed_low, weight, bias):
    rows, width = normed_low.shape
    columns = weight.shape[1]
    tile = tile_of(columns, 768)
    out = jax.ShapeDtypeStruct((rows, columns), BF16)
    block = pl.BlockSpec((rows, tile), lambda i: (0, i))
    return pl.pallas_call(
        expand_kernel,
        grid=(columns // tile,),
        in_specs=[
            whole((rows, width)),
            pl.BlockSpec((width, tile), lambda i: (0, i)),
            pl.BlockSpec((1, tile), lambda i: (0, i)),
        ],
        out_specs=[block, block],
        out_shape=[out, out],
        compiler_params=params(),
        cost_estimate=cost(2 * rows * width * columns, 2 * width * columns + 4 * rows * columns),
        name="expand_act",
    )(normed_low, weight, bias)


def second_kernel(captions, active, weight, bias, unit, gain, shift, gain2, shift2, cotangent, out, low, grad, sums, *, seq):
    normed = unit[...] * gain[...] + shift[...]
    total = normed + (dot(active[...], weight[...]) + bias[...])
    unit2, scale2 = norm_parts(total)
    out[...] = (unit2 * gain2[...] + shift2[...]).astype(BF16)
    tile = unit.shape[0]
    at = lax.broadcasted_iota(jnp.int32, (tile, 1), 0)
    live = jnp.zeros((tile, 1), jnp.bool_)
    for pair in range(tile // seq):
        count = captions[pl.program_id(0) * (tile // seq) + pair] + 2 + REGIONS
        live = live | ((at >= pair * seq) & (at < pair * seq + count))
    upstream = jnp.where(live, cotangent[...].astype(F32), 0.0)
    second = norm_back(upstream, unit2, scale2, gain2[...])
    grad[...] = second
    low[...] = second.astype(BF16)
    add_sums(sums, (upstream * unit2, upstream, second))


def second_norm(captions, active, weight, bias, unit, gain, shift, gain2, shift2, cotangent, seq):
    rows, width = unit.shape
    hidden = active.shape[1]
    tile = rows_of(rows, 416)
    block = pl.BlockSpec((tile, width), lambda i, c: (i, 0))
    row = whole((1, width))
    return pl.pallas_call(
        functools.partial(second_kernel, seq=seq),
        grid_spec=pltpu.PrefetchScalarGridSpec(
            num_scalar_prefetch=1,
            grid=(rows // tile,),
            in_specs=[
                pl.BlockSpec((tile, hidden), lambda i, c: (i, 0)),
                whole((hidden, width)),
                row, block, row, row, row, row, block,
            ],
            out_specs=[block, block, block, whole((8, width))],
        ),
        out_shape=[
            jax.ShapeDtypeStruct((rows, width), BF16),
            jax.ShapeDtypeStruct((rows, width), BF16),
            jax.ShapeDtypeStruct((rows, width), F32),
            jax.ShapeDtypeStruct((8, width), F32),
        ],
        compiler_params=params(),
        cost_estimate=cost(2 * rows * width * hidden, 2 * hidden * width + 2 * rows * hidden + 14 * rows * width),
        name="second_norm",
    )(captions, active, weight, bias, unit, gain, shift, gain2, shift2, cotangent)


def hidden_back_kernel(low, weight, slope, out, sums):
    grad = dot(low[...], weight[...], NT) * slope[...].astype(F32)
    out[...] = grad.astype(BF16)
    sums[...] = jnp.sum(grad, axis=0, keepdims=True)


def hidden_back(low, weight, slope):
    rows, width = low.shape
    hidden = weight.shape[0]
    tile = tile_of(hidden, 768)
    return pl.pallas_call(
        hidden_back_kernel,
        grid=(hidden // tile,),
        in_specs=[
            whole((rows, width)),
            pl.BlockSpec((tile, width), lambda i: (i, 0)),
            pl.BlockSpec((rows, tile), lambda i: (0, i)),
        ],
        out_specs=[
            pl.BlockSpec((rows, tile), lambda i: (0, i)),
            pl.BlockSpec((1, tile), lambda i: (0, i)),
        ],
        out_shape=[
            jax.ShapeDtypeStruct((rows, hidden), BF16),
            jax.ShapeDtypeStruct((1, hidden), F32),
        ],
        compiler_params=params(),
        cost_estimate=cost(2 * rows * width * hidden, 2 * hidden * width + 4 * rows * hidden),
        name="hidden_back",
    )(low, weight, slope)


def first_back_kernel(hidden, weight, second, unit, scale, gain, out_weight, grad, low, context_grad, sums):
    normed_grad = dot(hidden[...], weight[...], NT) + second[...]
    first = norm_back(normed_grad, unit[...], scale[...], gain[...])
    grad[...] = first
    first_low = first.astype(BF16)
    low[...] = first_low
    context_grad[...] = dot(first_low, out_weight[...], NT).astype(BF16)
    add_sums(sums, (normed_grad * unit[...], normed_grad, first))


def first_back(hidden, weight, second, unit, scale, gain, out_weight):
    rows, width = second.shape
    columns = hidden.shape[1]
    tile = rows_of(rows, 416)
    block = pl.BlockSpec((tile, width), lambda i: (i, 0))
    return pl.pallas_call(
        first_back_kernel,
        grid=(rows // tile,),
        in_specs=[
            pl.BlockSpec((tile, columns), lambda i: (i, 0)),
            whole((width, columns)),
            block, block,
            pl.BlockSpec((tile, 1), lambda i: (i, 0)),
            whole((1, width)),
            whole((width, width)),
        ],
        out_specs=[block, block, block, whole((8, width))],
        out_shape=[
            jax.ShapeDtypeStruct((rows, width), F32),
            jax.ShapeDtypeStruct((rows, width), BF16),
            jax.ShapeDtypeStruct((rows, width), BF16),
            jax.ShapeDtypeStruct((8, width), F32),
        ],
        compiler_params=params(),
        cost_estimate=cost(2 * rows * width * (columns + width), 2 * columns * width + 2 * rows * columns + 16 * rows * width),
        name="first_back",
    )(hidden, weight, second, unit, scale, gain, out_weight)


def token_back_kernel(grads, weight, first, out):
    out[...] = dot(grads[...], weight[...], NT) + first[...]


def token_back(grads, weight, first):
    rows, width = first.shape
    columns = grads.shape[1]
    tile = rows_of(rows, 416)
    block = pl.BlockSpec((tile, width), lambda i: (i, 0))
    return pl.pallas_call(
        token_back_kernel,
        grid=(rows // tile,),
        in_specs=[pl.BlockSpec((tile, columns), lambda i: (i, 0)), whole((width, columns)), block],
        out_specs=block,
        out_shape=jax.ShapeDtypeStruct((rows, width), F32),
        compiler_params=params(),
        cost_estimate=cost(2 * rows * width * columns, 2 * columns * (width + rows) + 8 * rows * width),
        name="token_back",
    )(grads, weight, first)


def weight_grad_kernel(left, right, out):
    out[...] = dot(left[...], right[...], TN).astype(BF16)


def weight_grad(left, right):
    rows, height = left.shape
    columns = right.shape[1]
    tile = tile_of(columns, 768)
    high = tile_of(height, 768)
    return pl.pallas_call(
        weight_grad_kernel,
        grid=(height // high, columns // tile),
        in_specs=[
            pl.BlockSpec((rows, high), lambda i, j: (0, i)),
            pl.BlockSpec((rows, tile), lambda i, j: (0, j)),
        ],
        out_specs=pl.BlockSpec((high, tile), lambda i, j: (i, j)),
        out_shape=jax.ShapeDtypeStruct((height, columns), BF16),
        compiler_params=params(),
        cost_estimate=cost(2 * rows * height * columns, 2 * (rows * height + rows * columns + height * columns)),
        name="weight_grad",
    )(left, right)


def gather(values):
    return lax.all_gather(values, "fsdp", axis=0, tiled=True)


def local(
    tokens,
    captions,
    cotangent,
    project_weight,
    project_bias,
    output_weight,
    output_bias,
    first_gain,
    first_shift,
    expand_weight,
    expand_bias,
    shrink_weight,
    shrink_bias,
    second_gain,
    second_shift,
):
    pairs, seq, width = tokens.shape
    rows = pairs * seq
    parts = lax.axis_size("fsdp")
    token_rows = tokens.reshape(rows, width)
    cot_rows = cotangent.reshape(rows, width)

    vectors = (project_bias, output_bias, first_gain, first_shift, expand_bias, shrink_bias, second_gain, second_shift)
    packed = gather(jnp.concatenate(vectors)[None, :])
    full, at = [], 0
    for vector in vectors:
        size = vector.shape[0]
        full.append(packed[:, at : at + size].reshape(1, parts * size).astype(F32))
        at += size
    bias_row, out_bias, gain1, shift1, hidden_bias, down_bias, gain2, shift2 = full
    bias_full = jnp.concatenate([bias_row[:, :width], jnp.zeros((1, width), F32), bias_row[:, width:]], axis=1)
    project = gather(project_weight)
    output = gather(output_weight)
    expand = gather(expand_weight)
    shrink = gather(shrink_weight)

    joined = join(token_rows, project, bias_full)
    joined3 = joined.reshape(pairs, seq, 3 * width)
    context, probs = attend(joined3, captions)
    context_rows = context.reshape(rows, width)
    unit1, scale1, normed_low = first_norm(context_rows, output, out_bias, token_rows, gain1, shift1)
    active, slope = expand_act(normed_low, expand, hidden_bias)
    out_rows, shrink_low, second_grad, sums2 = second_norm(
        captions, active, shrink, down_bias, unit1, gain1, shift1, gain2, shift2, cot_rows, seq
    )
    grad_shrink = weight_grad(active, shrink_low)
    expand_low, sums_hidden = hidden_back(shrink_low, shrink, slope)
    grad_expand = weight_grad(normed_low, expand_low)
    first_grad, branch_low, context_grad, sums1 = first_back(
        expand_low, expand, second_grad, unit1, scale1, gain1, output
    )
    grad_output = weight_grad(context_rows, branch_low)
    joined_grad, sums_joined = attend_back(joined3, probs, context_grad.reshape(pairs, seq, width))
    joined_grad_rows = joined_grad.reshape(rows, 3 * width)
    grad_project = weight_grad(token_rows, joined_grad_rows)
    token_grad = token_back(joined_grad_rows, project, first_grad)

    def owned(grad):
        part = lax.psum_scatter(grad, "fsdp", scatter_dimension=0, tiled=True)
        return lax.psum(part, "dp").astype(F32)

    small = (sums_joined[0], sums1[2], sums1[0], sums1[1], sums_hidden[0], sums2[2], sums2[0], sums2[1])
    packed_grad = jnp.concatenate([v.reshape(parts, -1) for v in small], axis=1).reshape(-1)
    shard = lax.psum(lax.psum_scatter(packed_grad, "fsdp", scatter_dimension=0, tiled=True), "dp")
    smalls, at = [], 0
    for vector in vectors:
        smalls.append(shard[at : at + vector.shape[0]])
        at += vector.shape[0]
    return (
        out_rows.reshape(pairs, seq, width),
        token_grad.reshape(pairs, seq, width),
        owned(grad_project),
        smalls[0],
        owned(grad_output),
        smalls[1],
        smalls[2],
        smalls[3],
        owned(grad_expand),
        smalls[4],
        owned(grad_shrink),
        smalls[5],
        smalls[6],
        smalls[7],
    )


def solution(mesh):
    rows3 = P(("dp", "fsdp"), None, None)
    matrix, vector = P("fsdp", None), P("fsdp")
    return jax.shard_map(
        local,
        mesh=mesh,
        in_specs=(
            rows3, P(("dp", "fsdp")), rows3,
            matrix, vector, matrix, vector, vector, vector,
            matrix, vector, matrix, vector, vector, vector,
        ),
        out_specs=(
            rows3, rows3,
            matrix, vector, matrix, vector, vector, vector,
            matrix, vector, matrix, vector, vector, vector,
        ),
        check_vma=False,
    )
```

time: 677 us -> 492 us (0.73)
  matrix products: 135 us -> 0 us
  Pallas kernels: 0 us -> 129 us
  local copies, waits for them, and re-layouts: 117 us -> 15.5 us
  other arithmetic: 38.6 us -> 7.56 us
  blocking collectives: 80.6 us -> 52.3 us
  waiting for transfers between devices: 282 us -> 271 us
    dot_general x18 -> x0, matrix products: 135 us -> none  [the longest x4 35.6 us: against(): lax.dot_general(left, right, (((1,), (1,)), ((), ())), preferred_element_...]
    pallas_call x0 -> x13, Pallas kernels: none -> 129 us  [the longest x4 29.6 us: weight_grad(): pl.pallas_call(weight_grad_kernel, grid=(height // high, columns // tile)...]
    all_gather x4, waiting for transfers between devices: 50.4 us -> 105 us  [gather(): return lax.all_gather(values, 'fsdp', axis=0, tiled=True)]
    reduce_scatter x3 -> x4, waiting for transfers between devices: 196 us -> 146 us  [owned(): part = lax.psum_scatter(grad, 'fsdp', scatter_dimension=0, tiled=True)]
    unnamed x66 -> x15, local copies, waits for them, and re-layouts: 40.2 us -> 1.31 us
    reshape x5 -> x1, local copies, waits for them, and re-layouts: 35.8 us -> 0.01 us  [local(): jnp.concatenate([v.reshape(parts, -1) for v in small], axis=1).reshape(-1)]
    unnamed x2 -> x1, blocking collectives: 57.9 us -> 26.4 us
    unnamed x10 -> x9, waiting for transfers between devices: 22.5 us -> 2.66 us
  transfers between devices with their start and end apart: 9 -> 9, of which waited for: 6 -> 7; matrix products, arithmetic and copies ran while one was open for 35% -> 3% of each run, Pallas kernels for 0% -> 18%
where the time goes in v1:
time: 492 us; the launch traced here: 490 us
  waiting for transfers between devices  271 us (55%)
  Pallas kernels  129 us (26%)
  blocking collectives  52.3 us (11%)
  local copies, waits for them, and re-layouts  15.5 us (3%)
  between operations  14.6 us (3%)
  other arithmetic  7.56 us (2%)
    reduce_scatter x4, waiting for transfers between devices, owned(): part = lax.psum_scatter(grad, 'fsdp', scatter_dimension=0, tiled=True)  146 us
    all_gather x4, waiting for transfers between devices, gather(): return lax.all_gather(values, 'fsdp', axis=0, tiled=True)  105 us
    pallas_call x4, Pallas kernels, weight_grad(): pl.pallas_call(weight_grad_kernel, grid=(height // high, columns // tile)...  29.6 us
    unnamed x1, blocking collectives  26.4 us
    psum x1, waiting for transfers between devices, owned(): return lax.psum(part, 'dp').astype(F32)  16.8 us
    pallas_call x1, Pallas kernels, attend(): pl.pallas_call(attend_kernel, grid_spec=pltpu.PrefetchScalarGridSpec(num_...  16.6 us
    all_gather x1, blocking collectives, gather(): return lax.all_gather(values, 'fsdp', axis=0, tiled=True)  16 us
    pallas_call x1, Pallas kernels, attend_back(): pl.pallas_call(attend_back_kernel, grid=(pairs,), in_specs=[pl.BlockSpec(...  15.6 us
  transfers between devices with their start and end apart: 9, of which 7 were waited for; matrix products, arithmetic and copies ran while one was open for 3% of the time, Pallas kernels for 18%

profile of v1, /device:TPU:0, one launch (start us, length us, event | category | flops | bytes accessed | tf_op | source)
XLA Modules:
  0.0 490.5 jit_solution(6489907290291250201)
XLA Ops:
  8.0 0.7 all-gather.9.cloned.1.call-update
  8.7 0.7 all-gather.11.cloned.1.call-update
  10.0 5.4 %concatenate.9 = bf16[1152]{0:T(1024)(128)(2,1)S(1)} concatenate(bf16[192]{0:T(256)(128)(2,1)} %param.19, bf16[96]{0:T(256)(128)(2,1)} %param.21, bf16[96]{0:T(256)(128)(2,1)} %param.22, bf16[96]{0:T(256)(128)(2,1)} %param.23, bf16[384]{0:T(512)(128)(2,1)} %param.25, bf16[96]{0:T(256)(128)(2,1)} %param.27, bf16[96]{0:T(256)(128)(2,1)} %param.28, bf16[96]{0:T(256)(128)(2,1)} %param.29), dimensions={0} | concatenate | bytes 4608 | tf_op jit(solution)/shard_map/concatenate | solution.py:464
  15.5 16.0 %all-gather.1 = bf16[8,1,1152]{2,1,0:T(2,128)(2,1)S(1)} all-gather(bf16[1,1,1152]{2,1,0:T(2,128)(2,1)S(1)} %reshape.193), channel_id=2, replica_groups=mesh['dp'=4,'fsdp'=8] {'fsdp'}, dimensions={0}, use_global_device_ids=true | all-gather | bytes 20736 | tf_op jit(solution)/shard_map/all_gather | solution.py:437
  36.9 17.2 %all-gather.7.cloned.1.call-done.weight = bf16[768,2304]{1,0:T(8,128)(2,1)} async-done(((bf16[96,2304]{1,0:T(8,128)(2,1)}), bf16[768,2304]{1,0:T(8,128)(2,1)}) %all-gather.7.cloned.1.call-update) | async-done | bytes 3538960 | tf_op jit(solution)/shard_map/all_gather | solution.py:437
  54.1 7.2 %join.1 = bf16[832,2304]{1,0:T(8,128)(2,1)} custom-call(bf16[832,768]{1,0:T(8,128)(2,1)} %bitcast.23, bf16[768,2304]{1,0:T(8,128)(2,1)} %all-gather.7.cloned.1.call-done.weight, f32[1,2304]{1,0:T(1,128)} %fusion.bias), custom_call_target="tpu_custom_call" | custom-call | flops 2944401408 | bytes 7372800 | tf_op jit(solution)/shard_map/join/pallas_call | solution.py:55
  61.3 16.6 %attend.1 = (bf16[8,104,768]{2,1,0:T(8,128)(2,1)}, bf16[8,6,104,256]{3,2,1,0:T(8,128)(2,1)}) custom-call(s32[8]{0:T(128)} %captions.3, bf16[8,104,2304]{2,1,0:T(8,128)(2,1)} %bitcast.16), custom_call_target="tpu_custom_call" | custom-call | flops 654311424 | bytes 3833856 | tf_op jit(solution)/shard_map/attend/pallas_call | solution.py:109
  78.0 5.2 %first_norm.1 = (f32[832,768]{1,0:T(8,128)}, f32[832,1]{1,0:T(8,128)}, bf16[832,768]{1,0:T(8,128)(2,1)}) custom-call(bf16[832,768]{1,0:T(8,128)(2,1)} %bitcast.18, bf16[768,768]{1,0:T(8,128)(2,1)} %all-gather.9.cloned.1.call-done.weight.out_weight, f32[1,768]{1,0:T(1,128)} %reshape.185.bias, bf16[832,768]{1,0:T(8,128)(2,1)} %bitcast.24, ...), custom_call_target="tpu_custom_call" | custom-call | flops 981467136 | bytes 7569408 | tf_op jit(solution)/shard_map/first_norm/pallas_call | solution.py:227
  83.1 47.4 %all-gather.11.cloned.1.call-done.weight = bf16[768,3072]{1,0:T(8,128)(2,1)} async-done(((bf16[96,3072]{1,0:T(8,128)(2,1)}), bf16[768,3072]{1,0:T(8,128)(2,1)}) %all-gather.11.cloned.1.call-update) | async-done | bytes 4718608 | tf_op jit(solution)/shard_map/all_gather | solution.py:437
  130.5 11.4 %expand_act.1 = (bf16[832,3072]{1,0:T(8,128)(2,1)}, bf16[832,3072]{1,0:T(8,128)(2,1)}) custom-call(bf16[832,768]{1,0:T(8,128)(2,1)} %get-tuple-element.34.normed_low.left, bf16[768,3072]{1,0:T(8,128)(2,1)} %all-gather.11.cloned.1.call-done.weight, f32[1,3072]{1,0:T(1,128)} %bitcast.30), custom_call_target="tpu_custom_call" | custom-call | flops 3925868544 | bytes 14942208 | tf_op jit(solution)/shard_map/expand_act/pallas_call | solution.py:256
  141.9 40.7 %all-gather.13.cloned.1.call-done.weight = bf16[3072,768]{1,0:T(8,128)(2,1)} async-done(((bf16[384,768]{1,0:T(8,128)(2,1)}), bf16[3072,768]{1,0:T(8,128)(2,1)}) %all-gather.13.cloned.1.call-update) | async-done | bytes 4718608 | tf_op jit(solution)/shard_map/all_gather | solution.py:437
  182.5 12.7 %second_norm.1 = (bf16[832,768]{1,0:T(8,128)(2,1)}, bf16[832,768]{1,0:T(8,128)(2,1)}, f32[832,768]{1,0:T(8,128)}, f32[8,768]{1,0:T(8,128)}) custom-call(s32[8]{0:T(128)} %captions.3, bf16[832,3072]{1,0:T(8,128)(2,1)} %get-tuple-element.35.active.left, bf16[3072,768]{1,0:T(8,128)(2,1)} %all-gather.13.cloned.1.call-done.weight, f32[1,768]{1,0:T(1,128)} %reshape.189.bias, ...), custom_call_target="tpu_custom_call" | custom-call | flops 3925868544 | bytes 18776064 | tf_op jit(solution)/shard_map/second_norm/pallas_call | solution.py:296
  195.2 9.3 %hidden_back.1 = (bf16[832,3072]{1,0:T(8,128)(2,1)}, f32[1,3072]{1,0:T(1,128)}) custom-call(bf16[832,768]{1,0:T(8,128)(2,1)} %get-tuple-element.39.low.right, bf16[3072,768]{1,0:T(8,128)(2,1)} %all-gather.13.cloned.1.call-done.weight, bf16[832,3072]{1,0:T(8,128)(2,1)} %get-tuple-element.40.slope), custom_call_target="tpu_custom_call" | custom-call | flops 3925868544 | bytes 14942208 | tf_op jit(solution)/shard_map/hidden_back/pallas_call | solution.py:330
  204.5 14.3 %first_back.1 = (f32[832,768]{1,0:T(8,128)}, bf16[832,768]{1,0:T(8,128)(2,1)}, bf16[832,768]{1,0:T(8,128)(2,1)}, f32[8,768]{1,0:T(8,128)}) custom-call(bf16[832,3072]{1,0:T(8,128)(2,1)} %get-tuple-element.41.hidden.right, bf16[768,3072]{1,0:T(8,128)(2,1)} %all-gather.11.cloned.1.call-done.weight, f32[832,768]{1,0:T(8,128)} %get-tuple-element.42.second, ...), custom_call_target="tpu_custom_call" | custom-call | flops 4907335680 | bytes 20054016 | tf_op jit(solution)/shard_map/first_back/pallas_call | solution.py:367
  218.8 4.1 weight_grad.5
  223.0 15.6 %attend_back.1 = (bf16[8,104,2304]{2,1,0:T(8,128)(2,1)}, f32[1,1536]{1,0:T(1,128)}) custom-call(bf16[8,104,2304]{2,1,0:T(8,128)(2,1)} %bitcast.17, bf16[8,6,104,256]{3,2,1,0:T(8,128)(2,1)} %get-tuple-element.38.probs, bf16[8,104,768]{2,1,0:T(8,128)(2,1)} %bitcast.26), custom_call_target="tpu_custom_call" | custom-call | flops 1635778560 | bytes 9584640 | tf_op jit(solution)/shard_map/attend_back/pallas_call | solution.py:168
  238.6 7.4 %weight_grad.4 = bf16[768,2304]{1,0:T(8,128)(2,1)} custom-call(bf16[832,768]{1,0:T(8,128)(2,1)} %bitcast.25, bf16[832,2304]{1,0:T(8,128)(2,1)} %bitcast.20), custom_call_target="tpu_custom_call" | custom-call | flops 2944401408 | bytes 8650752 | tf_op jit(solution)/shard_map/weight_grad/pallas_call | solution.py:421
  246.1 8.9 %weight_grad.7 = bf16[3072,768]{1,0:T(8,128)(2,1)} custom-call(bf16[832,3072]{1,0:T(8,128)(2,1)} %get-tuple-element.35.active.left, bf16[832,768]{1,0:T(8,128)(2,1)} %get-tuple-element.39.low.right), custom_call_target="tpu_custom_call" | custom-call | flops 3925868544 | bytes 11108352 | tf_op jit(solution)/shard_map/weight_grad/pallas_call | solution.py:421
  255.0 9.1 %weight_grad.6 = bf16[768,3072]{1,0:T(8,128)(2,1)} custom-call(bf16[832,768]{1,0:T(8,128)(2,1)} %get-tuple-element.34.normed_low.left, bf16[832,3072]{1,0:T(8,128)(2,1)} %get-tuple-element.41.hidden.right), custom_call_target="tpu_custom_call" | custom-call | flops 3925868544 | bytes 11108352 | tf_op jit(solution)/shard_map/weight_grad/pallas_call | solution.py:421
  264.3 34.6 %reduce-scatter.5.cloned.1.call-done = bf16[96,2304]{1,0:T(8,128)(2,1)} async-done(((bf16[768,2304]{1,0:T(8,128)(2,1)}), bf16[96,2304]{1,0:T(8,128)(2,1)}) %reduce-scatter.5.cloned.1.call-update) | async-done | bytes 442384 | tf_op jit(solution)/shard_map/reduce_scatter | solution.py:499
  298.9 55.9 %reduce-scatter.11.cloned.1.call-done = bf16[384,768]{1,0:T(8,128)(2,1)} async-done(((bf16[3072,768]{1,0:T(8,128)(2,1)}), bf16[384,768]{1,0:T(8,128)(2,1)}) %reduce-scatter.11.cloned.1.call-update) | async-done | bytes 589840 | tf_op jit(solution)/shard_map/reduce_scatter | solution.py:499
  354.8 55.7 %reduce-scatter.9.cloned.1.call-done = bf16[96,3072]{1,0:T(8,128)(2,1)} async-done(((bf16[768,3072]{1,0:T(8,128)(2,1)}), bf16[96,3072]{1,0:T(8,128)(2,1)}) %reduce-scatter.9.cloned.1.call-update) | async-done | bytes 589840 | tf_op jit(solution)/shard_map/reduce_scatter | solution.py:499
  411.9 0.9 slice_reduce_fusion.3
  414.2 0.9 slice_reduce_fusion
  415.4 26.4 %all-reduce = f32[9216]{0:T(1024)S(1)} all-reduce(f32[9216]{0:T(1024)S(1)} %reshape.183), channel_id=4, replica_groups=mesh['dp'=4,'fsdp'=8] {'fsdp'}, use_global_device_ids=true, to_apply=%region_2.0.clone | all-reduce | flops 9216 | bytes 73728
  441.8 10.0 %psum.36 = f32[1152]{0:T(1024)S(1)} all-reduce(f32[1152]{0:T(1024)S(1)} %dynamic-slice.1), channel_id=1, replica_groups=mesh['dp'=4,'fsdp'=8] {'dp'}, use_global_device_ids=true, to_apply=%region_3.0 | all-reduce | flops 1152 | bytes 9216 | tf_op jit(solution)/shard_map/psum | solution.py:504
  453.6 7.4 %token_back.1 = f32[832,768]{1,0:T(8,128)} custom-call(bf16[832,2304]{1,0:T(8,128)(2,1)} %bitcast.21, bf16[768,2304]{1,0:T(8,128)(2,1)} %all-gather.7.cloned.1.call-done.weight, f32[832,768]{1,0:T(8,128)} %get-tuple-element.46.first), custom_call_target="tpu_custom_call" | custom-call | flops 2944401408 | bytes 12484608 | tf_op jit(solution)/shard_map/token_back/pallas_call | solution.py:400
  461.0 16.8 %all-reduce.4.cloned.1.call-done = (bf16[96,2304]{1,0:T(8,128)(2,1)}, bf16[96,768]{1,0:T(8,128)(2,1)}, bf16[96,3072]{1,0:T(8,128)(2,1)}, bf16[384,768]{1,0:T(8,128)(2,1)}) async-done(((bf16[96,2304]{1,0:T(8,128)(2,1)}, bf16[96,768]{1,0:T(8,128)(2,1)}, bf16[96,3072]{1,0:T(8,128)(2,1)}, bf16[384,768]{1,0:T(8,128)(2,1)}), (bf16[96,2304]{1,0:T(8,128)(2,1)}, bf16[96,768]{1,0:T(8,128)(2,1)}, ...) | async-done | bytes 1769488 | tf_op jit(solution)/shard_map/psum | solution.py:500
  477.9 2.2 convert_element_type.79
  480.1 2.2 convert_element_type.80
  482.2 1.0 convert_element_type.77
  483.2 0.7 convert_element_type.78
  (63 shorter events, 11.4 us)
Async XLA Ops:
  7.2 46.9 %all-gather.7.cloned.1.call-start = ((), (), s32[]{:S(2)}) async-start(), calls=%async_computation.4 | async-start | bytes 3981312 | tf_op jit(solution)/shard_map/all_gather | solution.py:437
  7.9 70.0 %all-gather.9.cloned.1.call-start = ((), (), s32[]{:S(2)}) async-start(), calls=%async_computation.5 | async-start | bytes 1327104 | tf_op jit(solution)/shard_map/all_gather | solution.py:437
  8.7 121.8 %all-gather.11.cloned.1.call-start = ((), (), s32[]{:S(2)}) async-start(), calls=%async_computation.6 | async-start | bytes 5308416 | tf_op jit(solution)/shard_map/all_gather | solution.py:437
  9.4 173.1 %all-gather.13.cloned.1.call-start = ((), (), s32[]{:S(2)}) async-start(), calls=%async_computation.7 | async-start | bytes 5308416 | tf_op jit(solution)/shard_map/all_gather | solution.py:437
  10.0 254.3 %reduce-scatter.7.cloned.1.call-start = ((), (), s32[]{:S(2)}) async-start(), calls=%async_computation.9 | async-start | bytes 1327104 | tf_op jit(solution)/shard_map/reduce_scatter | solution.py:499
  222.9 75.9 %reduce-scatter.5.cloned.1.call-start = ((), (), s32[]{:S(2)}) async-start(), calls=%async_computation.8 | async-start | bytes 3981312 | tf_op jit(solution)/shard_map/reduce_scatter | solution.py:499
  246.0 108.7 %reduce-scatter.11.cloned.1.call-start = ((), (), s32[]{:S(2)}) async-start(), calls=%async_computation.11 | async-start | bytes 5308416 | tf_op jit(solution)/shard_map/reduce_scatter | solution.py:499
  255.0 155.5 %reduce-scatter.9.cloned.1.call-start = ((), (), s32[]{:S(2)}) async-start(), calls=%async_computation.10 | async-start | bytes 5308416 | tf_op jit(solution)/shard_map/reduce_scatter | solution.py:499
  264.2 146.4 %copy-start.4 = (u32[32]{0:T(128)S(1)}, u32[32]{0:T(128)}, u32[]{:S(2)}) copy-start(u32[32]{0:T(128)} %constant.7) | copy-start | bytes 388
  264.2 147.6 %copy-start.3 = (f32[1,1536]{1,0:T(1,128)S(1)}, f32[1,1536]{1,0:T(1,128)}, u32[]{:S(2)}) copy-start(f32[1,1536]{1,0:T(1,128)} %get-tuple-element.47) | copy-start | bytes 18436
  264.2 149.3 %copy-start.2 = (f32[1,3072]{1,0:T(1,128)S(1)}, f32[1,3072]{1,0:T(1,128)}, u32[]{:S(2)}) copy-start(f32[1,3072]{1,0:T(1,128)} %get-tuple-element.49) | copy-start | bytes 36868
  264.2 213.7 %all-reduce.4.cloned.1.call-start = ((), (), s32[]{:S(2)}) async-start(), calls=%async_computation.12 | async-start | bytes 3538944 | tf_op jit(solution)/shard_map/psum | solution.py:500
  477.8 4.4 copy-start
  477.8 5.4 %copy-start.1 = (bf16[96,768]{1,0:T(8,128)(2,1)S(1)}, bf16[96,768]{1,0:T(8,128)(2,1)}, u32[]{:S(2)}) copy-start(bf16[96,768]{1,0:T(8,128)(2,1)} %get-tuple-element.59) | copy-start | bytes 442372
Sparse Core Ops, SparseCore 0:
  9.7 44.3 all-gather.6
  55.7 21.7 all-gather.8
  79.2 51.2 all-gather.10
  132.0 50.5 all-gather.12
  223.0 31.6 reduce-scatter.6
  256.9 41.8 reduce-scatter.4
  301.3 53.4 reduce-scatter.10
  357.2 53.2 reduce-scatter.8
  414.3 63.4 all-reduce.3

commit v2 on v1

v2 whole, which is shorter than its diff:
```python
import functools

import jax
import jax.numpy as jnp
from jax import lax
from jax.experimental import pallas as pl
from jax.experimental.pallas import tpu as pltpu
from jax.sharding import PartitionSpec as P

HEADS = 12
HEAD_DIM = 64
REGIONS = 36
BF16 = jnp.bfloat16
F32 = jnp.float32

COVER = 100 * 10**9

NN = (((1,), (0,)), ((), ()))
NT = (((1,), (1,)), ((), ()))
TN = (((0,), (0,)), ((), ()))


def dot(left, right, dims=NN):
    return lax.dot_general(left, right, dims, preferred_element_type=F32)


def params(mebibytes):
    return pltpu.CompilerParams(vmem_limit_bytes=mebibytes * 1024 * 1024)


def cost(flops=0):
    return pl.CostEstimate(flops=flops, bytes_accessed=0, transcendentals=0)


def whole(shape, buffers=None):
    mode = None if buffers is None else pl.Buffered(buffers)
    return pl.BlockSpec(shape, lambda *at: (0,) * len(shape), pipeline_mode=mode)


HELD = pl.BlockSpec(memory_space=pltpu.VMEM)


def inside(shape, dtype=BF16):
    return pltpu.VMEM(shape, dtype)


def outside(shape, dtype=BF16):
    return pltpu.HBM(shape, dtype)


def in_vmem(values):
    return pltpu.with_memory_space_constraint(values, pltpu.VMEM)


def in_hbm(values):
    return pltpu.with_memory_space_constraint(values, pltpu.HBM)


def tile_of(size, most):
    return max(t for t in range(128, most + 1, 128) if size % t == 0)


def rows_of(count, most):
    fits = [t for t in range(16, most + 1, 16) if count % t == 0]
    return max(fits) if fits else count


def chip_of(pos, flip):
    return pos[0] ^ flip


def halves_copies(refs, into, pos, high, wide):
    half = wide // 2
    rows = high // 2
    for side in range(2):
        core = pos[1] if side == 0 else 1 - pos[1]
        shard = pos[0] * 2 + core
        yield refs[side], into.at[pl.ds(pl.multiple_of(shard * high, 16), high), :]
        for flip in range(4):
            buffer, at = refs[2 + side * 2 + (flip > 0)], max(flip - 1, 0) * 3 * rows
            up = pos[2] ^ (flip // 2)
            along = pos[3] ^ (flip % 2)
            for back in range(1, 4):
                shard = chip_of(pos, back) * 2 + core
                to_row = pl.multiple_of(shard * high + up * rows, 16)
                to_column = pl.multiple_of(along * half, 128)
                yield (
                    buffer.at[pl.ds(at + (back - 1) * rows, rows), :],
                    into.at[pl.ds(to_row, rows), pl.ds(to_column, half)],
                )


def stacked_copies(refs, into, pos, high, wide):
    rows = high // 8
    for side in range(2):
        core = pos[1] if side == 0 else 1 - pos[1]
        shard = pos[0] * 2 + core
        yield refs[side], into.at[pl.ds(pl.multiple_of(shard * high, 16), high), :]
        for flip in range(4):
            buffer, at = refs[2 + side * 2 + (flip > 0)], max(flip - 1, 0) * 3 * rows
            quarter = (pos[2] * 2 + pos[3]) ^ flip
            for back in range(1, 4):
                shard = chip_of(pos, back) * 2 + core
                for part in range(2):
                    to_row = pl.multiple_of(shard * high + (quarter * 2 + part) * rows, 16)
                    yield (
                        buffer.at[pl.ds(at + (back - 1) * rows, rows), pl.ds(part * wide, wide)],
                        into.at[pl.ds(to_row, rows), :],
                    )


MOST_PIECES = 64


def assemble(copies, refs, into, pos, sems):
    started = [
        pltpu.make_async_copy(source, target, sems.at[at])
        for at, (source, target) in enumerate(copies(refs, into, pos))
    ]
    for copy in started:
        copy.start()
    for copy in started:
        copy.wait()


ANYWHERE = pl.BlockSpec(memory_space=pl.ANY)


def natural_copies(refs, into, pos):
    yield refs[0], into


class Weight:
    def __init__(self, shape, arrays, copies=natural_copies):
        self.shape, self.copies = shape, copies
        self.arrays = [in_hbm(array) for array in arrays]

    def specs(self):
        return [ANYWHERE] * len(self.arrays)

    def out(self):
        return inside(self.shape)

    def scratch(self):
        return [pltpu.SemaphoreType.DMA((MOST_PIECES,))]

    def split(self, refs):
        return refs[: len(self.arrays)], refs[len(self.arrays) : -2], refs[-2], refs[-1]

    def arrive(self, refs, full, pos, sems):
        @pl.when(pl.program_id(0) == 0)
        def _():
            assemble(self.copies, refs, full, pos, sems)


def spread_kernel(pos, own, other, bias, hidden, rows, held):
    part = held.shape[2] * 3 // 4
    for back in range(4):
        held[chip_of(pos, back) * 2 + pos[1]] = own[back * 16 : back * 16 + 16].astype(F32)
        held[chip_of(pos, back) * 2 + 1 - pos[1]] = other[back * 16 : back * 16 + 16].astype(F32)
    bias[...] = jnp.zeros_like(bias)
    width = rows.shape[1]
    for shard in range(8):
        for at in range(2):
            to = (shard * 2 + at) * part
            to += width if to >= width else 0
            bias[0:1, to : to + part] = held[shard, at : at + 1, :part]
        for at in range(4):
            to = (shard * 4 + at) * part
            hidden[0:1, to : to + part] = held[shard, 5 + at : 6 + at, :part]
        to = shard * part
        rows[0:3, to : to + part] = held[shard, 2:5, :part]
        rows[3:6, to : to + part] = held[shard, 9:12, :part]


def spread(pos, shards, width, hidden_width):
    shapes = [(1, 3 * width), (1, hidden_width), (8, width)]
    return pl.pallas_call(
        spread_kernel,
        grid_spec=pltpu.PrefetchScalarGridSpec(
            num_scalar_prefetch=1,
            grid=(1,),
            in_specs=[whole((64, 128))] * 2,
            out_specs=[whole(shape) for shape in shapes],
            scratch_shapes=[pltpu.VMEM((8, 16, 128), F32)],
        ),
        out_shape=[jax.ShapeDtypeStruct(shape, F32) for shape in shapes],
        compiler_params=params(4),
        cost_estimate=cost(COVER),
        name="spread",
    )(pos, *shards)


def bundle_kernel(joined, first, second, hidden, out):
    part = out.shape[2] * 3 // 4
    out[...] = jnp.zeros_like(out)
    for shard in range(8):
        for at in range(2):
            of = (shard * 2 + at) * part
            out[shard, at : at + 1, :part] = joined[0:1, of : of + part]
        for at in range(4):
            of = (shard * 4 + at) * part
            out[shard, 5 + at : 6 + at, :part] = hidden[0:1, of : of + part]
        of = shard * part
        out[shard, 2:5, :part] = first[0:3, of : of + part]
        out[shard, 9:12, :part] = second[0:3, of : of + part]


def bundle(joined, first, second, hidden):
    return pl.pallas_call(
        bundle_kernel,
        out_shape=jax.ShapeDtypeStruct((8, 16, 128), F32),
        compiler_params=params(4),
        cost_estimate=cost(),
        name="bundle",
    )(joined, first, second, hidden)


def step_of(size):
    return pl.ds(pl.multiple_of(pl.program_id(0) * size, 16), size)


def columns_of(size):
    return pl.ds(pl.multiple_of(pl.program_id(0) * size, 128), size)


def join_kernel(pos, tokens, bias, *rest, weight, tile):
    pieces, (out,), full, sems = weight.split(rest)
    weight.arrive(pieces, full, pos, sems)
    out[...] = (dot(tokens[...], full[:, columns_of(tile)]) + bias[...]).astype(BF16)


def join(pos, token_rows, weight, bias):
    rows, width = token_rows.shape
    columns = weight.shape[1]
    tile = tile_of(columns, 768)
    return pl.pallas_call(
        functools.partial(join_kernel, weight=weight, tile=tile),
        grid_spec=pltpu.PrefetchScalarGridSpec(
            num_scalar_prefetch=1,
            grid=(columns // tile,),
            in_specs=[whole((rows, width), 1), pl.BlockSpec((1, tile), lambda i, p: (0, i))] + weight.specs(),
            out_specs=[pl.BlockSpec((rows, tile), lambda i, p: (0, i)), HELD],
            scratch_shapes=weight.scratch(),
        ),
        out_shape=[outside((rows, columns)), weight.out()],
        compiler_params=params(14),
        cost_estimate=cost(),
        name="join",
    )(pos, token_rows, bias, *weight.arrays)


def head_stack(block, low_half, padded):
    rows = block.shape[0]
    filler = jnp.zeros((padded - rows, block.shape[1]), F32)
    first = jnp.where(low_half, block, 0.0)
    second = jnp.where(low_half, 0.0, block)
    return jnp.concatenate([first, filler, second, filler], axis=0).astype(BF16)


def attend_kernel(captions, joined, context, probs):
    seq = joined.shape[1]
    width = context.shape[2]
    padded = probs.shape[3] // 2
    valid = captions[pl.program_id(0)] + 2 + REGIONS
    keep = lax.broadcasted_iota(jnp.int32, (seq, 2 * padded), 0) < valid
    low_half = lax.broadcasted_iota(jnp.int32, (1, 2 * HEAD_DIM), 1) < HEAD_DIM
    for pair in range(HEADS // 2):
        at = pair * 2 * HEAD_DIM
        query = joined[0, :, at : at + 2 * HEAD_DIM].astype(F32)
        keys = joined[0, :, width + at : width + at + 2 * HEAD_DIM]
        values = joined[0, :, 2 * width + at : 2 * width + at + 2 * HEAD_DIM]
        stacked = head_stack(query, low_half, padded)
        scores = dot(keys, stacked, NT) * HEAD_DIM ** (-0.5)
        scores = jnp.where(keep, scores, -1000000000.0)
        top = jnp.max(scores, axis=0, keepdims=True)
        grown = jnp.exp(scores - top)
        total = jnp.sum(grown, axis=0, keepdims=True)
        prob = (grown * (1.0 / total)).astype(BF16)
        probs[0, pair] = prob
        mixed = dot(prob, values, TN)
        context[0, :, at : at + 2 * HEAD_DIM] = jnp.where(
            low_half, mixed[:seq], mixed[padded : padded + seq]
        ).astype(BF16)


def attend(joined, captions):
    pairs, seq, columns = joined.shape
    width = columns // 3
    padded = (seq + 127) // 128 * 128
    return pl.pallas_call(
        attend_kernel,
        grid_spec=pltpu.PrefetchScalarGridSpec(
            num_scalar_prefetch=1,
            grid=(pairs,),
            in_specs=[pl.BlockSpec((1, seq, columns), lambda i, c: (i, 0, 0))],
            out_specs=[
                pl.BlockSpec((1, seq, width), lambda i, c: (i, 0, 0)),
                pl.BlockSpec((1, HEADS // 2, seq, 2 * padded), lambda i, c: (i, 0, 0, 0)),
            ],
        ),
        out_shape=[
            inside((pairs, seq, width)),
            outside((pairs, HEADS // 2, seq, 2 * padded)),
        ],
        compiler_params=params(8),
        cost_estimate=cost(),
        name="attend",
    )(captions, in_hbm(joined))


def attend_back_kernel(joined, probs, grads, out, sums):
    seq = joined.shape[1]
    width = grads.shape[2]
    padded = probs.shape[3] // 2
    low_half = lax.broadcasted_iota(jnp.int32, (1, 2 * HEAD_DIM), 1) < HEAD_DIM

    @pl.when(pl.program_id(0) == 0)
    def _():
        sums[...] = jnp.zeros_like(sums)

    for pair in range(HEADS // 2):
        at = pair * 2 * HEAD_DIM
        query = joined[0, :, at : at + 2 * HEAD_DIM].astype(F32)
        keys = joined[0, :, width + at : width + at + 2 * HEAD_DIM]
        values = joined[0, :, 2 * width + at : 2 * width + at + 2 * HEAD_DIM]
        grad = grads[0, :, at : at + 2 * HEAD_DIM].astype(F32)
        query_stack = head_stack(query, low_half, padded)
        grad_stack = head_stack(grad, low_half, padded)
        prob = probs[0, pair]
        prob_full = prob.astype(F32)
        prob_grad = dot(values, grad_stack, NT)
        row_dot = jnp.sum(prob_full * prob_grad, axis=0, keepdims=True)
        score_grad = (prob_full * (prob_grad - row_dot) * HEAD_DIM ** (-0.5)).astype(BF16)
        values_grad = dot(prob, grad_stack)
        keys_grad = dot(score_grad, query_stack)
        mixed = dot(score_grad, keys, TN)
        query_grad = jnp.where(low_half, mixed[:seq], mixed[padded : padded + seq])
        out[0, :, at : at + 2 * HEAD_DIM] = query_grad.astype(BF16)
        out[0, :, width + at : width + at + 2 * HEAD_DIM] = keys_grad.astype(BF16)
        out[0, :, 2 * width + at : 2 * width + at + 2 * HEAD_DIM] = values_grad.astype(BF16)
        sums[:, at : at + 2 * HEAD_DIM] += jnp.sum(query_grad, axis=0, keepdims=True)
        sums[:, width + at : width + at + 2 * HEAD_DIM] += jnp.sum(values_grad, axis=0, keepdims=True)


def attend_back(joined, probs, grads):
    pairs, seq, columns = joined.shape
    width = columns // 3
    padded = probs.shape[3] // 2
    return pl.pallas_call(
        attend_back_kernel,
        grid=(pairs,),
        in_specs=[
            pl.BlockSpec((1, seq, columns), lambda i: (i, 0, 0)),
            pl.BlockSpec((1, HEADS // 2, seq, 2 * padded), lambda i: (i, 0, 0, 0)),
            pl.BlockSpec((1, seq, width), lambda i: (i, 0, 0)),
        ],
        out_specs=[
            pl.BlockSpec((1, seq, columns), lambda i: (i, 0, 0)),
            pl.BlockSpec((1, 2 * width), lambda i: (0, 0)),
        ],
        out_shape=[
            inside((pairs, seq, columns)),
            jax.ShapeDtypeStruct((1, 2 * width), F32),
        ],
        compiler_params=params(10),
        cost_estimate=cost(),
        name="attend_back",
    )(in_hbm(joined), in_hbm(probs), in_vmem(grads))


def norm_parts(values):
    centred = values - jnp.mean(values, axis=-1, keepdims=True)
    spread = jnp.mean(centred * centred, axis=-1, keepdims=True)
    scale = lax.rsqrt(spread + 1e-05)
    return centred * scale, scale


def norm_back(upstream, unit, scale, gain):
    scaled = upstream * gain
    return scale * (
        scaled
        - jnp.mean(scaled, axis=-1, keepdims=True)
        - unit * jnp.mean(scaled * unit, axis=-1, keepdims=True)
    )


def add_sums(sums, rows):
    @pl.when(pl.program_id(0) == 0)
    def _():
        sums[...] = jnp.zeros_like(sums)

    for at, values in enumerate(rows):
        sums[at : at + 1, :] += jnp.sum(values, axis=0, keepdims=True)


def first_kernel(pos, context, bias, tokens, gain, shift, *rest, weight):
    pieces, (unit, scale, normed_low), full, sems = weight.split(rest)
    weight.arrive(pieces, full, pos, sems)
    at = step_of(tokens.shape[0])
    total = tokens[...].astype(F32) + (dot(context[at, :], full[...]) + bias[...])
    unit_rows, scale_rows = norm_parts(total)
    unit[at, :] = unit_rows
    scale[at, :] = scale_rows
    normed_low[at, :] = (unit_rows * gain[...] + shift[...]).astype(BF16)


def first_norm(pos, context, weight, bias, token_rows, gain, shift):
    rows, width = token_rows.shape
    tile = rows_of(rows, 416)
    row = whole((1, width))
    return pl.pallas_call(
        functools.partial(first_kernel, weight=weight),
        grid_spec=pltpu.PrefetchScalarGridSpec(
            num_scalar_prefetch=1,
            grid=(rows // tile,),
            in_specs=[HELD, row, pl.BlockSpec((tile, width), lambda i, p: (i, 0)), row, row] + weight.specs(),
            out_specs=[HELD] * 4,
            scratch_shapes=weight.scratch(),
        ),
        out_shape=[inside((rows, width), F32), inside((rows, 1), F32), inside((rows, width)), weight.out()],
        compiler_params=params(14),
        cost_estimate=cost(),
        name="first_norm",
    )(pos, in_vmem(context), bias, token_rows, gain, shift, *weight.arrays)


def expand_kernel(pos, normed_low, bias, *rest, weight, tile):
    pieces, (active, slope), full, sems = weight.split(rest)
    weight.arrive(pieces, full, pos, sems)
    at = columns_of(tile)
    expand = dot(normed_low[...], full[:, at]) + bias[...]
    half = 0.5 * (1.0 + lax.erf(expand * 0.7071067811865476))
    active[:, at] = (expand * half).astype(BF16)
    slope[:, at] = (half + expand * jnp.exp(-0.5 * expand * expand) * 0.3989422804014327).astype(BF16)


def expand_act(pos, normed_low, weight, bias):
    rows, width = normed_low.shape
    columns = weight.shape[1]
    tile = tile_of(columns, 768)
    return pl.pallas_call(
        functools.partial(expand_kernel, weight=weight, tile=tile),
        grid_spec=pltpu.PrefetchScalarGridSpec(
            num_scalar_prefetch=1,
            grid=(columns // tile,),
            in_specs=[HELD, pl.BlockSpec((1, tile), lambda i, p: (0, i))] + weight.specs(),
            out_specs=[HELD] * 3,
            scratch_shapes=weight.scratch(),
        ),
        out_shape=[inside((rows, columns))] * 2 + [weight.out()],
        compiler_params=params(16),
        cost_estimate=cost(),
        name="expand_act",
    )(pos, in_vmem(normed_low), bias, *weight.arrays)


def second_kernel(pos, captions, active, bias, unit, gain, shift, gain2, shift2, cotangent, *rest, weight, seq):
    pieces, (out, low, grad, sums), full, sems = weight.split(rest)
    weight.arrive(pieces, full, pos, sems)
    tile = out.shape[0]
    at = step_of(tile)
    normed = unit[at, :] * gain[...] + shift[...]
    total = normed + (dot(active[at, :], full[...]) + bias[...])
    unit2, scale2 = norm_parts(total)
    out[...] = (unit2 * gain2[...] + shift2[...]).astype(BF16)
    row = lax.broadcasted_iota(jnp.int32, (tile, 1), 0)
    live = jnp.zeros((tile, 1), jnp.bool_)
    for pair in range(tile // seq):
        count = captions[pl.program_id(0) * (tile // seq) + pair] + 2 + REGIONS
        live = live | ((row >= pair * seq) & (row < pair * seq + count))
    upstream = jnp.where(live, cotangent[...].astype(F32), 0.0)
    second = norm_back(upstream, unit2, scale2, gain2[...])
    grad[at, :] = second
    low[at, :] = second.astype(BF16)
    add_sums(sums, (second, upstream * unit2, upstream))


def second_norm(pos, captions, active, weight, bias, unit, gain, shift, gain2, shift2, cotangent, seq):
    rows, width = unit.shape
    hidden = active.shape[1]
    tile = rows_of(rows, 416)
    block = pl.BlockSpec((tile, width), lambda i, p, c: (i, 0))
    row = whole((1, width))
    return pl.pallas_call(
        functools.partial(second_kernel, weight=weight, seq=seq),
        grid_spec=pltpu.PrefetchScalarGridSpec(
            num_scalar_prefetch=2,
            grid=(rows // tile,),
            in_specs=[HELD, row, HELD, row, row, row, row, block] + weight.specs(),
            out_specs=[block, HELD, HELD, whole((8, width)), HELD],
            scratch_shapes=weight.scratch(),
        ),
        out_shape=[
            outside((rows, width)),
            inside((rows, width)),
            inside((rows, width), F32),
            jax.ShapeDtypeStruct((8, width), F32),
            weight.out(),
        ],
        compiler_params=params(18),
        cost_estimate=cost(),
        name="second_norm",
    )(pos, captions, in_vmem(active), bias, in_vmem(unit), gain, shift, gain2, shift2, cotangent, *weight.arrays)


def hidden_back_kernel(low, weight, slope, out, sums):
    at = columns_of(sums.shape[1])
    grad = dot(low[...], weight[at, :], NT) * slope[:, at].astype(F32)
    out[:, at] = grad.astype(BF16)
    sums[...] = jnp.sum(grad, axis=0, keepdims=True)


def hidden_back(low, weight, slope):
    rows, width = low.shape
    hidden = weight.shape[0]
    tile = tile_of(hidden, 768)
    return pl.pallas_call(
        hidden_back_kernel,
        grid=(hidden // tile,),
        in_specs=[HELD] * 3,
        out_specs=[HELD, pl.BlockSpec((1, tile), lambda i: (0, i))],
        out_shape=[inside((rows, hidden)), jax.ShapeDtypeStruct((1, hidden), F32)],
        compiler_params=params(14),
        cost_estimate=cost(),
        name="hidden_back",
    )(in_vmem(low), in_vmem(weight), in_vmem(slope))


def first_back_kernel(hidden, weight, second, unit, scale, gain, out_weight, grad, low, context_grad, sums):
    at = step_of(grad.shape[0])
    unit_rows = unit[at, :]
    normed_grad = dot(hidden[at, :], weight[...], NT) + second[at, :]
    first = norm_back(normed_grad, unit_rows, scale[at, :], gain[...])
    grad[...] = first
    first_low = first.astype(BF16)
    low[at, :] = first_low
    context_grad[at, :] = dot(first_low, out_weight[...], NT).astype(BF16)
    add_sums(sums, (first, normed_grad * unit_rows, normed_grad))


def first_back(hidden, weight, second, unit, scale, gain, out_weight):
    rows, width = second.shape
    columns = hidden.shape[1]
    tile = rows_of(rows, 416)
    return pl.pallas_call(
        first_back_kernel,
        grid=(rows // tile,),
        in_specs=[HELD] * 5 + [whole((1, width)), HELD],
        out_specs=[pl.BlockSpec((tile, width), lambda i: (i, 0)), HELD, HELD, whole((8, width))],
        out_shape=[
            outside((rows, width), F32),
            inside((rows, width)),
            inside((rows, width)),
            jax.ShapeDtypeStruct((8, width), F32),
        ],
        compiler_params=params(18),
        cost_estimate=cost(),
        name="first_back",
    )(in_vmem(hidden), in_vmem(weight), in_vmem(second), in_vmem(unit), in_vmem(scale), gain, in_vmem(out_weight))


def token_back_kernel(grads, weight, first, out):
    out[...] = dot(grads[step_of(out.shape[0]), :], weight[...], NT) + first[...]


def token_back(grads, weight, first):
    rows, width = first.shape
    columns = grads.shape[1]
    tile = rows_of(rows, 416)
    block = pl.BlockSpec((tile, width), lambda i: (i, 0))
    return pl.pallas_call(
        token_back_kernel,
        grid=(rows // tile,),
        in_specs=[HELD, HELD, block],
        out_specs=block,
        out_shape=outside((rows, width), F32),
        compiler_params=params(14),
        cost_estimate=cost(COVER),
        name="token_back",
    )(in_vmem(grads), in_vmem(weight), in_hbm(first))


def weight_grad_kernel(left, right, out):
    out[...] = dot(left[...], right[...], TN).astype(BF16)


def weight_grad(left, right):
    rows, height = left.shape
    columns = right.shape[1]
    tile = tile_of(columns, 768)
    high = tile_of(height, 768)
    return pl.pallas_call(
        weight_grad_kernel,
        grid=(height // high, columns // tile),
        in_specs=[
            pl.BlockSpec((rows, high), lambda i, j: (0, i)),
            pl.BlockSpec((rows, tile), lambda i, j: (0, j)),
        ],
        out_specs=pl.BlockSpec((high, tile), lambda i, j: (i, j)),
        out_shape=outside((height, columns)),
        compiler_params=params(24),
        cost_estimate=cost(),
        name="weight_grad",
    )(left, right)


def store_halves(out, core, grads, pos, rows, extra):
    for chip in range(4):
        ahead = chip ^ pos[0]
        for up in range(2):
            at = ((chip * 2 + core) * 2 + up) * rows
            across = up ^ pos[2]
            block = grads[at : at + rows].astype(BF16)
            out[ahead, across, 0, :, : block.shape[1]] = block
            if extra is not None:
                out[ahead, across, 0, :, block.shape[1] :] = jnp.zeros((rows, 128), BF16)
                out[ahead, across, 0, 0:16, block.shape[1] :] = extra[chip * 2 + core].astype(BF16)


def halves_grad_kernel(pos, left, right, *rest, tile):
    extra, (mine, theirs) = (rest[0] if len(rest) == 3 else None), rest[-2:]
    step = pl.program_id(0) * pl.num_programs(1) + pl.program_id(1)
    grads = dot(left[...], right[:, pl.ds(pl.multiple_of(step * tile, 128), tile)], TN)
    rows = mine.shape[3]

    @pl.when(pos[1] == 0)
    def _():
        store_halves(mine, 0, grads, pos, rows, extra)
        store_halves(theirs, 1, grads, pos, rows, extra)

    @pl.when(pos[1] == 1)
    def _():
        store_halves(mine, 1, grads, pos, rows, extra)
        store_halves(theirs, 0, grads, pos, rows, extra)


def halves_grad(pos, left, right, extra=None, held=True, flops=0):
    rows, height = left.shape
    half = right.shape[1] // 2
    tile = half if extra is not None else tile_of(half, 768)
    steps = half // tile
    room = 0 if extra is None else 128
    out = outside((4, 2, 2, height // 16, half + room))
    block = pl.BlockSpec((4, 2, 1, height // 16, tile + room), lambda i, j, p: (0, 0, i ^ p[3], 0, j))
    return pl.pallas_call(
        functools.partial(halves_grad_kernel, tile=tile),
        grid_spec=pltpu.PrefetchScalarGridSpec(
            num_scalar_prefetch=1,
            grid=(2, steps),
            in_specs=[HELD if held else whole((rows, height), 1), HELD]
            + ([] if extra is None else [whole(extra.shape)]),
            out_specs=[block, block],
        ),
        out_shape=[out, out],
        compiler_params=params(14),
        cost_estimate=cost(flops),
        name="halves_grad",
    )(pos, in_vmem(left) if held else left, in_vmem(right), *(() if extra is None else (extra,)))


def store_stacked(out, core, grads, pos, rows):
    wide = grads.shape[1]
    for quarter in range(4):
        for part in range(2):
            at = ((core * 4 + quarter) * 2 + part) * rows
            block = grads[at : at + rows].astype(BF16)
            out[0, (quarter // 2) ^ pos[2], (quarter % 2) ^ pos[3], :, part * wide : (part + 1) * wide] = block


def stacked_grad_kernel(pos, left, right, mine, theirs):
    wide = left.shape[1] // 4
    grads = dot(left[:, columns_of(wide)], right[...], TN)
    rows = mine.shape[3]

    @pl.when(pos[1] == 0)
    def _():
        store_stacked(mine, 0, grads, pos, rows)
        store_stacked(theirs, 1, grads, pos, rows)

    @pl.when(pos[1] == 1)
    def _():
        store_stacked(mine, 1, grads, pos, rows)
        store_stacked(theirs, 0, grads, pos, rows)


def stacked_grad(pos, left, right):
    rows, height = left.shape
    wide = right.shape[1]
    out = outside((4, 2, 2, height // 64, 2 * wide))
    block = pl.BlockSpec((1, 2, 2, height // 64, 2 * wide), lambda i, p: (i ^ p[0], 0, 0, 0, 0))
    return pl.pallas_call(
        stacked_grad_kernel,
        grid_spec=pltpu.PrefetchScalarGridSpec(
            num_scalar_prefetch=1,
            grid=(4,),
            in_specs=[HELD, HELD],
            out_specs=[block, block],
        ),
        out_shape=[out, out],
        compiler_params=params(14),
        cost_estimate=cost(),
        name="stacked_grad",
    )(pos, in_vmem(left), in_vmem(right))


def core_sum_kernel(*refs, count):
    outs = refs[2 * count :]
    for flip in range(4):
        at = 0
        for mine, theirs in zip(refs[:count], refs[count : 2 * count]):
            wide = mine.shape[4]
            pick = (0, flip // 2, flip % 2)
            outs[flip][0, :, at : at + wide] = (mine[pick].astype(F32) + theirs[pick].astype(F32)).astype(BF16)
            at += wide


def core_sum(mine, theirs):
    rows = mine[0].shape[3]
    wide = sum(m.shape[4] for m in mine)
    return pl.pallas_call(
        functools.partial(core_sum_kernel, count=len(mine)),
        grid=(4,),
        in_specs=[pl.BlockSpec((1,) + m.shape[1:], lambda i: (i, 0, 0, 0, 0)) for m in (*mine, *theirs)],
        out_specs=[pl.BlockSpec((1, rows, wide), lambda i: (i, 0, 0))] * 4,
        out_shape=[inside((4, rows, wide))] * 4,
        compiler_params=params(10),
        cost_estimate=cost(),
        name="core_sum",
    )(*map(in_hbm, (*mine, *theirs)))


def plane_sum_kernel(own, one, two, three, *outs):
    for flip in range(4):
        total = own[flip].astype(F32) + one[flip].astype(F32)
        total += two[flip].astype(F32) + three[flip].astype(F32)
        if len(outs) == 4:
            outs[flip][...] = total.astype(BF16)
        else:
            outs[flip // 2][flip % 2] = total.astype(BF16)


def plane_sum(parts, apart):
    _, rows, wide = parts[0].shape
    outs = [inside((rows, wide))] * 4 if apart else [inside((2, rows, wide))] * 2
    return pl.pallas_call(
        plane_sum_kernel,
        in_specs=[HELD] * 4,
        out_specs=[HELD] * len(outs),
        out_shape=outs,
        compiler_params=params(4),
        cost_estimate=cost(),
        name="plane_sum",
    )(*map(in_vmem, parts))


def pair_sum_kernel(near, received, one, two):
    one[...] = (near[0].astype(F32) + received[0].astype(F32)).astype(BF16)
    two[...] = (near[1].astype(F32) + received[1].astype(F32)).astype(BF16)


def pair_sum(near, received):
    _, rows, wide = near.shape
    return pl.pallas_call(
        pair_sum_kernel,
        in_specs=[HELD] * 2,
        out_specs=[HELD] * 2,
        out_shape=[inside((rows, wide))] * 2,
        compiler_params=params(4),
        cost_estimate=cost(),
        name="pair_sum",
    )(in_vmem(near), in_vmem(received))


def chip_sum_kernel(*refs, count):
    out, at = refs[-1], 0
    for group in range(count):
        terms = refs[group:-1:count]
        wide = terms[0].shape[1]
        total = terms[0][...].astype(F32)
        for term in terms[1:]:
            total += term[...].astype(F32)
        out[:, at : at + wide] = total.astype(BF16)
        at += wide


def chip_sum(*lists, flops=0):
    parts = [part for parts in lists for part in parts]
    rows = parts[0].shape[0]
    wide = sum(part.shape[1] for part in lists[0])
    return pl.pallas_call(
        functools.partial(chip_sum_kernel, count=len(lists[0])),
        in_specs=[HELD] * len(parts),
        out_specs=HELD,
        out_shape=inside((rows, wide)),
        compiler_params=params(4),
        cost_estimate=cost(flops),
        name="chip_sum",
    )(*map(in_vmem, parts))


def place_kernel(pos, *refs, layout):
    parts, outs = refs[:4], refs[4:]
    rows = parts[0].shape[0]
    for flip, part in enumerate(parts):
        up, along = pos[2] ^ (flip // 2), pos[3] ^ (flip % 2)
        at = 0
        for (kind, wide), out in zip(layout, outs):
            if kind == "halves":
                to_row = pl.multiple_of(up * rows, 16)
                to_column = pl.multiple_of(along * wide, 128)
                out[pl.ds(to_row, rows), pl.ds(to_column, wide)] = part[:, at : at + wide].astype(F32)
            elif kind == "stacked":
                for side in range(2):
                    to_row = pl.multiple_of(((up * 2 + along) * 2 + side) * rows, 16)
                    from_column = at + side * (wide // 2)
                    out[pl.ds(to_row, rows), :] = part[:, from_column : from_column + wide // 2].astype(F32)
            else:

                @pl.when((up == 0) & (along == 0))
                def _(out=out, part=part, at=at, wide=wide):
                    out[...] = part[0:16, at : at + wide].astype(F32)

            at += wide


def place(pos, parts, layout):
    rows = parts[0].shape[0]
    shapes = {
        "halves": lambda wide: (2 * rows, 2 * wide),
        "stacked": lambda wide: (8 * rows, wide // 2),
        "small": lambda wide: (16, wide),
    }
    outs = [jax.ShapeDtypeStruct(shapes[kind](wide), F32) for kind, wide in layout]
    return pl.pallas_call(
        functools.partial(place_kernel, layout=layout),
        grid_spec=pltpu.PrefetchScalarGridSpec(
            num_scalar_prefetch=1,
            grid=(1,),
            in_specs=[HELD] * 4,
            out_specs=[whole(out.shape, 1) for out in outs],
        ),
        out_shape=outs,
        compiler_params=params(10),
        cost_estimate=cost(),
        name="place",
    )(pos, *map(in_vmem, parts))


def from_core(values):
    return lax.ppermute(values, "fsdp", [(i, i ^ 1) for i in range(8)])


def from_plane(values):
    parts = values if isinstance(values, (list, tuple)) else [values] * 3
    return [
        lax.ppermute(part, "dp", [(i, i ^ flip) for i in range(4)]) for flip, part in zip((1, 2, 3), parts)
    ]


def from_chips(values):
    parts = values if isinstance(values, (list, tuple)) else [values] * 3
    return [from_chip(part, flip) for flip, part in zip((1, 2, 3), parts)]


def from_chip(values, flip):
    return lax.ppermute(values, "fsdp", [(i, i ^ (2 * flip)) for i in range(8)])


def below_kernel(*refs):
    at = 0
    for ref in refs[:-1]:
        rows, wide = ref.shape[0], refs[-1].shape[1]
        refs[-1][at : at + rows] = ref[:, :wide]
        at += rows


def below(*parts, wide=None):
    rows = sum(part.shape[0] for part in parts)
    return pl.pallas_call(
        below_kernel,
        in_specs=[HELD] * len(parts),
        out_specs=HELD,
        out_shape=inside((rows, wide or parts[0].shape[1])),
        compiler_params=params(4),
        cost_estimate=cost(),
        name="below",
    )(*map(in_vmem, parts))


def after(values, *others):
    return lax.optimization_barrier((values, others))[0]


def half_of(pos, shard):
    rows, wide = shard.shape[0] // 2, shard.shape[1] // 2
    return lax.dynamic_slice(shard, (pos[2] * rows, pos[3] * wide), (rows, wide))


def both_cores(pieces):
    return [*pieces, *(from_core(piece) for piece in pieces)]


def gather(values):
    return lax.all_gather(values, "fsdp", axis=0, tiled=True)


def local(
    pieces,
    tokens,
    captions,
    cotangent,
    project_weight,
    project_bias,
    output_weight,
    output_bias,
    first_gain,
    first_shift,
    expand_weight,
    expand_bias,
    shrink_weight,
    shrink_bias,
    second_gain,
    second_shift,
):
    pairs, seq, width = tokens.shape
    rows = pairs * seq
    parts = lax.axis_size("fsdp")
    token_rows = tokens.reshape(rows, width)
    cot_rows = cotangent.reshape(rows, width)

    vectors = (project_bias, output_bias, first_gain, first_shift, expand_bias, shrink_bias, second_gain, second_shift)
    widths = [vector.shape[0] for vector in vectors]
    replica, part = lax.axis_index("dp"), lax.axis_index("fsdp")
    pos = jnp.stack([part // 2, part % 2, replica // 2, replica % 2]).astype(jnp.int32)
    shapes = [(parts * shard.shape[0], shard.shape[1]) for shard in (project_weight, output_weight, expand_weight, shrink_weight)]
    if pieces:
        held = jnp.concatenate([vector.reshape(-1, 96) for vector in vectors], axis=0)
        held = jnp.pad(held, ((0, 4), (0, 32)))
        quarter_p, wide_p = half_of(pos, project_weight), project_weight.shape[1] // 2
        chips_p = from_chips(jnp.concatenate([quarter_p, jnp.pad(held, ((0, 32), (0, 0)))], axis=1))
        sibling_p = from_core(project_weight)
        chips_p = after(chips_p, sibling_p)
        mine_p = below(*chips_p, wide=wide_p)
        held = jnp.concatenate([held, *(chip[:16, wide_p:] for chip in chips_p)], axis=0)
        quarter_e = after(half_of(pos, expand_weight), *chips_p)
        one_e = from_chip(quarter_e, 1)
        plane_p = from_plane(mine_p)
        far_e = from_chip(below(quarter_e, one_e), 2)
        plane_p = below(*after(plane_p, one_e))
        other_p = [from_core(mine_p), from_core(plane_p)]
        project = Weight(
            shapes[0],
            [project_weight, sibling_p, mine_p, plane_p, *other_p],
            functools.partial(halves_copies, high=project_weight.shape[0], wide=project_weight.shape[1]),
        )
        rows_s = shrink_weight.shape[0] // 8
        quarter_s = lax.dynamic_slice(
            shrink_weight, ((pos[2] * 2 + pos[3]) * 2 * rows_s, 0), (2 * rows_s, shrink_weight.shape[1])
        )
        quarter_s = jnp.concatenate([quarter_s[:rows_s], quarter_s[rows_s:]], axis=1)
        one_s = from_chip(after(quarter_s, plane_p), 1)
        mine_e = below(one_e, far_e)
        plane_e = from_plane(mine_e)
        held = after(held, mine_e)
        bias_full, hidden_bias, rows6 = spread(pos, [held, from_core(held)], width, expand_weight.shape[1])
        out_bias, gain1, shift1, down_bias, gain2, shift2 = (rows6[at : at + 1] for at in range(6))
    else:
        project, output, expand, shrink = (
            Weight(shape, [gather(shard)])
            for shape, shard in zip(shapes, (project_weight, output_weight, expand_weight, shrink_weight))
        )
        packed = gather(jnp.concatenate(vectors)[None, :])
        full, at = [], 0
        for size in widths:
            full.append(packed[:, at : at + size].reshape(1, parts * size).astype(F32))
            at += size
        bias_row, out_bias, gain1, shift1, hidden_bias, down_bias, gain2, shift2 = full
        bias_full = jnp.concatenate([bias_row[:, :width], jnp.zeros((1, width), F32), bias_row[:, width:]], axis=1)

    joined, project = join(pos, token_rows, project, bias_full)
    joined3 = joined.reshape(pairs, seq, 3 * width)
    if pieces:
        output = Weight(shapes[1], [gather(after(output_weight, far_e))])
        far_s = below(quarter_s, after(one_s, joined))
        joined3 = after(joined3, far_s)
        far_s = from_chip(far_s, 2)
    context, probs = attend(joined3, captions)
    context_rows = context.reshape(rows, width)
    if pieces:
        far_s = after(far_s, context)
        plane_e = below(*after(plane_e, far_s))
        other_e = [from_core(mine_e), from_core(plane_e)]
        sibling_e = from_core(after(expand_weight, context))
        expand = Weight(
            shapes[2],
            [expand_weight, sibling_e, mine_e, plane_e, *other_e],
            functools.partial(halves_copies, high=expand_weight.shape[0], wide=expand_weight.shape[1]),
        )
        mine_s = below(one_s, after(far_s, plane_e))
        plane_s = from_plane(mine_s)
        context_rows = after(context_rows, mine_s)
    unit1, scale1, normed_low, output = first_norm(pos, context_rows, output, out_bias, token_rows, gain1, shift1)
    active, slope, expand = expand_act(pos, normed_low, expand, hidden_bias)
    if pieces:
        plane_s = below(*after(plane_s, active))
        other_s = [from_core(mine_s), from_core(plane_s)]
        sibling_s = from_core(after(shrink_weight, active))
        shrink = Weight(
            shapes[3],
            [shrink_weight, sibling_s, mine_s, plane_s, *other_s],
            functools.partial(stacked_copies, high=shrink_weight.shape[0], wide=shrink_weight.shape[1]),
        )
    out_rows, shrink_low, second_grad, sums2, shrink = second_norm(
        pos, captions, active, shrink, down_bias, unit1, gain1, shift1, gain2, shift2, cot_rows, seq
    )
    if pieces:
        mine_s, theirs_s = stacked_grad(pos, active, shrink_low)
        theirs_s = from_core(theirs_s)
        shrink_low = after(shrink_low, mine_s)
    else:
        grad_shrink = weight_grad(active, shrink_low)
    expand_low, sums_hidden = hidden_back(shrink_low, shrink, slope)
    if pieces:
        own_s, *out_s = core_sum([mine_s], [after(theirs_s, expand_low)])
        plane_s = from_plane(out_s)
        expand_low = after(expand_low, own_s)
        mine_e, theirs_e = halves_grad(pos, normed_low, expand_low)
        theirs_e = from_core(theirs_e)
        expand_low = after(expand_low, mine_e)
    first_grad, branch_low, context_grad, sums1 = first_back(
        expand_low, expand, second_grad, unit1, scale1, gain1, output
    )
    if pieces:
        near_s, far_s = plane_sum([own_s, *after(plane_s, branch_low)], False)
        far_s = from_chip(far_s, 2)
        mine_o, theirs_o = halves_grad(pos, context_rows, after(branch_low, near_s), flops=COVER)
        theirs_o = from_core(theirs_o)
        own_eo, *out_eo = core_sum([mine_e, mine_o], after([theirs_e, theirs_o], mine_o))
        plane_eo = from_plane(out_eo)
        context_grad = after(context_grad, own_eo)
    else:
        grad_expand = weight_grad(normed_low, expand_low)
        grad_output = weight_grad(context_rows, branch_low)
    joined_grad, sums_joined = attend_back(joined3, probs, context_grad.reshape(pairs, seq, width))
    joined_grad_rows = joined_grad.reshape(rows, 3 * width)
    if pieces:
        near_s, last_s = pair_sum(near_s, after(far_s, joined_grad))
        last_s = from_chip(last_s, 1)
        extra = after(bundle(sums_joined, sums1, sums2, sums_hidden), near_s)
        mine_p, theirs_p = halves_grad(pos, token_rows, joined_grad_rows, extra, held=False)
        theirs_p = from_core(theirs_p)
        near_eo, far_eo = plane_sum([own_eo, *after(plane_eo, mine_p)], False)
        far_eo = from_chip(far_eo, 2)
        joined_grad_rows = after(joined_grad_rows, near_eo)
    else:
        grad_project = weight_grad(token_rows, joined_grad_rows)

        def owned(grad):
            part = lax.psum_scatter(grad, "fsdp", scatter_dimension=0, tiled=True)
            return lax.psum(part, "dp").astype(F32)

        own_project, own_output, own_expand, own_shrink = (
            owned(grad) for grad in (grad_project, grad_output, grad_expand, grad_shrink)
        )
        small = (sums_joined[0], sums1[0], sums1[1], sums1[2], sums_hidden[0], sums2[0], sums2[1], sums2[2])
        packed_grad = jnp.concatenate([v.reshape(parts, -1) for v in small], axis=1)
        shard = lax.psum(lax.psum_scatter(packed_grad.reshape(-1), "fsdp", scatter_dimension=0, tiled=True), "dp")
    token_grad = token_back(joined_grad_rows, project, first_grad)
    if pieces:
        half_p, half_e, half_o = project_weight.shape[1] // 2, expand_weight.shape[1] // 2, width // 2
        own_p, *out_p = core_sum([mine_p], [after(theirs_p, token_grad)])
        plane_p = from_plane(out_p)
        near_eo, last_eo = pair_sum(near_eo, after(far_eo, own_p))
        last_eo = from_chip(last_eo, 1)
        ahead_p = plane_sum([own_p, *after(plane_p, near_eo)], True)
        chips_p = from_chips(ahead_p[1:])
        total_seo = chip_sum([near_s, near_eo], after([last_s, last_eo], ahead_p[0]))
        quarters_seo = from_plane(total_seo)
        total_p = chip_sum([ahead_p[0]], *([chip] for chip in after(chips_p, total_seo)), flops=COVER)
        quarters_p = from_plane(after(total_p, *quarters_seo))
        own_shrink, own_expand, own_output = place(
            pos, [total_seo, *after(quarters_seo, total_p)], (("stacked", 2 * width), ("halves", half_e), ("halves", half_o))
        )
        own_project, shard = place(
            pos, [total_p, *after(quarters_p, own_expand)], (("halves", half_p), ("small", 128))
        )
        shard = shard[:12, :96].reshape(-1)

    smalls, at = [], 0
    for size in widths:
        smalls.append(shard[at : at + size])
        at += size
    return (
        out_rows.reshape(pairs, seq, width),
        token_grad.reshape(pairs, seq, width),
        own_project,
        smalls[0],
        own_output,
        smalls[1],
        smalls[2],
        smalls[3],
        own_expand,
        smalls[4],
        own_shrink,
        smalls[5],
        smalls[6],
        smalls[7],
    )


def solution(mesh):
    rows3 = P(("dp", "fsdp"), None, None)
    matrix, vector = P("fsdp", None), P("fsdp")
    pieces = mesh.shape["dp"] == 4 and mesh.shape["fsdp"] == 8
    return jax.shard_map(
        functools.partial(local, pieces),
        mesh=mesh,
        in_specs=(
            rows3, P(("dp", "fsdp")), rows3,
            matrix, vector, matrix, vector, vector, vector,
            matrix, vector, matrix, vector, vector, vector,
        ),
        out_specs=(
            rows3, rows3,
            matrix, vector, matrix, vector, vector, vector,
            matrix, vector, matrix, vector, vector, vector,
        ),
        check_vma=False,
    )
```

time: 492 us -> 303 us (0.62)
  waiting for transfers between devices: 271 us -> 90.2 us
  blocking collectives: 52.3 us -> 0 us
  starting transfers between devices: 0.36 us -> 48.5 us
  other arithmetic: 7.56 us -> 0.11 us
    reduce_scatter x4 -> x0, waiting for transfers between devices: 146 us -> none  [owned(): part = lax.psum_scatter(grad, 'fsdp', scatter_dimension=0, tiled=True)]
    all_gather x4 -> x1, waiting for transfers between devices: 105 us -> 0.02 us  [gather(): return lax.all_gather(values, 'fsdp', axis=0, tiled=True)]
    ppermute x0 -> x52, waiting for transfers between devices: none -> 90.2 us  [the longest x14 48.3 us: from_chip(): return lax.ppermute(values, 'fsdp', [(i, i ^ 2 * flip) for i in range(8)])]
    ppermute x0 -> x52, starting transfers between devices: none -> 48.5 us  [the longest x24 28.7 us: from_plane(): lax.ppermute(part, 'dp', [(i, i ^ flip) for i in range(4)])]
    unnamed x1 -> x0, blocking collectives: 26.4 us -> none
    psum x1 -> x0, waiting for transfers between devices: 16.8 us -> none  [owned(): return lax.psum(part, 'dp').astype(F32)]
    all_gather x1 -> x0, blocking collectives: 16 us -> none  [gather(): return lax.all_gather(values, 'fsdp', axis=0, tiled=True)]
    psum x1 -> x0, blocking collectives: 9.98 us -> none  [local(): lax.psum(lax.psum_scatter(packed_grad, 'fsdp', scatter_dimension=0, tiled...]
  transfers between devices with their start and end apart: 9 -> 53, of which waited for: 7 -> 19; matrix products, arithmetic and copies ran while one was open for 3% -> 2% of each run, Pallas kernels for 18% -> 33%
where the time goes in v2:
time: 303 us; the launch traced here: 302 us
  Pallas kernels  130 us (43%)
  waiting for transfers between devices  90.2 us (30%)
  starting transfers between devices  48.5 us (16%)
  local copies, waits for them, and re-layouts  18.6 us (6%)
  between operations  14.7 us (5%)
    ppermute x14, waiting for transfers between devices, from_chip(): return lax.ppermute(values, 'fsdp', [(i, i ^ 2 * flip) for i in range(8)])  48.3 us
    ppermute x24, waiting for transfers between devices, from_plane(): lax.ppermute(part, 'dp', [(i, i ^ flip) for i in range(4)])  35.7 us
    ppermute x24, starting transfers between devices, from_plane(): lax.ppermute(part, 'dp', [(i, i ^ flip) for i in range(4)])  28.7 us
    pallas_call x3, Pallas kernels, halves_grad(): pl.pallas_call(functools.partial(halves_grad_kernel, tile=tile), grid_spe...  18.4 us
    ppermute x14, starting transfers between devices, from_chip(): return lax.ppermute(values, 'fsdp', [(i, i ^ 2 * flip) for i in range(8)])  17.1 us
    pallas_call x1, Pallas kernels, attend(): pl.pallas_call(attend_kernel, grid_spec=pltpu.PrefetchScalarGridSpec(num_...  16.3 us
    pallas_call x1, Pallas kernels, attend_back(): pl.pallas_call(attend_back_kernel, grid=(pairs,), in_specs=[pl.BlockSpec(...  14.7 us
    pallas_call x1, Pallas kernels, expand_act(): pl.pallas_call(functools.partial(expand_kernel, weight=weight, tile=tile)...  11.1 us
  transfers between devices with their start and end apart: 53, of which 19 were waited for; matrix products, arithmetic and copies ran while one was open for 2% of the time, Pallas kernels for 33%

profile of v2, /device:TPU:0, one launch (start us, length us, event | category | flops | bytes accessed | tf_op | source)
XLA Modules:
  0.0 302.2 jit_solution(17950173310028120146)
XLA Ops:
  11.7 4.7 %collective-permute-start.2 = (bf16[48,1280]{1,0:T(8,128)(2,1)S(1)}, bf16[48,1280]{1,0:T(8,128)(2,1)S(1)}, u32[]{:S(2)}, u32[]{:S(2)}) collective-permute-start(bf16[48,1280]{1,0:T(8,128)(2,1)S(1)} %fusion.1), channel_id=1, source_target_pairs={{0,6},{1,7},{2,4},{3,5},{4,2},{5,3},{6,0},{7,1},{8,14},{9,15},{10,... | collective-permute-start | bytes 368648 | tf_op jit(solution)/shard_map/ppermute | solution.py:867
  18.0 2.7 collective-permute-done.2.refs_2_
  20.7 6.7 %collective-permute-done.1.refs_1_ = bf16[48,1280]{1,0:T(8,128)(2,1)S(1)} collective-permute-done((bf16[48,1280]{1,0:T(8,128)(2,1)S(1)}, bf16[48,1280]{1,0:T(8,128)(2,1)S(1)}, u32[]{:S(2)}, u32[]{:S(2)}) %collective-permute-start.1) | collective-permute-done | bytes 122912 | tf_op jit(solution)/shard_map/ppermute | solution.py:867
  28.6 2.5 collective-permute-start.9
  32.9 2.3 collective-permute-start.5
  35.3 13.0 %collective-permute-done.5.refs_1_ = bf16[96,1536]{1,0:T(8,128)(2,1)S(1)} collective-permute-done((bf16[96,1536]{1,0:T(8,128)(2,1)S(1)}, bf16[96,1536]{1,0:T(8,128)(2,1)S(1)}, u32[]{:S(2)}, u32[]{:S(2)}) %collective-permute-start.5) | collective-permute-done | bytes 294944 | tf_op jit(solution)/shard_map/ppermute | solution.py:867
  50.9 2.4 collective-permute-start.16
  55.2 7.9 %join.1 = (bf16[832,2304]{1,0:T(8,128)(2,1)}, bf16[768,2304]{1,0:T(8,128)(2,1)S(1)}) custom-call(s32[4]{0:T(128)S(1)} %pad_add_fusion.pos, bf16[832,768]{1,0:T(8,128)(2,1)S(1)} %bitcast.30, f32[1,2304]{1,0:T(1,128)S(1)} %get-tuple-element.140.bias, bf16[96,2304]{1,0:T(8,128)(2,1)} %rest_0_.3, bf16[96,2304]{1,0:T(8,128)(2,1)} %copy-done.25, ...), custom_call_target="tpu_custom_call" | custom-call | tf_op jit(solution)/shard_map/join/pallas_call | solution.py:237
  63.2 2.8 collective-permute-start.13
  66.0 16.3 %attend.1 = (bf16[8,104,768]{2,1,0:T(8,128)(2,1)S(1)}, bf16[8,6,104,256]{3,2,1,0:T(8,128)(2,1)}) custom-call(s32[8]{0:T(128)S(1)} %copy-done.15, bf16[8,104,2304]{2,1,0:T(8,128)(2,1)} %bitcast.39), custom_call_target="tpu_custom_call" | custom-call | tf_op jit(solution)/shard_map/attend/pallas_call | solution.py:291
  88.2 2.5 collective-permute-start.23
  93.5 4.5 %first_norm.1 = (f32[832,768]{1,0:T(8,128)S(1)}, f32[832,1]{1,0:T(8,128)S(1)}, bf16[832,768]{1,0:T(8,128)(2,1)S(1)}, bf16[768,768]{1,0:T(8,128)(2,1)S(1)}) custom-call(s32[4]{0:T(128)S(1)} %pad_add_fusion.pos, bf16[832,768]{1,0:T(8,128)(2,1)S(1)} %bitcast.35, f32[1,768]{1,0:T(1,128)S(1)} %get-tuple-element.263.bias, bf16[832,768]{1,0:T(8,128)(2,1)S(1)} %bitcast.31, ...), custom_call_target="tpu_custom_call" | custom-call | tf_op jit(solution)/shard_map/first_norm/pallas_call | solution.py:412
  98.0 11.1 %expand_act.1 = (bf16[832,3072]{1,0:T(8,128)(2,1)S(1)}, bf16[832,3072]{1,0:T(8,128)(2,1)S(1)}, bf16[768,3072]{1,0:T(8,128)(2,1)S(1)}) custom-call(s32[4]{0:T(128)S(1)} %pad_add_fusion.pos, bf16[832,768]{1,0:T(8,128)(2,1)S(1)} %get-tuple-element.157.normed_low.left, f32[1,3072]{1,0:T(1,128)S(1)} %get-tuple-element.158.bias, bf16[96,3072]{1,0:T(8,128)(2,1)} %rest_0_.4, ...), custom_call_target="tpu_custom_call" | custom-call | tf_op jit(solution)/shard_map/expand_act/pallas_call | solution.py:442
  113.2 3.9 %collective-permute-done.24.rest_4_ = bf16[144,1536]{1,0:T(8,128)(2,1)S(1)} collective-permute-done((bf16[144,1536]{1,0:T(8,128)(2,1)S(1)}, bf16[144,1536]{1,0:T(8,128)(2,1)S(1)}, u32[]{:S(2)}, u32[]{:S(2)}) %collective-permute-start.24) | collective-permute-done | bytes 442400 | tf_op jit(solution)/shard_map/ppermute | solution.py:851
  118.6 10.8 %second_norm.1 = (bf16[832,768]{1,0:T(8,128)(2,1)}, bf16[832,768]{1,0:T(8,128)(2,1)S(1)}, f32[832,768]{1,0:T(8,128)S(1)}, f32[8,768]{1,0:T(8,128)S(1)}, bf16[3072,768]{1,0:T(8,128)(2,1)S(1)}) custom-call(s32[4]{0:T(128)S(1)} %pad_add_fusion.pos, s32[8]{0:T(128)S(1)} %copy-done.15, bf16[832,3072]{1,0:T(8,128)(2,1)S(1)} %get-tuple-element.160.active.left, ...), custom_call_target="tpu_custom_call" | custom-call | tf_op jit(solution)/shard_map/second_norm/pallas_call | solution.py:485
  129.4 8.2 %stacked_grad.1 = (bf16[4,2,2,48,1536]{4,3,2,1,0:T(8,128)(2,1)}, bf16[4,2,2,48,1536]{4,3,2,1,0:T(8,128)(2,1)}) custom-call(s32[4]{0:T(128)S(1)} %pad_add_fusion.pos, bf16[832,3072]{1,0:T(8,128)(2,1)S(1)} %get-tuple-element.160.active.left, bf16[832,768]{1,0:T(8,128)(2,1)S(1)} %get-tuple-element.170.right.low), custom_call_target="tpu_custom_call" | custom-call | tf_op jit(solution)/shard_map/stacked_grad/pallas_call | solution.py:692
  137.7 4.9 %hidden_back.1 = (bf16[832,3072]{1,0:T(8,128)(2,1)S(1)}, f32[1,3072]{1,0:T(1,128)S(1)}) custom-call(bf16[832,768]{1,0:T(8,128)(2,1)S(1)} %get-tuple-element.170.right.low, bf16[3072,768]{1,0:T(8,128)(2,1)S(1)} %get-tuple-element.171.weight, bf16[832,3072]{1,0:T(8,128)(2,1)S(1)} %get-tuple-element.172.slope), custom_call_target="tpu_custom_call" | custom-call | tf_op jit(solution)/shard_map/hidden_back/pallas_call | solution.py:518
  144.2 3.2 %core_sum.3 = (bf16[4,48,1536]{2,1,0:T(8,128)(2,1)S(1)}, bf16[4,48,1536]{2,1,0:T(8,128)(2,1)S(1)}, bf16[4,48,1536]{2,1,0:T(8,128)(2,1)S(1)}, bf16[4,48,1536]{2,1,0:T(8,128)(2,1)S(1)}) custom-call(bf16[4,2,2,48,1536]{4,3,2,1,0:T(8,128)(2,1)} %get-tuple-element.169.refs_0_, bf16[4,2,2,48,1536]{4,3,2,1,0:T(8,128)(2,1)} %copy-done.18), custom_call_target="tpu_custom_call" | custom-call | tf_op jit(solution)/shard_map/core_sum/pallas_call | solution.py:721
  151.0 8.0 %halves_grad.3 = (bf16[4,2,2,48,1536]{4,3,2,1,0:T(8,128)(2,1)}, bf16[4,2,2,48,1536]{4,3,2,1,0:T(8,128)(2,1)}) custom-call(s32[4]{0:T(128)S(1)} %pad_add_fusion.pos, bf16[832,768]{1,0:T(8,128)(2,1)S(1)} %get-tuple-element.157.normed_low.left, bf16[832,3072]{1,0:T(8,128)(2,1)S(1)} %get-tuple-element.179.right.hidden), custom_call_target="tpu_custom_call" | custom-call | tf_op jit(solution)/shard_map/halves_grad/pallas_call | solution.py:646
  159.0 9.5 %first_back.1 = (f32[832,768]{1,0:T(8,128)}, bf16[832,768]{1,0:T(8,128)(2,1)S(1)}, bf16[832,768]{1,0:T(8,128)(2,1)S(1)}, f32[8,768]{1,0:T(8,128)S(1)}) custom-call(bf16[832,3072]{1,0:T(8,128)(2,1)S(1)} %get-tuple-element.179.right.hidden, bf16[768,3072]{1,0:T(8,128)(2,1)S(1)} %get-tuple-element.180.weight, f32[832,768]{1,0:T(8,128)S(1)} %get-tuple-element.181.second, ...), custom_call_target="tpu_custom_call" | custom-call | tf_op jit(solution)/shard_map/first_back/pallas_call | solution.py:546
  168.5 8.4 %collective-permute-done.28.two = bf16[4,48,1536]{2,1,0:T(8,128)(2,1)S(1)} collective-permute-done((bf16[4,48,1536]{2,1,0:T(8,128)(2,1)S(1)}, bf16[4,48,1536]{2,1,0:T(8,128)(2,1)S(1)}, u32[]{:S(2)}, u32[]{:S(2)}) %collective-permute-start.28) | collective-permute-done | bytes 589856 | tf_op jit(solution)/shard_map/ppermute | solution.py:857
  177.3 3.5 %halves_grad.4 = (bf16[4,2,2,48,384]{4,3,2,1,0:T(8,128)(2,1)}, bf16[4,2,2,48,384]{4,3,2,1,0:T(8,128)(2,1)}) custom-call(s32[4]{0:T(128)S(1)} %pad_add_fusion.pos, bf16[832,768]{1,0:T(8,128)(2,1)S(1)} %bitcast.36, bf16[832,768]{1,0:T(8,128)(2,1)S(1)} %get-tuple-element.193.right), custom_call_target="tpu_custom_call" | custom-call | flops 99999997952 | tf_op jit(solution)/shard_map/halves_grad/pallas_call | solution.py:646
  184.6 3.6 %core_sum.4 = (bf16[4,48,1920]{2,1,0:T(8,128)(2,1)S(1)}, bf16[4,48,1920]{2,1,0:T(8,128)(2,1)S(1)}, bf16[4,48,1920]{2,1,0:T(8,128)(2,1)S(1)}, bf16[4,48,1920]{2,1,0:T(8,128)(2,1)S(1)}) custom-call(bf16[4,2,2,48,1536]{4,3,2,1,0:T(8,128)(2,1)} %get-tuple-element.178.refs_0_, bf16[4,2,2,48,384]{4,3,2,1,0:T(8,128)(2,1)} %get-tuple-element.194.refs_1_, ...), custom_call_target="tpu_custom_call" | custom-call | tf_op jit(solution)/shard_map/core_sum/pallas_call | solution.py:721
  191.7 14.7 %attend_back.1 = (bf16[8,104,2304]{2,1,0:T(8,128)(2,1)S(1)}, f32[1,1536]{1,0:T(1,128)S(1)}) custom-call(bf16[8,104,2304]{2,1,0:T(8,128)(2,1)} %bitcast.40, bf16[8,6,104,256]{3,2,1,0:T(8,128)(2,1)} %get-tuple-element.167.probs, bf16[8,104,768]{2,1,0:T(8,128)(2,1)S(1)} %bitcast.38), custom_call_target="tpu_custom_call" | custom-call | tf_op jit(solution)/shard_map/attend_back/pallas_call | solution.py:350
  206.6 7.0 %halves_grad.5 = (bf16[4,2,2,48,1280]{4,3,2,1,0:T(8,128)(2,1)}, bf16[4,2,2,48,1280]{4,3,2,1,0:T(8,128)(2,1)}) custom-call(s32[4]{0:T(128)S(1)} %pad_add_fusion.pos, bf16[832,768]{1,0:T(8,128)(2,1)S(1)} %bitcast.32, bf16[832,2304]{1,0:T(8,128)(2,1)S(1)} %bitcast.33, f32[8,16,128]{2,1,0:T(8,128)S(1)} %bundle.1.rest_0_), custom_call_target="tpu_custom_call" | custom-call | tf_op jit(solution)/shard_map/halves_grad/pallas_call | solution.py:646
  213.6 8.2 %collective-permute-done.33.two = bf16[4,48,1920]{2,1,0:T(8,128)(2,1)S(1)} collective-permute-done((bf16[4,48,1920]{2,1,0:T(8,128)(2,1)S(1)}, bf16[4,48,1920]{2,1,0:T(8,128)(2,1)S(1)}, u32[]{:S(2)}, u32[]{:S(2)}) %collective-permute-start.33) | collective-permute-done | bytes 737312 | tf_op jit(solution)/shard_map/ppermute | solution.py:857
  223.2 5.7 %token_back.1 = f32[832,768]{1,0:T(8,128)} custom-call(bf16[832,2304]{1,0:T(8,128)(2,1)S(1)} %bitcast.34, bf16[768,2304]{1,0:T(8,128)(2,1)S(1)} %copy-done.17, f32[832,768]{1,0:T(8,128)} %get-tuple-element.220.first), custom_call_target="tpu_custom_call" | custom-call | flops 99999997952 | tf_op jit(solution)/shard_map/token_back/pallas_call | solution.py:572
  230.3 3.0 core_sum.5
  236.8 16.8 %collective-permute-done.40.received = bf16[2,48,1920]{2,1,0:T(8,128)(2,1)S(1)} collective-permute-done((bf16[2,48,1920]{2,1,0:T(8,128)(2,1)S(1)}, bf16[2,48,1920]{2,1,0:T(8,128)(2,1)S(1)}, u32[]{:S(2)}, u32[]{:S(2)}) %collective-permute-start.40) | collective-permute-done | bytes 368672 | tf_op jit(solution)/shard_map/ppermute | solution.py:867
  262.0 5.1 %collective-permute-done.44.refs_2_ = bf16[48,1536]{1,0:T(8,128)(2,1)S(1)} collective-permute-done((bf16[48,1536]{1,0:T(8,128)(2,1)S(1)}, bf16[48,1536]{1,0:T(8,128)(2,1)S(1)}, u32[]{:S(2)}, u32[]{:S(2)}) %collective-permute-start.44) | collective-permute-done | bytes 147488 | tf_op jit(solution)/shard_map/ppermute | solution.py:867
  271.8 7.0 %collective-permute-done.48.refs_3_ = bf16[48,3456]{1,0:T(8,128)(2,1)S(1)} collective-permute-done((bf16[48,3456]{1,0:T(8,128)(2,1)S(1)}, bf16[48,3456]{1,0:T(8,128)(2,1)S(1)}, u32[]{:S(2)}, u32[]{:S(2)}) %collective-permute-start.48) | collective-permute-done | bytes 331808 | tf_op jit(solution)/shard_map/ppermute | solution.py:857
  278.8 4.3 %collective-permute-done.47.refs_2_ = bf16[48,3456]{1,0:T(8,128)(2,1)S(1)} collective-permute-done((bf16[48,3456]{1,0:T(8,128)(2,1)S(1)}, bf16[48,3456]{1,0:T(8,128)(2,1)S(1)}, u32[]{:S(2)}, u32[]{:S(2)}) %collective-permute-start.47) | collective-permute-done | bytes 331808 | tf_op jit(solution)/shard_map/ppermute | solution.py:857
  (186 shorter events, 72.1 us)
Async XLA Ops:
  7.2 85.0 %all-gather.2.cloned.1.call-start = ((), (), s32[]{:S(2)}) async-start(), calls=%async_computation | async-start | bytes 1327104 | tf_op jit(solution)/shard_map/all_gather | solution.py:905
  7.2 20.2 %collective-permute-start.3 = (bf16[96,2304]{1,0:T(8,128)(2,1)}, bf16[96,2304]{1,0:T(8,128)(2,1)S(1)}, u32[]{:S(2)}, u32[]{:S(2)}) collective-permute-start(bf16[96,2304]{1,0:T(8,128)(2,1)} %rest_0_.3), channel_id=1, source_target_pairs={{0,1},{1,0},{2,3},{3,2},{4,5},{5,4},{6,7},{7,6},{8,9},{9,8},{10,11... | collective-permute-start | bytes 1327112 | tf_op jit(solution)/shard_map/ppermute | solution.py:851
  28.6 24.8 %collective-permute-start.10 = (bf16[144,1152]{1,0:T(8,128)(2,1)S(1)}, bf16[144,1152]{1,0:T(8,128)(2,1)}, u32[]{:S(2)}, u32[]{:S(2)}) collective-permute-start(bf16[144,1152]{1,0:T(8,128)(2,1)S(1)} %below.10.rest_2_), channel_id=1, source_target_pairs={{0,1},{1,0},{2,3},{3,2},{4,5},{5,4},{6,7},{7,6},{8,9},{9,8},{10,11... | collective-permute-start | bytes 995336 | tf_op jit(solution)/shard_map/ppermute | solution.py:851
  28.6 19.9 %collective-permute-start.9 = (bf16[144,1152]{1,0:T(8,128)(2,1)S(1)}, bf16[144,1152]{1,0:T(8,128)(2,1)S(1)}, u32[]{:S(2)}, u32[]{:S(2)}) collective-permute-start(bf16[144,1152]{1,0:T(8,128)(2,1)S(1)} %below.10.rest_2_), channel_id=1, source_target_pairs={{0,24},{8,16},{16,8},{24,0},{1,25},{9,17},{17,9},{25,1},{2,26},{10... | collective-permute-start | bytes 995336 | tf_op jit(solution)/shard_map/ppermute | solution.py:857
  31.1 17.4 %collective-permute-start.8 = (bf16[144,1152]{1,0:T(8,128)(2,1)S(1)}, bf16[144,1152]{1,0:T(8,128)(2,1)S(1)}, u32[]{:S(2)}, u32[]{:S(2)}) collective-permute-start(bf16[144,1152]{1,0:T(8,128)(2,1)S(1)} %below.10.rest_2_), channel_id=1, source_target_pairs={{0,16},{8,24},{16,0},{24,8},{1,17},{9,25},{17,1},{25,9},{2,18},{10... | collective-permute-start | bytes 995336 | tf_op jit(solution)/shard_map/ppermute | solution.py:857
  31.7 16.9 %collective-permute-start.7 = (bf16[144,1152]{1,0:T(8,128)(2,1)S(1)}, bf16[144,1152]{1,0:T(8,128)(2,1)S(1)}, u32[]{:S(2)}, u32[]{:S(2)}) collective-permute-start(bf16[144,1152]{1,0:T(8,128)(2,1)S(1)} %below.10.rest_2_), channel_id=1, source_target_pairs={{0,8},{8,0},{16,24},{24,16},{1,9},{9,1},{17,25},{25,17},{2,10},{10... | collective-permute-start | bytes 995336 | tf_op jit(solution)/shard_map/ppermute | solution.py:857
  32.9 15.4 %collective-permute-start.5 = (bf16[96,1536]{1,0:T(8,128)(2,1)S(1)}, bf16[96,1536]{1,0:T(8,128)(2,1)S(1)}, u32[]{:S(2)}, u32[]{:S(2)}) collective-permute-start(bf16[96,1536]{1,0:T(8,128)(2,1)S(1)} %below.8), channel_id=1, source_target_pairs={{0,4},{1,5},{2,6},{3,7},{4,0},{5,1},{6,2},{7,3},{8,12},{9,13},{10,... | collective-permute-start | bytes 884744 | tf_op jit(solution)/shard_map/ppermute | solution.py:867
  50.9 34.6 %collective-permute-start.16 = (bf16[144,1536]{1,0:T(8,128)(2,1)S(1)}, bf16[144,1536]{1,0:T(8,128)(2,1)}, u32[]{:S(2)}, u32[]{:S(2)}) collective-permute-start(bf16[144,1536]{1,0:T(8,128)(2,1)S(1)} %below.9.rest_2_), channel_id=1, source_target_pairs={{0,24},{8,16},{16,8},{24,0},{1,25},{9,17},{17,9},{25,1},{2,26},{10... | collective-permute-start | bytes 1327112 | tf_op jit(solution)/shard_map/ppermute | solution.py:857
  53.4 32.1 %collective-permute-start.15 = (bf16[144,1536]{1,0:T(8,128)(2,1)S(1)}, bf16[144,1536]{1,0:T(8,128)(2,1)S(1)}, u32[]{:S(2)}, u32[]{:S(2)}) collective-permute-start(bf16[144,1536]{1,0:T(8,128)(2,1)S(1)} %below.9.rest_2_), channel_id=1, source_target_pairs={{0,16},{8,24},{16,0},{24,8},{1,17},{9,25},{17,1},{25,9},{2,18},{10... | collective-permute-start | bytes 1327112 | tf_op jit(solution)/shard_map/ppermute | solution.py:857
  54.0 31.5 %collective-permute-start.14 = (bf16[144,1536]{1,0:T(8,128)(2,1)S(1)}, bf16[144,1536]{1,0:T(8,128)(2,1)S(1)}, u32[]{:S(2)}, u32[]{:S(2)}) collective-permute-start(bf16[144,1536]{1,0:T(8,128)(2,1)S(1)} %below.9.rest_2_), channel_id=1, source_target_pairs={{0,8},{8,0},{16,24},{24,16},{1,9},{9,1},{17,25},{25,17},{2,10},{10... | collective-permute-start | bytes 1327112 | tf_op jit(solution)/shard_map/ppermute | solution.py:857
  63.2 22.3 %collective-permute-start.13 = (bf16[96,1536]{1,0:T(8,128)(2,1)S(1)}, bf16[96,1536]{1,0:T(8,128)(2,1)S(1)}, u32[]{:S(2)}, u32[]{:S(2)}) collective-permute-start(bf16[96,1536]{1,0:T(8,128)(2,1)S(1)} %below.12), channel_id=1, source_target_pairs={{0,4},{1,5},{2,6},{3,7},{4,0},{5,1},{6,2},{7,3},{8,12},{9,13},{10,... | collective-permute-start | bytes 884744 | tf_op jit(solution)/shard_map/ppermute | solution.py:867
  88.2 20.9 %collective-permute-start.23 = (bf16[144,1536]{1,0:T(8,128)(2,1)S(1)}, bf16[144,1536]{1,0:T(8,128)(2,1)}, u32[]{:S(2)}, u32[]{:S(2)}) collective-permute-start(bf16[144,1536]{1,0:T(8,128)(2,1)S(1)} %below.14.rest_2_), channel_id=1, source_target_pairs={{0,24},{8,16},{16,8},{24,0},{1,25},{9,17},{17,9},{25,1},{2,26},{10... | collective-permute-start | bytes 1327112 | tf_op jit(solution)/shard_map/ppermute | solution.py:857
  90.7 20.6 %collective-permute-start.22 = (bf16[144,1536]{1,0:T(8,128)(2,1)S(1)}, bf16[144,1536]{1,0:T(8,128)(2,1)}, u32[]{:S(2)}, u32[]{:S(2)}) collective-permute-start(bf16[144,1536]{1,0:T(8,128)(2,1)S(1)} %below.14.rest_2_), channel_id=1, source_target_pairs={{0,16},{8,24},{16,0},{24,8},{1,17},{9,25},{17,1},{25,9},{2,18},{10... | collective-permute-start | bytes 1327112 | tf_op jit(solution)/shard_map/ppermute | solution.py:857
  91.2 20.1 %collective-permute-start.21 = (bf16[144,1536]{1,0:T(8,128)(2,1)S(1)}, bf16[144,1536]{1,0:T(8,128)(2,1)S(1)}, u32[]{:S(2)}, u32[]{:S(2)}) collective-permute-start(bf16[144,1536]{1,0:T(8,128)(2,1)S(1)} %below.14.rest_2_), channel_id=1, source_target_pairs={{0,8},{8,0},{16,24},{24,16},{1,9},{9,1},{17,25},{25,17},{2,10},{10... | collective-permute-start | bytes 1327112 | tf_op jit(solution)/shard_map/ppermute | solution.py:857
  147.5 21.1 %collective-permute-start.27 = (bf16[4,48,1536]{2,1,0:T(8,128)(2,1)S(1)}, bf16[4,48,1536]{2,1,0:T(8,128)(2,1)S(1)}, u32[]{:S(2)}, u32[]{:S(2)}) collective-permute-start(bf16[4,48,1536]{2,1,0:T(8,128)(2,1)S(1)} %get-tuple-element.186), channel_id=1, source_target_pairs={{0,8},{8,0},{16,24},{24,16},{1,9},{9,1},{17,25},{25,17},{2,10},{10... | collective-permute-start | bytes 1769480 | tf_op jit(solution)/shard_map/ppermute | solution.py:857
  149.0 27.9 %collective-permute-start.28 = (bf16[4,48,1536]{2,1,0:T(8,128)(2,1)S(1)}, bf16[4,48,1536]{2,1,0:T(8,128)(2,1)S(1)}, u32[]{:S(2)}, u32[]{:S(2)}) collective-permute-start(bf16[4,48,1536]{2,1,0:T(8,128)(2,1)S(1)} %get-tuple-element.187), channel_id=1, source_target_pairs={{0,16},{8,24},{16,0},{24,8},{1,17},{9,25},{17,1},{25,9},{2,18},{10... | collective-permute-start | bytes 1769480 | tf_op jit(solution)/shard_map/ppermute | solution.py:857
  149.8 27.1 %collective-permute-start.29 = (bf16[4,48,1536]{2,1,0:T(8,128)(2,1)S(1)}, bf16[4,48,1536]{2,1,0:T(8,128)(2,1)S(1)}, u32[]{:S(2)}, u32[]{:S(2)}) collective-permute-start(bf16[4,48,1536]{2,1,0:T(8,128)(2,1)S(1)} %get-tuple-element.188), channel_id=1, source_target_pairs={{0,24},{8,16},{16,8},{24,0},{1,25},{9,17},{17,9},{25,1},{2,26},{10... | collective-permute-start | bytes 1769480 | tf_op jit(solution)/shard_map/ppermute | solution.py:857
  159.0 24.0 %collective-permute-start.30 = (bf16[4,2,2,48,1536]{4,3,2,1,0:T(8,128)(2,1)}, bf16[4,2,2,48,1536]{4,3,2,1,0:T(8,128)(2,1)S(1)}, u32[]{:S(2)}, u32[]{:S(2)}) collective-permute-start(bf16[4,2,2,48,1536]{4,3,2,1,0:T(8,128)(2,1)} %get-tuple-element.195), channel_id=1, source_target_pairs={{0,1},{1,0},{2,3},{3,2},{4,5},{5,4},{6,7},{7,6},{8,9},{9,8},{10,11... | collective-permute-start | bytes 7077896 | tf_op jit(solution)/shard_map/ppermute | solution.py:851
  188.1 25.5 %collective-permute-start.32 = (bf16[4,48,1920]{2,1,0:T(8,128)(2,1)S(1)}, bf16[4,48,1920]{2,1,0:T(8,128)(2,1)S(1)}, u32[]{:S(2)}, u32[]{:S(2)}) collective-permute-start(bf16[4,48,1920]{2,1,0:T(8,128)(2,1)S(1)} %get-tuple-element.202), channel_id=1, source_target_pairs={{0,8},{8,0},{16,24},{24,16},{1,9},{9,1},{17,25},{25,17},{2,10},{10... | collective-permute-start | bytes 2211848 | tf_op jit(solution)/shard_map/ppermute | solution.py:857
  188.7 33.1 %collective-permute-start.33 = (bf16[4,48,1920]{2,1,0:T(8,128)(2,1)S(1)}, bf16[4,48,1920]{2,1,0:T(8,128)(2,1)S(1)}, u32[]{:S(2)}, u32[]{:S(2)}) collective-permute-start(bf16[4,48,1920]{2,1,0:T(8,128)(2,1)S(1)} %get-tuple-element.203), channel_id=1, source_target_pairs={{0,16},{8,24},{16,0},{24,8},{1,17},{9,25},{17,1},{25,9},{2,18},{10... | collective-permute-start | bytes 2211848 | tf_op jit(solution)/shard_map/ppermute | solution.py:857
  190.2 32.5 %collective-permute-start.34 = (bf16[4,48,1920]{2,1,0:T(8,128)(2,1)S(1)}, bf16[4,48,1920]{2,1,0:T(8,128)(2,1)S(1)}, u32[]{:S(2)}, u32[]{:S(2)}) collective-permute-start(bf16[4,48,1920]{2,1,0:T(8,128)(2,1)S(1)} %get-tuple-element.204), channel_id=1, source_target_pairs={{0,24},{8,16},{16,8},{24,0},{1,25},{9,17},{17,9},{25,1},{2,26},{10... | collective-permute-start | bytes 2211848 | tf_op jit(solution)/shard_map/ppermute | solution.py:857
  191.7 14.7 %collective-permute-start.35 = (bf16[2,48,1536]{2,1,0:T(8,128)(2,1)S(1)}, bf16[2,48,1536]{2,1,0:T(8,128)(2,1)S(1)}, u32[]{:S(2)}, u32[]{:S(2)}) collective-permute-start(bf16[2,48,1536]{2,1,0:T(8,128)(2,1)S(1)} %get-tuple-element.209), channel_id=1, source_target_pairs={{0,4},{1,5},{2,6},{3,7},{4,0},{5,1},{6,2},{7,3},{8,12},{9,13},{10,... | collective-permute-start | bytes 884744 | tf_op jit(solution)/shard_map/ppermute | solution.py:867
  213.6 15.3 %collective-permute-start.36 = (bf16[4,2,2,48,1280]{4,3,2,1,0:T(8,128)(2,1)}, bf16[4,2,2,48,1280]{4,3,2,1,0:T(8,128)(2,1)S(1)}, u32[]{:S(2)}, u32[]{:S(2)}) collective-permute-start(bf16[4,2,2,48,1280]{4,3,2,1,0:T(8,128)(2,1)} %get-tuple-element.221), channel_id=1, source_target_pairs={{0,1},{1,0},{2,3},{3,2},{4,5},{5,4},{6,7},{7,6},{8,9},{9,8},{10,11... | collective-permute-start | bytes 5898248 | tf_op jit(solution)/shard_map/ppermute | solution.py:851
  233.2 22.6 %collective-permute-start.37 = (bf16[4,48,1280]{2,1,0:T(8,128)(2,1)S(1)}, bf16[4,48,1280]{2,1,0:T(8,128)(2,1)S(1)}, u32[]{:S(2)}, u32[]{:S(2)}) collective-permute-start(bf16[4,48,1280]{2,1,0:T(8,128)(2,1)S(1)} %get-tuple-element.224), channel_id=1, source_target_pairs={{0,8},{8,0},{16,24},{24,16},{1,9},{9,1},{17,25},{25,17},{2,10},{10... | collective-permute-start | bytes 1474568 | tf_op jit(solution)/shard_map/ppermute | solution.py:857
  234.8 22.5 %collective-permute-start.38 = (bf16[4,48,1280]{2,1,0:T(8,128)(2,1)S(1)}, bf16[4,48,1280]{2,1,0:T(8,128)(2,1)S(1)}, u32[]{:S(2)}, u32[]{:S(2)}) collective-permute-start(bf16[4,48,1280]{2,1,0:T(8,128)(2,1)S(1)} %get-tuple-element.225), channel_id=1, source_target_pairs={{0,16},{8,24},{16,0},{24,8},{1,17},{9,25},{17,1},{25,9},{2,18},{10... | collective-permute-start | bytes 1474568 | tf_op jit(solution)/shard_map/ppermute | solution.py:857
  235.6 21.6 %collective-permute-start.39 = (bf16[4,48,1280]{2,1,0:T(8,128)(2,1)S(1)}, bf16[4,48,1280]{2,1,0:T(8,128)(2,1)S(1)}, u32[]{:S(2)}, u32[]{:S(2)}) collective-permute-start(bf16[4,48,1280]{2,1,0:T(8,128)(2,1)S(1)} %get-tuple-element.226), channel_id=1, source_target_pairs={{0,24},{8,16},{16,8},{24,0},{1,25},{9,17},{17,9},{25,1},{2,26},{10... | collective-permute-start | bytes 1474568 | tf_op jit(solution)/shard_map/ppermute | solution.py:857
  236.8 16.8 %collective-permute-start.40 = (bf16[2,48,1920]{2,1,0:T(8,128)(2,1)S(1)}, bf16[2,48,1920]{2,1,0:T(8,128)(2,1)S(1)}, u32[]{:S(2)}, u32[]{:S(2)}) collective-permute-start(bf16[2,48,1920]{2,1,0:T(8,128)(2,1)S(1)} %get-tuple-element.227), channel_id=1, source_target_pairs={{0,4},{1,5},{2,6},{3,7},{4,0},{5,1},{6,2},{7,3},{8,12},{9,13},{10,... | collective-permute-start | bytes 1105928 | tf_op jit(solution)/shard_map/ppermute | solution.py:867
  253.7 13.4 %collective-permute-start.45 = (bf16[48,1920]{1,0:T(8,128)(2,1)S(1)}, bf16[48,1920]{1,0:T(8,128)(2,1)S(1)}, u32[]{:S(2)}, u32[]{:S(2)}) collective-permute-start(bf16[48,1920]{1,0:T(8,128)(2,1)S(1)} %get-tuple-element.238), channel_id=1, source_target_pairs={{0,2},{1,3},{2,0},{3,1},{4,6},{5,7},{6,4},{7,5},{8,10},{9,11},{10,... | collective-permute-start | bytes 552968 | tf_op jit(solution)/shard_map/ppermute | solution.py:867
  253.8 13.3 %collective-permute-start.44 = (bf16[48,1536]{1,0:T(8,128)(2,1)S(1)}, bf16[48,1536]{1,0:T(8,128)(2,1)S(1)}, u32[]{:S(2)}, u32[]{:S(2)}) collective-permute-start(bf16[48,1536]{1,0:T(8,128)(2,1)S(1)} %get-tuple-element.237), channel_id=1, source_target_pairs={{0,2},{1,3},{2,0},{3,1},{4,6},{5,7},{6,4},{7,5},{8,10},{9,11},{10,... | collective-permute-start | bytes 442376 | tf_op jit(solution)/shard_map/ppermute | solution.py:867
  257.6 13.1 %collective-permute-start.42 = (bf16[48,1280]{1,0:T(8,128)(2,1)S(1)}, bf16[48,1280]{1,0:T(8,128)(2,1)S(1)}, u32[]{:S(2)}, u32[]{:S(2)}) collective-permute-start(bf16[48,1280]{1,0:T(8,128)(2,1)S(1)} %get-tuple-element.235), channel_id=1, source_target_pairs={{0,4},{1,5},{2,6},{3,7},{4,0},{5,1},{6,2},{7,3},{8,12},{9,13},{10,... | collective-permute-start | bytes 368648 | tf_op jit(solution)/shard_map/ppermute | solution.py:867
  268.4 14.7 %collective-permute-start.47 = (bf16[48,3456]{1,0:T(8,128)(2,1)S(1)}, bf16[48,3456]{1,0:T(8,128)(2,1)S(1)}, u32[]{:S(2)}, u32[]{:S(2)}) collective-permute-start(bf16[48,3456]{1,0:T(8,128)(2,1)S(1)} %chip_sum.2.refs_0_), channel_id=1, source_target_pairs={{0,16},{8,24},{16,0},{24,8},{1,17},{9,25},{17,1},{25,9},{2,18},{10... | collective-permute-start | bytes 995336 | tf_op jit(solution)/shard_map/ppermute | solution.py:857
  269.9 13.3 %collective-permute-start.46 = (bf16[48,3456]{1,0:T(8,128)(2,1)S(1)}, bf16[48,3456]{1,0:T(8,128)(2,1)S(1)}, u32[]{:S(2)}, u32[]{:S(2)}) collective-permute-start(bf16[48,3456]{1,0:T(8,128)(2,1)S(1)} %chip_sum.2.refs_0_), channel_id=1, source_target_pairs={{0,8},{8,0},{16,24},{24,16},{1,9},{9,1},{17,25},{25,17},{2,10},{10... | collective-permute-start | bytes 995336 | tf_op jit(solution)/shard_map/ppermute | solution.py:857
  (49 other events, 407.1 us)
Sparse Core Ops, SparseCore 0:
  53.5 30.6 all-gather.1

commit v3 on v2

--- a/solution.py
+++ b/solution.py
@@ -65,11 +65,10 @@
     return max(fits) if fits else count
 
 
-def chip_of(pos, flip):
-    return pos[0] ^ flip
-
-
-def halves_copies(refs, into, pos, high, wide):
+CHIPS = (1, 3, 2)
+
+
+def halves_copies(refs, into, pos, at, high, wide):
     half = wide // 2
     rows = high // 2
     for side in range(2):
@@ -77,15 +76,15 @@
         shard = pos[0] * 2 + core
         yield refs[side], into.at[pl.ds(pl.multiple_of(shard * high, 16), high), :]
         for flip in range(4):
-            buffer, at = refs[2 + side * 2 + (flip > 0)], max(flip - 1, 0) * 3 * rows
+            buffer, first = refs[2 + side * 2 + (flip > 0)], max(flip - 1, 0) * 3 * rows
             up = pos[2] ^ (flip // 2)
             along = pos[3] ^ (flip % 2)
-            for back in range(1, 4):
-                shard = chip_of(pos, back) * 2 + core
+            for place, chip in enumerate(CHIPS):
+                shard = (pos[0] ^ chip) * 2 + core
                 to_row = pl.multiple_of(shard * high + up * rows, 16)
                 to_column = pl.multiple_of(along * half, 128)
                 yield (
-                    buffer.at[pl.ds(at + (back - 1) * rows, rows), :],
+                    buffer.at[pl.ds(first + place * rows, rows), pl.ds(at, half)],
                     into.at[pl.ds(to_row, rows), pl.ds(to_column, half)],
                 )
 
@@ -97,14 +96,14 @@
         shard = pos[0] * 2 + core
         yield refs[side], into.at[pl.ds(pl.multiple_of(shard * high, 16), high), :]
         for flip in range(4):
-            buffer, at = refs[2 + side * 2 + (flip > 0)], max(flip - 1, 0) * 3 * rows
+            buffer, first = refs[2 + side * 2 + (flip > 0)], max(flip - 1, 0) * 3 * rows
             quarter = (pos[2] * 2 + pos[3]) ^ flip
-            for back in range(1, 4):
-                shard = chip_of(pos, back) * 2 + core
+            for place, chip in enumerate(CHIPS):
+                shard = (pos[0] ^ chip) * 2 + core
                 for part in range(2):
                     to_row = pl.multiple_of(shard * high + (quarter * 2 + part) * rows, 16)
                     yield (
-                        buffer.at[pl.ds(at + (back - 1) * rows, rows), pl.ds(part * wide, wide)],
+                        buffer.at[pl.ds(first + place * rows, rows), pl.ds(part * wide, wide)],
                         into.at[pl.ds(to_row, rows), :],
                     )
 
@@ -155,9 +154,9 @@
 
 def spread_kernel(pos, own, other, bias, hidden, rows, held):
     part = held.shape[2] * 3 // 4
-    for back in range(4):
-        held[chip_of(pos, back) * 2 + pos[1]] = own[back * 16 : back * 16 + 16].astype(F32)
-        held[chip_of(pos, back) * 2 + 1 - pos[1]] = other[back * 16 : back * 16 + 16].astype(F32)
+    for at, chip in enumerate((0, *CHIPS)):
+        held[(pos[0] ^ chip) * 2 + pos[1]] = own[at * 16 : at * 16 + 16].astype(F32)
+        held[(pos[0] ^ chip) * 2 + 1 - pos[1]] = other[at * 16 : at * 16 + 16].astype(F32)
     bias[...] = jnp.zeros_like(bias)
     width = rows.shape[1]
     for shard in range(8):
@@ -555,7 +554,7 @@
             jax.ShapeDtypeStruct((8, width), F32),
         ],
         compiler_params=params(18),
-        cost_estimate=cost(),
+        cost_estimate=cost(COVER),
         name="first_back",
     )(in_vmem(hidden), in_vmem(weight), in_vmem(second), in_vmem(unit), in_vmem(scale), gain, in_vmem(out_weight))
 
@@ -576,7 +575,7 @@
         out_specs=block,
         out_shape=outside((rows, width), F32),
         compiler_params=params(14),
-        cost_estimate=cost(COVER),
+        cost_estimate=cost(),
         name="token_back",
     )(in_vmem(grads), in_vmem(weight), in_hbm(first))
 
@@ -635,13 +634,13 @@
         store_halves(theirs, 0, grads, pos, rows, extra)
 
 
-def halves_grad(pos, left, right, extra=None, held=True, flops=0):
+def halves_grad(pos, left, right, extra=None, held=True):
     rows, height = left.shape
     half = right.shape[1] // 2
     tile = half if extra is not None else tile_of(half, 768)
     steps = half // tile
     room = 0 if extra is None else 128
-    out = outside((4, 2, 2, height // 16, half + room))
+    out = inside((4, 2, 2, height // 16, half + room))
     block = pl.BlockSpec((4, 2, 1, height // 16, tile + room), lambda i, j, p: (0, 0, i ^ p[3], 0, j))
     return pl.pallas_call(
         functools.partial(halves_grad_kernel, tile=tile),
@@ -654,7 +653,7 @@
         ),
         out_shape=[out, out],
         compiler_params=params(14),
-        cost_estimate=cost(flops),
+        cost_estimate=cost(),
         name="halves_grad",
     )(pos, in_vmem(left) if held else left, in_vmem(right), *(() if extra is None else (extra,)))
 
@@ -687,7 +686,7 @@
 def stacked_grad(pos, left, right):
     rows, height = left.shape
     wide = right.shape[1]
-    out = outside((4, 2, 2, height // 64, 2 * wide))
+    out = inside((4, 2, 2, height // 64, 2 * wide))
     block = pl.BlockSpec((1, 2, 2, height // 64, 2 * wide), lambda i, p: (i ^ p[0], 0, 0, 0, 0))
     return pl.pallas_call(
         stacked_grad_kernel,
@@ -704,99 +703,99 @@
     )(pos, in_vmem(left), in_vmem(right))
 
 
+def held_call(kernel, name, outs, values, flops=0):
+    return pl.pallas_call(
+        kernel,
+        in_specs=[HELD] * len(values),
+        out_specs=[HELD] * len(outs),
+        out_shape=[inside(out) for out in outs],
+        compiler_params=params(4),
+        cost_estimate=cost(flops),
+        name=name,
+    )(*map(in_vmem, values))
+
+
+def add(*terms):
+    total = terms[0].astype(F32)
+    for term in terms[1:]:
+        total += term.astype(F32)
+    return total
+
+
 def core_sum_kernel(*refs, count):
-    outs = refs[2 * count :]
+    outs = refs[-4:]
     for flip in range(4):
         at = 0
         for mine, theirs in zip(refs[:count], refs[count : 2 * count]):
             wide = mine.shape[4]
-            pick = (0, flip // 2, flip % 2)
-            outs[flip][0, :, at : at + wide] = (mine[pick].astype(F32) + theirs[pick].astype(F32)).astype(BF16)
+            for chip in range(4):
+                pick = (chip, flip // 2, flip % 2)
+                outs[flip][chip, :, at : at + wide] = add(mine[pick], theirs[pick]).astype(BF16)
             at += wide
-
-
-def core_sum(mine, theirs):
+        if len(refs) > 2 * count + 4:
+            near, far = refs[2 * count : 2 * count + 2]
+            total = add(near[flip], far[flip]).astype(BF16)
+            wide = total.shape[1] // 4
+            for part in range(4):
+                outs[flip][part, :, at:] = total[:, part * wide : (part + 1) * wide]
+
+
+def core_sum(mine, theirs, more=()):
     rows = mine[0].shape[3]
-    wide = sum(m.shape[4] for m in mine)
-    return pl.pallas_call(
-        functools.partial(core_sum_kernel, count=len(mine)),
-        grid=(4,),
-        in_specs=[pl.BlockSpec((1,) + m.shape[1:], lambda i: (i, 0, 0, 0, 0)) for m in (*mine, *theirs)],
-        out_specs=[pl.BlockSpec((1, rows, wide), lambda i: (i, 0, 0))] * 4,
-        out_shape=[inside((4, rows, wide))] * 4,
-        compiler_params=params(10),
-        cost_estimate=cost(),
-        name="core_sum",
-    )(*map(in_hbm, (*mine, *theirs)))
-
-
-def plane_sum_kernel(own, one, two, three, *outs):
-    for flip in range(4):
-        total = own[flip].astype(F32) + one[flip].astype(F32)
-        total += two[flip].astype(F32) + three[flip].astype(F32)
-        if len(outs) == 4:
-            outs[flip][...] = total.astype(BF16)
-        else:
-            outs[flip // 2][flip % 2] = total.astype(BF16)
-
-
-def plane_sum(parts, apart):
+    wide = sum(m.shape[4] for m in mine) + sum(m.shape[2] // 8 for m in more)
+    kernel = functools.partial(core_sum_kernel, count=len(mine))
+    return held_call(kernel, "core_sum", [(4, rows, wide)] * 4, [*mine, *theirs, *more])
+
+
+def near_sum_kernel(mine, theirs, keep, near):
+    for chip in range(4):
+        for flip in range(4):
+            pick = (chip, flip // 2, flip % 2)
+            (keep, near)[chip % 2][chip // 2, flip] = add(mine[pick], theirs[pick]).astype(BF16)
+
+
+def near_sum(mine, theirs):
+    shape = (2, 4) + mine.shape[3:]
+    return held_call(near_sum_kernel, "near_sum", [shape] * 2, [mine, theirs])
+
+
+def plane_sum_kernel(own, one, two, three, keep, near, *more):
+    wide = keep.shape[2]
+    for chip in range(4):
+        total = add(own[chip], one[chip], two[chip], three[chip]).astype(BF16)
+        (keep, near)[chip % 2][chip // 2] = total[:, :wide]
+        if more:
+            part = total.shape[1] - wide
+            more[0][:, chip * part : (chip + 1) * part] = total[:, wide:]
+
+
+def plane_sum(parts, more=0, flops=0):
     _, rows, wide = parts[0].shape
-    outs = [inside((rows, wide))] * 4 if apart else [inside((2, rows, wide))] * 2
-    return pl.pallas_call(
-        plane_sum_kernel,
-        in_specs=[HELD] * 4,
-        out_specs=[HELD] * len(outs),
-        out_shape=outs,
-        compiler_params=params(4),
-        cost_estimate=cost(),
-        name="plane_sum",
-    )(*map(in_vmem, parts))
-
-
-def pair_sum_kernel(near, received, one, two):
-    one[...] = (near[0].astype(F32) + received[0].astype(F32)).astype(BF16)
-    two[...] = (near[1].astype(F32) + received[1].astype(F32)).astype(BF16)
-
-
-def pair_sum(near, received):
-    _, rows, wide = near.shape
-    return pl.pallas_call(
-        pair_sum_kernel,
-        in_specs=[HELD] * 2,
-        out_specs=[HELD] * 2,
-        out_shape=[inside((rows, wide))] * 2,
-        compiler_params=params(4),
-        cost_estimate=cost(),
-        name="pair_sum",
-    )(in_vmem(near), in_vmem(received))
-
-
-def chip_sum_kernel(*refs, count):
-    out, at = refs[-1], 0
-    for group in range(count):
-        terms = refs[group:-1:count]
-        wide = terms[0].shape[1]
-        total = terms[0][...].astype(F32)
-        for term in terms[1:]:
-            total += term[...].astype(F32)
-        out[:, at : at + wide] = total.astype(BF16)
-        at += wide
-
-
-def chip_sum(*lists, flops=0):
-    parts = [part for parts in lists for part in parts]
-    rows = parts[0].shape[0]
-    wide = sum(part.shape[1] for part in lists[0])
-    return pl.pallas_call(
-        functools.partial(chip_sum_kernel, count=len(lists[0])),
-        in_specs=[HELD] * len(parts),
-        out_specs=HELD,
-        out_shape=inside((rows, wide)),
-        compiler_params=params(4),
-        cost_estimate=cost(flops),
-        name="chip_sum",
-    )(*map(in_vmem, parts))
+    shape = (2, rows, wide - more)
+    outs = [shape] * 2 + ([(rows, 4 * more)] if more else [])
+    return held_call(plane_sum_kernel, "plane_sum", outs, parts, flops)
+
+
+def pair_sum_kernel(keep, received, one, two):
+    one[...] = add(keep[0], received[0]).astype(BF16)
+    two[...] = add(keep[1], received[1]).astype(BF16)
+
+
+def pair_sum(keep, received, flops=0):
+    return held_call(pair_sum_kernel, "pair_sum", [keep.shape[1:]] * 2, [keep, received], flops)
+
+
+def last_sum_kernel(*refs):
+    out, at = refs[-1], refs[-1].shape[1] - refs[-2].shape[1]
+    if at:
+        out[:, :at] = refs[0][...]
+    out[:, at:] = add(refs[-3][...], refs[-2][...]).astype(BF16)
+
+
+def last_sum(one, two, beside=None):
+    values = [one, two] if beside is None else [beside, one, two]
+    rows, wide = one.shape[0], one.shape[1] + (0 if beside is None else beside.shape[1])
+    return held_call(last_sum_kernel, "last_sum", [(rows, wide)], values)[0]
 
 
 def place_kernel(pos, *refs, layout):
@@ -859,8 +858,7 @@
 
 
 def from_chips(values):
-    parts = values if isinstance(values, (list, tuple)) else [values] * 3
-    return [from_chip(part, flip) for flip, part in zip((1, 2, 3), parts)]
+    return [from_chip(values, flip) for flip in CHIPS]
 
 
 def from_chip(values, flip):
@@ -935,33 +933,37 @@
     pos = jnp.stack([part // 2, part % 2, replica // 2, replica % 2]).astype(jnp.int32)
     shapes = [(parts * shard.shape[0], shard.shape[1]) for shard in (project_weight, output_weight, expand_weight, shrink_weight)]
     if pieces:
+        chips_p = from_chips(half_of(pos, project_weight))
+        sibling_p = from_core(project_weight)
         held = jnp.concatenate([vector.reshape(-1, 96) for vector in vectors], axis=0)
         held = jnp.pad(held, ((0, 4), (0, 32)))
-        quarter_p, wide_p = half_of(pos, project_weight), project_weight.shape[1] // 2
-        chips_p = from_chips(jnp.concatenate([quarter_p, jnp.pad(held, ((0, 32), (0, 0)))], axis=1))
-        sibling_p = from_core(project_weight)
-        chips_p = after(chips_p, sibling_p)
-        mine_p = below(*chips_p, wide=wide_p)
-        held = jnp.concatenate([held, *(chip[:16, wide_p:] for chip in chips_p)], axis=0)
-        quarter_e = after(half_of(pos, expand_weight), *chips_p)
-        one_e = from_chip(quarter_e, 1)
+        quarter_e = [half_of(pos, expand_weight), half_of(pos, output_weight), jnp.pad(held, ((0, 32), (0, 0)))]
+        quarter_e = jnp.concatenate(quarter_e, axis=1)
+        wide_e = quarter_e.shape[1] - 128
+        chips_p = after(chips_p, sibling_p, quarter_e)
+        mine_p = below(*chips_p)
+        quarter_e = after(quarter_e, *chips_p)
+        far_e = from_chip(quarter_e, 2)
+        near_e = [from_chip(quarter_e, 1), from_chip(far_e, 1)]
         plane_p = from_plane(mine_p)
-        far_e = from_chip(below(quarter_e, one_e), 2)
-        plane_p = below(*after(plane_p, one_e))
+        plane_p = below(*after(plane_p, *near_e))
         other_p = [from_core(mine_p), from_core(plane_p)]
-        project = Weight(
-            shapes[0],
-            [project_weight, sibling_p, mine_p, plane_p, *other_p],
-            functools.partial(halves_copies, high=project_weight.shape[0], wide=project_weight.shape[1]),
-        )
+
+        def halves(shape, shard, sibling, group, at):
+            copies = functools.partial(halves_copies, at=at, high=shard.shape[0], wide=shard.shape[1])
+            return Weight(shape, [shard, sibling, *group], copies)
+
+        project = halves(shapes[0], project_weight, sibling_p, (mine_p, plane_p, *other_p), 0)
         rows_s = shrink_weight.shape[0] // 8
         quarter_s = lax.dynamic_slice(
             shrink_weight, ((pos[2] * 2 + pos[3]) * 2 * rows_s, 0), (2 * rows_s, shrink_weight.shape[1])
         )
         quarter_s = jnp.concatenate([quarter_s[:rows_s], quarter_s[rows_s:]], axis=1)
-        one_s = from_chip(after(quarter_s, plane_p), 1)
-        mine_e = below(one_e, far_e)
+        quarter_s = after(quarter_s, plane_p)
+        far_s = from_chip(quarter_s, 2)
+        mine_e = below(*near_e, far_e, wide=wide_e)
         plane_e = from_plane(mine_e)
+        held = jnp.concatenate([held, *(chip[:16, wide_e:] for chip in (*near_e, far_e))], axis=0)
         held = after(held, mine_e)
         bias_full, hidden_bias, rows6 = spread(pos, [held, from_core(held)], width, expand_weight.shape[1])
         out_bias, gain1, shift1, down_bias, gain2, shift2 = (rows6[at : at + 1] for at in range(6))
@@ -981,23 +983,20 @@
     joined, project = join(pos, token_rows, project, bias_full)
     joined3 = joined.reshape(pairs, seq, 3 * width)
     if pieces:
-        output = Weight(shapes[1], [gather(after(output_weight, far_e))])
-        far_s = below(quarter_s, after(one_s, joined))
+        far_s = after(far_s, joined)
         joined3 = after(joined3, far_s)
-        far_s = from_chip(far_s, 2)
+        near_s = [from_chip(quarter_s, 1), from_chip(far_s, 1)]
     context, probs = attend(joined3, captions)
     context_rows = context.reshape(rows, width)
     if pieces:
-        far_s = after(far_s, context)
-        plane_e = below(*after(plane_e, far_s))
-        other_e = [from_core(mine_e), from_core(plane_e)]
+        near_s = after(near_s, context)
+        plane_e = below(*after(plane_e, *near_s))
+        group_e = (mine_e, plane_e, from_core(mine_e), from_core(plane_e))
         sibling_e = from_core(after(expand_weight, context))
-        expand = Weight(
-            shapes[2],
-            [expand_weight, sibling_e, mine_e, plane_e, *other_e],
-            functools.partial(halves_copies, high=expand_weight.shape[0], wide=expand_weight.shape[1]),
-        )
-        mine_s = below(one_s, after(far_s, plane_e))
+        sibling_o = from_core(after(output_weight, context))
+        expand = halves(shapes[2], expand_weight, sibling_e, group_e, 0)
+        output = halves(shapes[1], output_weight, sibling_o, group_e, expand_weight.shape[1] // 2)
+        mine_s = below(*near_s, after(far_s, plane_e))
         plane_s = from_plane(mine_s)
         context_rows = after(context_rows, mine_s)
     unit1, scale1, normed_low, output = first_norm(pos, context_rows, output, out_bias, token_rows, gain1, shift1)
@@ -1022,9 +1021,9 @@
         grad_shrink = weight_grad(active, shrink_low)
     expand_low, sums_hidden = hidden_back(shrink_low, shrink, slope)
     if pieces:
-        own_s, *out_s = core_sum([mine_s], [after(theirs_s, expand_low)])
-        plane_s = from_plane(out_s)
-        expand_low = after(expand_low, own_s)
+        keep_s, near_s = near_sum(mine_s, after(theirs_s, expand_low))
+        expand_low = after(expand_low, near_s)
+        near_s = from_chip(near_s, 1)
         mine_e, theirs_e = halves_grad(pos, normed_low, expand_low)
         theirs_e = from_core(theirs_e)
         expand_low = after(expand_low, mine_e)
@@ -1032,27 +1031,28 @@
         expand_low, expand, second_grad, unit1, scale1, gain1, output
     )
     if pieces:
-        near_s, far_s = plane_sum([own_s, *after(plane_s, branch_low)], False)
+        mine_o, theirs_o = halves_grad(pos, context_rows, branch_low)
+        theirs_o = from_core(theirs_o)
+        own_eo, *out_eo = core_sum([mine_e, mine_o], [theirs_e, theirs_o])
+        plane_eo = from_plane(out_eo)
+        keep_s, far_s = pair_sum(keep_s, after(near_s, own_eo))
+        context_grad = after(context_grad, keep_s)
         far_s = from_chip(far_s, 2)
-        mine_o, theirs_o = halves_grad(pos, context_rows, after(branch_low, near_s), flops=COVER)
-        theirs_o = from_core(theirs_o)
-        own_eo, *out_eo = core_sum([mine_e, mine_o], after([theirs_e, theirs_o], mine_o))
-        plane_eo = from_plane(out_eo)
-        context_grad = after(context_grad, own_eo)
     else:
         grad_expand = weight_grad(normed_low, expand_low)
         grad_output = weight_grad(context_rows, branch_low)
     joined_grad, sums_joined = attend_back(joined3, probs, context_grad.reshape(pairs, seq, width))
     joined_grad_rows = joined_grad.reshape(rows, 3 * width)
     if pieces:
-        near_s, last_s = pair_sum(near_s, after(far_s, joined_grad))
-        last_s = from_chip(last_s, 1)
-        extra = after(bundle(sums_joined, sums1, sums2, sums_hidden), near_s)
+        extra = bundle(sums_joined, sums1, sums2, sums_hidden)
         mine_p, theirs_p = halves_grad(pos, token_rows, joined_grad_rows, extra, held=False)
         theirs_p = from_core(theirs_p)
-        near_eo, far_eo = plane_sum([own_eo, *after(plane_eo, mine_p)], False)
-        far_eo = from_chip(far_eo, 2)
-        joined_grad_rows = after(joined_grad_rows, near_eo)
+        far_s = after(far_s, mine_p)
+        keep_eo, near_eo = plane_sum([own_eo, *after(plane_eo, far_s)], flops=COVER)
+        own_p, *out_p = core_sum([mine_p], [after(theirs_p, near_eo)], (keep_s, far_s))
+        near_eo = from_chip(near_eo, 1)
+        plane_p = from_plane(out_p)
+        joined_grad_rows = after(joined_grad_rows, own_p)
     else:
         grad_project = weight_grad(token_rows, joined_grad_rows)
 
@@ -1069,16 +1069,15 @@
     token_grad = token_back(joined_grad_rows, project, first_grad)
     if pieces:
         half_p, half_e, half_o = project_weight.shape[1] // 2, expand_weight.shape[1] // 2, width // 2
-        own_p, *out_p = core_sum([mine_p], [after(theirs_p, token_grad)])
-        plane_p = from_plane(out_p)
-        near_eo, last_eo = pair_sum(near_eo, after(far_eo, own_p))
-        last_eo = from_chip(last_eo, 1)
-        ahead_p = plane_sum([own_p, *after(plane_p, near_eo)], True)
-        chips_p = from_chips(ahead_p[1:])
-        total_seo = chip_sum([near_s, near_eo], after([last_s, last_eo], ahead_p[0]))
+        keep_eo, far_eo = pair_sum(keep_eo, after(near_eo, token_grad))
+        far_eo = from_chip(far_eo, 2)
+        keep_p, near_p, total_s = plane_sum([own_p, *after(plane_p, keep_eo)], more=2 * width // 4)
+        near_p = from_chip(near_p, 1)
+        total_seo = last_sum(keep_eo, after(far_eo, keep_p), total_s)
         quarters_seo = from_plane(total_seo)
-        total_p = chip_sum([ahead_p[0]], *([chip] for chip in after(chips_p, total_seo)), flops=COVER)
-        quarters_p = from_plane(after(total_p, *quarters_seo))
+        keep_p, far_p = pair_sum(keep_p, after(near_p, total_seo))
+        total_p = last_sum(keep_p, from_chip(far_p, 2))
+        quarters_p = from_plane(total_p)
         own_shrink, own_expand, own_output = place(
             pos, [total_seo, *after(quarters_seo, total_p)], (("stacked", 2 * width), ("halves", half_e), ("halves", half_o))
         )

time: 303 us -> 242 us (0.80)
  waiting for transfers between devices: 90.2 us -> 61 us
  Pallas kernels: 130 us -> 116 us
  between operations: 14.7 us -> 1.3 us
  local copies, waits for them, and re-layouts: 18.6 us -> 13.1 us
    ppermute x14 -> x15, waiting for transfers between devices: 48.3 us -> 31.9 us  [from_chip(): return lax.ppermute(values, 'fsdp', [(i, i ^ 2 * flip) for i in range(8)])]
    ppermute x24 -> x21, waiting for transfers between devices: 35.7 us -> 21.5 us  [from_plane(): lax.ppermute(part, 'dp', [(i, i ^ flip) for i in range(4)])]
    pallas_call x10, Pallas kernels: 11 us -> 2.98 us  [held_call(): pl.pallas_call(kernel, in_specs=[HELD] * len(values), out_specs=[HELD] *...]
    unnamed x56 -> x48, local copies, waits for them, and re-layouts: 10.9 us -> 4.73 us
    ppermute x14 -> x15, starting transfers between devices: 17.1 us -> 19.9 us  [from_chip(): return lax.ppermute(values, 'fsdp', [(i, i ^ 2 * flip) for i in range(8)])]
    ppermute x24 -> x21, starting transfers between devices: 28.7 us -> 26.1 us  [from_plane(): lax.ppermute(part, 'dp', [(i, i ^ flip) for i in range(4)])]
    ppermute x14 -> x15, waiting for transfers between devices: 6.18 us -> 7.64 us  [from_core(): return lax.ppermute(values, 'fsdp', [(i, i ^ 1) for i in range(8)])]
  transfers between devices with their start and end apart: 53 -> 51, of which waited for: 19 -> 20; matrix products, arithmetic and copies ran while one was open for 2% -> 3% of each run, Pallas kernels for 33% -> 40%
where the time goes in v3:
time: 242 us; the launch traced here: 241 us
  Pallas kernels  116 us (48%)
  waiting for transfers between devices  61 us (25%)
  starting transfers between devices  49.2 us (20%)
  local copies, waits for them, and re-layouts  13.1 us (5%)
    ppermute x15, waiting for transfers between devices, from_chip(): return lax.ppermute(values, 'fsdp', [(i, i ^ 2 * flip) for i in range(8)])  31.9 us
    ppermute x21, starting transfers between devices, from_plane(): lax.ppermute(part, 'dp', [(i, i ^ flip) for i in range(4)])  26.1 us
    ppermute x21, waiting for transfers between devices, from_plane(): lax.ppermute(part, 'dp', [(i, i ^ flip) for i in range(4)])  21.5 us
    ppermute x15, starting transfers between devices, from_chip(): return lax.ppermute(values, 'fsdp', [(i, i ^ 2 * flip) for i in range(8)])  19.9 us
    pallas_call x1, Pallas kernels, attend(): pl.pallas_call(attend_kernel, grid_spec=pltpu.PrefetchScalarGridSpec(num_...  16.3 us
    pallas_call x3, Pallas kernels, halves_grad(): pl.pallas_call(functools.partial(halves_grad_kernel, tile=tile), grid_spe...  15.9 us
    pallas_call x1, Pallas kernels, attend_back(): pl.pallas_call(attend_back_kernel, grid=(pairs,), in_specs=[pl.BlockSpec(...  14.7 us
    pallas_call x1, Pallas kernels, expand_act(): pl.pallas_call(functools.partial(expand_kernel, weight=weight, tile=tile)...  11.1 us
  transfers between devices with their start and end apart: 51, of which 20 were waited for; matrix products, arithmetic and copies ran while one was open for 3% of the time, Pallas kernels for 40%

profile of v3, /device:TPU:0, one launch (start us, length us, event | category | flops | bytes accessed | tf_op | source)
XLA Modules:
  0.0 241.0 jit_solution(8319510605141135258)
XLA Ops:
  2.1 3.7 %collective-permute-start.2 = (bf16[48,1152]{1,0:T(8,128)(2,1)S(1)}, bf16[48,1152]{1,0:T(8,128)(2,1)S(1)}, u32[]{:S(2)}, u32[]{:S(2)}) collective-permute-start(bf16[48,1152]{1,0:T(8,128)(2,1)S(1)} %dynamic_slice.14), channel_id=1, source_target_pairs={{0,4},{1,5},{2,6},{3,7},{4,0},{5,1},{6,2},{7,3},{8,12},{9,13},{10,... | collective-permute-start | bytes 331784 | tf_op jit(solution)/shard_map/ppermute | solution.py:865
  12.1 2.4 collective-permute-done.2.refs_2_
  15.6 3.7 %collective-permute-start.5 = (bf16[48,2048]{1,0:T(8,128)(2,1)S(1)}, bf16[48,2048]{1,0:T(8,128)(2,1)S(1)}, u32[]{:S(2)}, u32[]{:S(2)}) collective-permute-start(bf16[48,2048]{1,0:T(8,128)(2,1)S(1)} %fusion.1), channel_id=1, source_target_pairs={{0,4},{1,5},{2,6},{3,7},{4,0},{5,1},{6,2},{7,3},{8,12},{9,13},{10,... | collective-permute-start | bytes 589832 | tf_op jit(solution)/shard_map/ppermute | solution.py:865
  20.7 2.5 %collective-permute-start.10 = (bf16[144,1152]{1,0:T(8,128)(2,1)S(1)}, bf16[144,1152]{1,0:T(8,128)(2,1)S(1)}, u32[]{:S(2)}, u32[]{:S(2)}) collective-permute-start(bf16[144,1152]{1,0:T(8,128)(2,1)S(1)} %below.7.rest_2_), channel_id=1, source_target_pairs={{0,24},{8,16},{16,8},{24,0},{1,25},{9,17},{17,9},{25,1},{2,26},{10... | collective-permute-start | bytes 995336 | tf_op jit(solution)/shard_map/ppermute | solution.py:856
  23.7 5.0 %collective-permute-done.5.refs_2_ = bf16[48,2048]{1,0:T(8,128)(2,1)S(1)} collective-permute-done((bf16[48,2048]{1,0:T(8,128)(2,1)S(1)}, bf16[48,2048]{1,0:T(8,128)(2,1)S(1)}, u32[]{:S(2)}, u32[]{:S(2)}) %collective-permute-start.5) | collective-permute-done | bytes 196640 | tf_op jit(solution)/shard_map/ppermute | solution.py:865
  30.5 6.1 %collective-permute-done.6.refs_1_ = bf16[48,2048]{1,0:T(8,128)(2,1)S(1)} collective-permute-done((bf16[48,2048]{1,0:T(8,128)(2,1)S(1)}, bf16[48,2048]{1,0:T(8,128)(2,1)S(1)}, u32[]{:S(2)}, u32[]{:S(2)}) %collective-permute-start.6) | collective-permute-done | bytes 196640 | tf_op jit(solution)/shard_map/ppermute | solution.py:865
  44.0 1.7 collective-permute-start.14
  45.7 7.8 %join.1 = (bf16[832,2304]{1,0:T(8,128)(2,1)}, bf16[768,2304]{1,0:T(8,128)(2,1)S(1)}) custom-call(s32[4]{0:T(128)S(1)} %pad_add_fusion.pos, bf16[832,768]{1,0:T(8,128)(2,1)S(1)} %bitcast.32, f32[1,2304]{1,0:T(1,128)S(1)} %get-tuple-element.128.bias, bf16[96,2304]{1,0:T(8,128)(2,1)} %rest_0_.4, bf16[96,2304]{1,0:T(8,128)(2,1)} %copy-done.19, ...), custom_call_target="tpu_custom_call" | custom-call | tf_op jit(solution)/shard_map/join/pallas_call | solution.py:236
  54.5 16.3 %attend.1 = (bf16[8,104,768]{2,1,0:T(8,128)(2,1)S(1)}, bf16[8,6,104,256]{3,2,1,0:T(8,128)(2,1)}) custom-call(s32[8]{0:T(128)S(1)} %copy-done.8, bf16[8,104,2304]{2,1,0:T(8,128)(2,1)} %bitcast.39), custom_call_target="tpu_custom_call" | custom-call | tf_op jit(solution)/shard_map/attend/pallas_call | solution.py:290
  73.7 1.7 collective-permute-done.20.rest_4_
  79.0 4.5 %first_norm.1 = (f32[832,768]{1,0:T(8,128)S(1)}, f32[832,1]{1,0:T(8,128)S(1)}, bf16[832,768]{1,0:T(8,128)(2,1)S(1)}, bf16[768,768]{1,0:T(8,128)(2,1)S(1)}) custom-call(s32[4]{0:T(128)S(1)} %pad_add_fusion.pos, bf16[832,768]{1,0:T(8,128)(2,1)S(1)} %bitcast.35, f32[1,768]{1,0:T(1,128)S(1)} %get-tuple-element.239.bias, bf16[832,768]{1,0:T(8,128)(2,1)S(1)} %bitcast.33, ...), custom_call_target="tpu_custom_call" | custom-call | tf_op jit(solution)/shard_map/first_norm/pallas_call | solution.py:411
  84.3 11.1 %expand_act.1 = (bf16[832,3072]{1,0:T(8,128)(2,1)S(1)}, bf16[832,3072]{1,0:T(8,128)(2,1)S(1)}, bf16[768,3072]{1,0:T(8,128)(2,1)S(1)}) custom-call(s32[4]{0:T(128)S(1)} %pad_add_fusion.pos, bf16[832,768]{1,0:T(8,128)(2,1)S(1)} %get-tuple-element.146.normed_low.left, f32[1,3072]{1,0:T(1,128)S(1)} %get-tuple-element.147.bias, bf16[96,3072]{1,0:T(8,128)(2,1)} %rest_0_.6, ...), custom_call_target="tpu_custom_call" | custom-call | tf_op jit(solution)/shard_map/expand_act/pallas_call | solution.py:441
  97.0 3.2 %collective-permute-done.27.rest_4_ = bf16[144,1536]{1,0:T(8,128)(2,1)S(1)} collective-permute-done((bf16[144,1536]{1,0:T(8,128)(2,1)S(1)}, bf16[144,1536]{1,0:T(8,128)(2,1)S(1)}, u32[]{:S(2)}, u32[]{:S(2)}) %collective-permute-start.27) | collective-permute-done | bytes 442400 | tf_op jit(solution)/shard_map/ppermute | solution.py:850
  101.6 10.8 %second_norm.1 = (bf16[832,768]{1,0:T(8,128)(2,1)}, bf16[832,768]{1,0:T(8,128)(2,1)S(1)}, f32[832,768]{1,0:T(8,128)S(1)}, f32[8,768]{1,0:T(8,128)S(1)}, bf16[3072,768]{1,0:T(8,128)(2,1)S(1)}) custom-call(s32[4]{0:T(128)S(1)} %pad_add_fusion.pos, s32[8]{0:T(128)S(1)} %copy-done.8, bf16[832,3072]{1,0:T(8,128)(2,1)S(1)} %get-tuple-element.149.active.left, ...), custom_call_target="tpu_custom_call" | custom-call | tf_op jit(solution)/shard_map/second_norm/pallas_call | solution.py:484
  112.4 7.2 %stacked_grad.1 = (bf16[4,2,2,48,1536]{4,3,2,1,0:T(8,128)(2,1)S(1)}, bf16[4,2,2,48,1536]{4,3,2,1,0:T(8,128)(2,1)S(1)}) custom-call(s32[4]{0:T(128)S(1)} %pad_add_fusion.pos, bf16[832,3072]{1,0:T(8,128)(2,1)S(1)} %get-tuple-element.149.active.left, bf16[832,768]{1,0:T(8,128)(2,1)S(1)} %get-tuple-element.159.right.low), custom_call_target="tpu_custom_call" | custom-call | tf_op jit(solution)/shard_map/stacked_grad/pallas_call | solution.py:691
  119.8 4.9 %hidden_back.1 = (bf16[832,3072]{1,0:T(8,128)(2,1)S(1)}, f32[1,3072]{1,0:T(1,128)S(1)}) custom-call(bf16[832,768]{1,0:T(8,128)(2,1)S(1)} %get-tuple-element.159.right.low, bf16[3072,768]{1,0:T(8,128)(2,1)S(1)} %get-tuple-element.160.weight, bf16[832,3072]{1,0:T(8,128)(2,1)S(1)} %get-tuple-element.161.slope), custom_call_target="tpu_custom_call" | custom-call | tf_op jit(solution)/shard_map/hidden_back/pallas_call | solution.py:517
  126.4 7.2 %halves_grad.3 = (bf16[4,2,2,48,1536]{4,3,2,1,0:T(8,128)(2,1)S(1)}, bf16[4,2,2,48,1536]{4,3,2,1,0:T(8,128)(2,1)S(1)}) custom-call(s32[4]{0:T(128)S(1)} %pad_add_fusion.pos, bf16[832,768]{1,0:T(8,128)(2,1)S(1)} %get-tuple-element.146.normed_low.left, bf16[832,3072]{1,0:T(8,128)(2,1)S(1)} %get-tuple-element.168.right.hidden), custom_call_target="tpu_custom_call" | custom-call | tf_op jit(solution)/shard_map/halves_grad/pallas_call | solution.py:645
  133.8 9.5 %first_back.1 = (f32[832,768]{1,0:T(8,128)}, bf16[832,768]{1,0:T(8,128)(2,1)S(1)}, bf16[832,768]{1,0:T(8,128)(2,1)S(1)}, f32[8,768]{1,0:T(8,128)S(1)}) custom-call(bf16[832,3072]{1,0:T(8,128)(2,1)S(1)} %get-tuple-element.168.right.hidden, bf16[768,3072]{1,0:T(8,128)(2,1)S(1)} %get-tuple-element.169.weight, f32[832,768]{1,0:T(8,128)S(1)} %copy-done.10, ...), custom_call_target="tpu_custom_call" | custom-call | flops 99999997952 | tf_op jit(solution)/shard_map/first_back/pallas_call | solution.py:545
  143.3 2.8 %halves_grad.4 = (bf16[4,2,2,48,384]{4,3,2,1,0:T(8,128)(2,1)S(1)}, bf16[4,2,2,48,384]{4,3,2,1,0:T(8,128)(2,1)S(1)}) custom-call(s32[4]{0:T(128)S(1)} %pad_add_fusion.pos, bf16[832,768]{1,0:T(8,128)(2,1)S(1)} %bitcast.36, bf16[832,768]{1,0:T(8,128)(2,1)S(1)} %get-tuple-element.175.right), custom_call_target="tpu_custom_call" | custom-call | tf_op jit(solution)/shard_map/halves_grad/pallas_call | solution.py:645
  146.5 1.6 collective-permute-done.32.refs_3_
  155.1 14.7 %attend_back.1 = (bf16[8,104,2304]{2,1,0:T(8,128)(2,1)S(1)}, f32[1,1536]{1,0:T(1,128)S(1)}) custom-call(bf16[8,104,2304]{2,1,0:T(8,128)(2,1)} %bitcast.40, bf16[8,6,104,256]{3,2,1,0:T(8,128)(2,1)} %get-tuple-element.156.probs, bf16[8,104,768]{2,1,0:T(8,128)(2,1)S(1)} %bitcast.38), custom_call_target="tpu_custom_call" | custom-call | tf_op jit(solution)/shard_map/attend_back/pallas_call | solution.py:349
  169.9 5.9 %halves_grad.5 = (bf16[4,2,2,48,1280]{4,3,2,1,0:T(8,128)(2,1)S(1)}, bf16[4,2,2,48,1280]{4,3,2,1,0:T(8,128)(2,1)S(1)}) custom-call(s32[4]{0:T(128)S(1)} %pad_add_fusion.pos, bf16[832,768]{1,0:T(8,128)(2,1)S(1)} %bitcast.34, bf16[832,2304]{1,0:T(8,128)(2,1)S(1)} %bitcast.30, f32[8,16,128]{2,1,0:T(8,128)S(1)} %bundle.1.rest_0_), custom_call_target="tpu_custom_call" | custom-call | tf_op jit(solution)/shard_map/halves_grad/pallas_call | solution.py:645
  175.9 6.3 %collective-permute-done.37.refs_3_ = bf16[4,48,1536]{2,1,0:T(8,128)(2,1)S(1)} collective-permute-done((bf16[4,48,1536]{2,1,0:T(8,128)(2,1)S(1)}, bf16[4,48,1536]{2,1,0:T(8,128)(2,1)S(1)}, u32[]{:S(2)}, u32[]{:S(2)}) %collective-permute-start.37) | collective-permute-done | bytes 589856 | tf_op jit(solution)/shard_map/ppermute | solution.py:865
  182.2 1.9 collective-permute-done.35.two
  189.6 5.8 %token_back.1 = f32[832,768]{1,0:T(8,128)} custom-call(bf16[832,2304]{1,0:T(8,128)(2,1)S(1)} %bitcast.31, bf16[768,2304]{1,0:T(8,128)(2,1)S(1)} %get-tuple-element.202.weight, f32[832,768]{1,0:T(8,128)} %get-tuple-element.203.first), custom_call_target="tpu_custom_call" | custom-call | tf_op jit(solution)/shard_map/token_back/pallas_call | solution.py:571
  195.4 2.3 collective-permute-done.41.received
  199.1 3.4 %collective-permute-done.38.one = bf16[4,48,1664]{2,1,0:T(8,128)(2,1)S(1)} collective-permute-done((bf16[4,48,1664]{2,1,0:T(8,128)(2,1)S(1)}, bf16[4,48,1664]{2,1,0:T(8,128)(2,1)S(1)}, u32[]{:S(2)}, u32[]{:S(2)}) %collective-permute-start.38) | collective-permute-done | bytes 639008 | tf_op jit(solution)/shard_map/ppermute | solution.py:856
  202.5 12.7 %collective-permute-done.39.two = bf16[4,48,1664]{2,1,0:T(8,128)(2,1)S(1)} collective-permute-done((bf16[4,48,1664]{2,1,0:T(8,128)(2,1)S(1)}, bf16[4,48,1664]{2,1,0:T(8,128)(2,1)S(1)}, u32[]{:S(2)}, u32[]{:S(2)}) %collective-permute-start.39) | collective-permute-done | bytes 639008 | tf_op jit(solution)/shard_map/ppermute | solution.py:856
  220.2 1.6 collective-permute-done.42.received
  223.2 5.9 %collective-permute-done.44.refs_1_ = bf16[48,1280]{1,0:T(8,128)(2,1)S(1)} collective-permute-done((bf16[48,1280]{1,0:T(8,128)(2,1)S(1)}, bf16[48,1280]{1,0:T(8,128)(2,1)S(1)}, u32[]{:S(2)}, u32[]{:S(2)}) %collective-permute-start.44) | collective-permute-done | bytes 122912 | tf_op jit(solution)/shard_map/ppermute | solution.py:865
  229.1 1.5 collective-permute-start.47
  234.6 2.2 place.2
  (172 shorter events, 61.8 us)
Async XLA Ops:
  0.6 14.9 %collective-permute-start.3 = (bf16[96,2304]{1,0:T(8,128)(2,1)}, bf16[96,2304]{1,0:T(8,128)(2,1)S(1)}, u32[]{:S(2)}, u32[]{:S(2)}) collective-permute-start(bf16[96,2304]{1,0:T(8,128)(2,1)} %rest_0_.4), channel_id=1, source_target_pairs={{0,1},{1,0},{2,3},{3,2},{4,5},{5,4},{6,7},{7,6},{8,9},{9,8},{10,11... | collective-permute-start | bytes 1327112 | tf_op jit(solution)/shard_map/ppermute | solution.py:850
  2.1 12.4 %collective-permute-start.2 = (bf16[48,1152]{1,0:T(8,128)(2,1)S(1)}, bf16[48,1152]{1,0:T(8,128)(2,1)S(1)}, u32[]{:S(2)}, u32[]{:S(2)}) collective-permute-start(bf16[48,1152]{1,0:T(8,128)(2,1)S(1)} %dynamic_slice.14), channel_id=1, source_target_pairs={{0,4},{1,5},{2,6},{3,7},{4,0},{5,1},{6,2},{7,3},{8,12},{9,13},{10,... | collective-permute-start | bytes 331784 | tf_op jit(solution)/shard_map/ppermute | solution.py:865
  15.6 13.2 %collective-permute-start.5 = (bf16[48,2048]{1,0:T(8,128)(2,1)S(1)}, bf16[48,2048]{1,0:T(8,128)(2,1)S(1)}, u32[]{:S(2)}, u32[]{:S(2)}) collective-permute-start(bf16[48,2048]{1,0:T(8,128)(2,1)S(1)} %fusion.1), channel_id=1, source_target_pairs={{0,4},{1,5},{2,6},{3,7},{4,0},{5,1},{6,2},{7,3},{8,12},{9,13},{10,... | collective-permute-start | bytes 589832 | tf_op jit(solution)/shard_map/ppermute | solution.py:865
  19.3 10.9 %collective-permute-start.4 = (bf16[48,2048]{1,0:T(8,128)(2,1)S(1)}, bf16[48,2048]{1,0:T(8,128)(2,1)S(1)}, u32[]{:S(2)}, u32[]{:S(2)}) collective-permute-start(bf16[48,2048]{1,0:T(8,128)(2,1)S(1)} %fusion.1), channel_id=1, source_target_pairs={{0,2},{1,3},{2,0},{3,1},{4,6},{5,7},{6,4},{7,5},{8,10},{9,11},{10,... | collective-permute-start | bytes 589832 | tf_op jit(solution)/shard_map/ppermute | solution.py:865
  20.6 20.7 %collective-permute-start.11 = (bf16[144,1152]{1,0:T(8,128)(2,1)S(1)}, bf16[144,1152]{1,0:T(8,128)(2,1)S(1)}, u32[]{:S(2)}, u32[]{:S(2)}) collective-permute-start(bf16[144,1152]{1,0:T(8,128)(2,1)S(1)} %below.7.rest_2_), channel_id=1, source_target_pairs={{0,1},{1,0},{2,3},{3,2},{4,5},{5,4},{6,7},{7,6},{8,9},{9,8},{10,11... | collective-permute-start | bytes 995336 | tf_op jit(solution)/shard_map/ppermute | solution.py:850
  20.7 16.1 %collective-permute-start.10 = (bf16[144,1152]{1,0:T(8,128)(2,1)S(1)}, bf16[144,1152]{1,0:T(8,128)(2,1)S(1)}, u32[]{:S(2)}, u32[]{:S(2)}) collective-permute-start(bf16[144,1152]{1,0:T(8,128)(2,1)S(1)} %below.7.rest_2_), channel_id=1, source_target_pairs={{0,24},{8,16},{16,8},{24,0},{1,25},{9,17},{17,9},{25,1},{2,26},{10... | collective-permute-start | bytes 995336 | tf_op jit(solution)/shard_map/ppermute | solution.py:856
  23.2 15.7 %collective-permute-start.9 = (bf16[144,1152]{1,0:T(8,128)(2,1)S(1)}, bf16[144,1152]{1,0:T(8,128)(2,1)S(1)}, u32[]{:S(2)}, u32[]{:S(2)}) collective-permute-start(bf16[144,1152]{1,0:T(8,128)(2,1)S(1)} %below.7.rest_2_), channel_id=1, source_target_pairs={{0,16},{8,24},{16,0},{24,8},{1,17},{9,25},{17,1},{25,9},{2,18},{10... | collective-permute-start | bytes 995336 | tf_op jit(solution)/shard_map/ppermute | solution.py:856
  28.8 11.7 %collective-permute-start.8 = (bf16[144,1152]{1,0:T(8,128)(2,1)S(1)}, bf16[144,1152]{1,0:T(8,128)(2,1)S(1)}, u32[]{:S(2)}, u32[]{:S(2)}) collective-permute-start(bf16[144,1152]{1,0:T(8,128)(2,1)S(1)} %below.7.rest_2_), channel_id=1, source_target_pairs={{0,8},{8,0},{16,24},{24,16},{1,9},{9,1},{17,25},{25,17},{2,10},{10... | collective-permute-start | bytes 995336 | tf_op jit(solution)/shard_map/ppermute | solution.py:856
  36.8 34.0 %collective-permute-start.18 = (bf16[144,1920]{1,0:T(8,128)(2,1)S(1)}, bf16[144,1920]{1,0:T(8,128)(2,1)S(1)}, u32[]{:S(2)}, u32[]{:S(2)}) collective-permute-start(bf16[144,1920]{1,0:T(8,128)(2,1)S(1)} %below.6.rest_2_), channel_id=1, source_target_pairs={{0,24},{8,16},{16,8},{24,0},{1,25},{9,17},{17,9},{25,1},{2,26},{10... | collective-permute-start | bytes 1658888 | tf_op jit(solution)/shard_map/ppermute | solution.py:856
  39.0 31.9 %collective-permute-start.17 = (bf16[144,1920]{1,0:T(8,128)(2,1)S(1)}, bf16[144,1920]{1,0:T(8,128)(2,1)S(1)}, u32[]{:S(2)}, u32[]{:S(2)}) collective-permute-start(bf16[144,1920]{1,0:T(8,128)(2,1)S(1)} %below.6.rest_2_), channel_id=1, source_target_pairs={{0,16},{8,24},{16,0},{24,8},{1,17},{9,25},{17,1},{25,9},{2,18},{10... | collective-permute-start | bytes 1658888 | tf_op jit(solution)/shard_map/ppermute | solution.py:856
  40.5 30.4 %collective-permute-start.16 = (bf16[144,1920]{1,0:T(8,128)(2,1)S(1)}, bf16[144,1920]{1,0:T(8,128)(2,1)S(1)}, u32[]{:S(2)}, u32[]{:S(2)}) collective-permute-start(bf16[144,1920]{1,0:T(8,128)(2,1)S(1)} %below.6.rest_2_), channel_id=1, source_target_pairs={{0,8},{8,0},{16,24},{24,16},{1,9},{9,1},{17,25},{25,17},{2,10},{10... | collective-permute-start | bytes 1658888 | tf_op jit(solution)/shard_map/ppermute | solution.py:856
  41.5 12.0 %collective-permute-start.13 = (bf16[48,1536]{1,0:T(8,128)(2,1)S(1)}, bf16[48,1536]{1,0:T(8,128)(2,1)S(1)}, u32[]{:S(2)}, u32[]{:S(2)}) collective-permute-start(bf16[48,1536]{1,0:T(8,128)(2,1)S(1)} %pad_maximum_fusion), channel_id=1, source_target_pairs={{0,4},{1,5},{2,6},{3,7},{4,0},{5,1},{6,2},{7,3},{8,12},{9,13},{10,... | collective-permute-start | bytes 442376 | tf_op jit(solution)/shard_map/ppermute | solution.py:865
  44.0 26.8 %collective-permute-start.14 = (bf16[48,1536]{1,0:T(8,128)(2,1)S(1)}, bf16[48,1536]{1,0:T(8,128)(2,1)S(1)}, u32[]{:S(2)}, u32[]{:S(2)}) collective-permute-start(bf16[48,1536]{1,0:T(8,128)(2,1)S(1)} %pad_maximum_fusion), channel_id=1, source_target_pairs={{0,2},{1,3},{2,0},{3,1},{4,6},{5,7},{6,4},{7,5},{8,10},{9,11},{10,... | collective-permute-start | bytes 442376 | tf_op jit(solution)/shard_map/ppermute | solution.py:865
  53.5 17.3 %collective-permute-start.15 = (bf16[48,1536]{1,0:T(8,128)(2,1)S(1)}, bf16[48,1536]{1,0:T(8,128)(2,1)S(1)}, u32[]{:S(2)}, u32[]{:S(2)}) collective-permute-start(bf16[48,1536]{1,0:T(8,128)(2,1)S(1)} %collective-permute-done.13.refs_2_), channel_id=1, source_target_pairs={{0,2},{1,3},{2,0},{3,1},{4,6},{5,7},{6,4},{7,5},{8,10},{9,11},{10,... | collective-permute-start | bytes 442376 | tf_op jit(solution)/shard_map/ppermute | solution.py:865
  71.9 11.6 %collective-permute-start.22 = (bf16[96,3072]{1,0:T(8,128)(2,1)S(1)}, bf16[96,3072]{1,0:T(8,128)(2,1)S(1)}, u32[]{:S(2)}, u32[]{:S(2)}) collective-permute-start(bf16[96,3072]{1,0:T(8,128)(2,1)S(1)} %copy-done.15), channel_id=1, source_target_pairs={{0,1},{1,0},{2,3},{3,2},{4,5},{5,4},{6,7},{7,6},{8,9},{9,8},{10,11... | collective-permute-start | bytes 1769480 | tf_op jit(solution)/shard_map/ppermute | solution.py:850
  72.5 23.0 %collective-permute-start.26 = (bf16[144,1536]{1,0:T(8,128)(2,1)S(1)}, bf16[144,1536]{1,0:T(8,128)(2,1)S(1)}, u32[]{:S(2)}, u32[]{:S(2)}) collective-permute-start(bf16[144,1536]{1,0:T(8,128)(2,1)S(1)} %below.10.rest_2_), channel_id=1, source_target_pairs={{0,24},{8,16},{16,8},{24,0},{1,25},{9,17},{17,9},{25,1},{2,26},{10... | collective-permute-start | bytes 1327112 | tf_op jit(solution)/shard_map/ppermute | solution.py:856
  75.4 20.0 %collective-permute-start.25 = (bf16[144,1536]{1,0:T(8,128)(2,1)S(1)}, bf16[144,1536]{1,0:T(8,128)(2,1)S(1)}, u32[]{:S(2)}, u32[]{:S(2)}) collective-permute-start(bf16[144,1536]{1,0:T(8,128)(2,1)S(1)} %below.10.rest_2_), channel_id=1, source_target_pairs={{0,16},{8,24},{16,0},{24,8},{1,17},{9,25},{17,1},{25,9},{2,18},{10... | collective-permute-start | bytes 1327112 | tf_op jit(solution)/shard_map/ppermute | solution.py:856
  76.6 18.8 %collective-permute-start.24 = (bf16[144,1536]{1,0:T(8,128)(2,1)S(1)}, bf16[144,1536]{1,0:T(8,128)(2,1)S(1)}, u32[]{:S(2)}, u32[]{:S(2)}) collective-permute-start(bf16[144,1536]{1,0:T(8,128)(2,1)S(1)} %below.10.rest_2_), channel_id=1, source_target_pairs={{0,8},{8,0},{16,24},{24,16},{1,9},{9,1},{17,25},{25,17},{2,10},{10... | collective-permute-start | bytes 1327112 | tf_op jit(solution)/shard_map/ppermute | solution.py:856
  125.3 28.3 %collective-permute-start.30 = (bf16[2,4,48,1536]{3,2,1,0:T(8,128)(2,1)S(1)}, bf16[2,4,48,1536]{3,2,1,0:T(8,128)(2,1)S(1)}, u32[]{:S(2)}, u32[]{:S(2)}) collective-permute-start(bf16[2,4,48,1536]{3,2,1,0:T(8,128)(2,1)S(1)} %get-tuple-element.165), channel_id=1, source_target_pairs={{0,2},{1,3},{2,0},{3,1},{4,6},{5,7},{6,4},{7,5},{8,10},{9,11},{10,... | collective-permute-start | bytes 3538952 | tf_op jit(solution)/shard_map/ppermute | solution.py:865
  133.7 14.5 %collective-permute-start.31 = (bf16[4,2,2,48,1536]{4,3,2,1,0:T(8,128)(2,1)S(1)}, bf16[4,2,2,48,1536]{4,3,2,1,0:T(8,128)(2,1)S(1)}, u32[]{:S(2)}, u32[]{:S(2)}) collective-permute-start(bf16[4,2,2,48,1536]{4,3,2,1,0:T(8,128)(2,1)S(1)} %get-tuple-element.177), channel_id=1, source_target_pairs={{0,1},{1,0},{2,3},{3,2},{4,5},{5,4},{6,7},{7,6},{8,9},{9,8},{10,11... | collective-permute-start | bytes 7077896 | tf_op jit(solution)/shard_map/ppermute | solution.py:850
  148.9 33.4 %collective-permute-start.34 = (bf16[4,48,1920]{2,1,0:T(8,128)(2,1)S(1)}, bf16[4,48,1920]{2,1,0:T(8,128)(2,1)S(1)}, u32[]{:S(2)}, u32[]{:S(2)}) collective-permute-start(bf16[4,48,1920]{2,1,0:T(8,128)(2,1)S(1)} %get-tuple-element.190), channel_id=1, source_target_pairs={{0,8},{8,0},{16,24},{24,16},{1,9},{9,1},{17,25},{25,17},{2,10},{10... | collective-permute-start | bytes 2211848 | tf_op jit(solution)/shard_map/ppermute | solution.py:856
  149.9 34.3 %collective-permute-start.35 = (bf16[4,48,1920]{2,1,0:T(8,128)(2,1)S(1)}, bf16[4,48,1920]{2,1,0:T(8,128)(2,1)S(1)}, u32[]{:S(2)}, u32[]{:S(2)}) collective-permute-start(bf16[4,48,1920]{2,1,0:T(8,128)(2,1)S(1)} %get-tuple-element.191), channel_id=1, source_target_pairs={{0,16},{8,24},{16,0},{24,8},{1,17},{9,25},{17,1},{25,9},{2,18},{10... | collective-permute-start | bytes 2211848 | tf_op jit(solution)/shard_map/ppermute | solution.py:856
  150.9 33.2 %collective-permute-start.36 = (bf16[4,48,1920]{2,1,0:T(8,128)(2,1)S(1)}, bf16[4,48,1920]{2,1,0:T(8,128)(2,1)S(1)}, u32[]{:S(2)}, u32[]{:S(2)}) collective-permute-start(bf16[4,48,1920]{2,1,0:T(8,128)(2,1)S(1)} %get-tuple-element.192), channel_id=1, source_target_pairs={{0,24},{8,16},{16,8},{24,0},{1,25},{9,17},{17,9},{25,1},{2,26},{10... | collective-permute-start | bytes 2211848 | tf_op jit(solution)/shard_map/ppermute | solution.py:856
  153.8 28.4 %collective-permute-start.37 = (bf16[4,48,1536]{2,1,0:T(8,128)(2,1)S(1)}, bf16[4,48,1536]{2,1,0:T(8,128)(2,1)S(1)}, u32[]{:S(2)}, u32[]{:S(2)}) collective-permute-start(bf16[4,48,1536]{2,1,0:T(8,128)(2,1)S(1)} %get-tuple-element.193), channel_id=1, source_target_pairs={{0,4},{1,5},{2,6},{3,7},{4,0},{5,1},{6,2},{7,3},{8,12},{9,13},{10,... | collective-permute-start | bytes 1769480 | tf_op jit(solution)/shard_map/ppermute | solution.py:865
  185.1 17.4 %collective-permute-start.38 = (bf16[4,48,1664]{2,1,0:T(8,128)(2,1)S(1)}, bf16[4,48,1664]{2,1,0:T(8,128)(2,1)S(1)}, u32[]{:S(2)}, u32[]{:S(2)}) collective-permute-start(bf16[4,48,1664]{2,1,0:T(8,128)(2,1)S(1)} %get-tuple-element.204), channel_id=1, source_target_pairs={{0,8},{8,0},{16,24},{24,16},{1,9},{9,1},{17,25},{25,17},{2,10},{10... | collective-permute-start | bytes 1916936 | tf_op jit(solution)/shard_map/ppermute | solution.py:856
  186.3 29.0 %collective-permute-start.39 = (bf16[4,48,1664]{2,1,0:T(8,128)(2,1)S(1)}, bf16[4,48,1664]{2,1,0:T(8,128)(2,1)S(1)}, u32[]{:S(2)}, u32[]{:S(2)}) collective-permute-start(bf16[4,48,1664]{2,1,0:T(8,128)(2,1)S(1)} %get-tuple-element.205), channel_id=1, source_target_pairs={{0,16},{8,24},{16,0},{24,8},{1,17},{9,25},{17,1},{25,9},{2,18},{10... | collective-permute-start | bytes 1916936 | tf_op jit(solution)/shard_map/ppermute | solution.py:856
  187.3 28.0 %collective-permute-start.40 = (bf16[4,48,1664]{2,1,0:T(8,128)(2,1)S(1)}, bf16[4,48,1664]{2,1,0:T(8,128)(2,1)S(1)}, u32[]{:S(2)}, u32[]{:S(2)}) collective-permute-start(bf16[4,48,1664]{2,1,0:T(8,128)(2,1)S(1)} %get-tuple-element.206), channel_id=1, source_target_pairs={{0,24},{8,16},{16,8},{24,0},{1,25},{9,17},{17,9},{25,1},{2,26},{10... | collective-permute-start | bytes 1916936 | tf_op jit(solution)/shard_map/ppermute | solution.py:856
  188.7 9.0 %collective-permute-start.41 = (bf16[2,48,1920]{2,1,0:T(8,128)(2,1)S(1)}, bf16[2,48,1920]{2,1,0:T(8,128)(2,1)S(1)}, u32[]{:S(2)}, u32[]{:S(2)}) collective-permute-start(bf16[2,48,1920]{2,1,0:T(8,128)(2,1)S(1)} %get-tuple-element.198), channel_id=1, source_target_pairs={{0,2},{1,3},{2,0},{3,1},{4,6},{5,7},{6,4},{7,5},{8,10},{9,11},{10,... | collective-permute-start | bytes 1105928 | tf_op jit(solution)/shard_map/ppermute | solution.py:865
  197.8 18.8 %collective-permute-start.43 = (bf16[48,1920]{1,0:T(8,128)(2,1)S(1)}, bf16[48,1920]{1,0:T(8,128)(2,1)S(1)}, u32[]{:S(2)}, u32[]{:S(2)}) collective-permute-start(bf16[48,1920]{1,0:T(8,128)(2,1)S(1)} %get-tuple-element.216), channel_id=1, source_target_pairs={{0,4},{1,5},{2,6},{3,7},{4,0},{5,1},{6,2},{7,3},{8,12},{9,13},{10,... | collective-permute-start | bytes 552968 | tf_op jit(solution)/shard_map/ppermute | solution.py:865
  216.7 15.0 %collective-permute-start.50 = (bf16[48,3456]{1,0:T(8,128)(2,1)S(1)}, bf16[48,3456]{1,0:T(8,128)(2,1)S(1)}, u32[]{:S(2)}, u32[]{:S(2)}) collective-permute-start(bf16[48,3456]{1,0:T(8,128)(2,1)S(1)} %last_sum.2.refs_0_), channel_id=1, source_target_pairs={{0,24},{8,16},{16,8},{24,0},{1,25},{9,17},{17,9},{25,1},{2,26},{10... | collective-permute-start | bytes 995336 | tf_op jit(solution)/shard_map/ppermute | solution.py:856
  218.2 15.5 %collective-permute-start.49 = (bf16[48,3456]{1,0:T(8,128)(2,1)S(1)}, bf16[48,3456]{1,0:T(8,128)(2,1)S(1)}, u32[]{:S(2)}, u32[]{:S(2)}) collective-permute-start(bf16[48,3456]{1,0:T(8,128)(2,1)S(1)} %last_sum.2.refs_0_), channel_id=1, source_target_pairs={{0,16},{8,24},{16,0},{24,8},{1,17},{9,25},{17,1},{25,9},{2,18},{10... | collective-permute-start | bytes 995336 | tf_op jit(solution)/shard_map/ppermute | solution.py:856
  219.2 15.4 %collective-permute-start.48 = (bf16[48,3456]{1,0:T(8,128)(2,1)S(1)}, bf16[48,3456]{1,0:T(8,128)(2,1)S(1)}, u32[]{:S(2)}, u32[]{:S(2)}) collective-permute-start(bf16[48,3456]{1,0:T(8,128)(2,1)S(1)} %last_sum.2.refs_0_), channel_id=1, source_target_pairs={{0,8},{8,0},{16,24},{24,16},{1,9},{9,1},{17,25},{25,17},{2,10},{10... | collective-permute-start | bytes 995336 | tf_op jit(solution)/shard_map/ppermute | solution.py:856
  (43 other events, 278.2 us)
